TPU v7x, 32 devices: a whole 2x2x4 slice. The times are simulated.
32 devices in a mesh: tile: 16 (over z, y, x), sub: 2 (over core).
Axes of the slice: x: 2, y: 2, z: 4, core: 2. Of those that a mesh axis runs over, the one named last changes fastest.
Arguments:
- grid: bfloat16 [32768, 512], P(('tile', 'sub')), may hold values from -6 to 6
- g2m_owner: int32 [256], P(('tile', 'sub')), may hold values from 0 to 31, as said below
- g2m_weight: float32 [32768], P(('tile', 'sub')), may hold values from 0.1 to 1
- m2g_owner: int32 [256], P(('tile', 'sub')), may hold values from 0 to 31, as said below
- m2g_weight: float32 [32768], P(('tile', 'sub')), may hold values from 0.2 to 2
- mesh_feat: bfloat16 [4096, 512], P(('tile', 'sub')), may hold values from -6 to 6
- neighbours: int32 [32, 3], P(('tile', 'sub')), may hold values from 0 to 31, as said below
- enc_w1: bfloat16 [512, 2048], replicated, may hold values from -0.25 to 0.25
- enc_w2: bfloat16 [2048, 512], replicated, may hold values from -0.125 to 0.125
- attn_gain: float32 [1, 512], replicated, may hold values from 0.25 to 1.75
- w_qkv: bfloat16 [1, 512, 1536], replicated, may hold values from -1 to 1
- w_out: bfloat16 [1, 512, 512], replicated, may hold values from -0.25 to 0.25
- dec_w1: bfloat16 [512, 2048], replicated, may hold values from -0.25 to 0.25
- dec_w2: bfloat16 [2048, 512], replicated, may hold values from -0.125 to 0.125
Outputs:
- decoded: bfloat16 [32768, 512], P(('tile', 'sub'))
- mesh_out: bfloat16 [4096, 512], P(('tile', 'sub'))
Inputs may be any that keep to these rules, and one draw needn't show every extreme that they name: g2m_owner[b] equals b // 8 + e modulo 32 with e between -2 and 2; both -2 and 2 occur. m2g_owner[b] equals b // 8 + e modulo 32 with e between -2 and 2; both -2 and 2 occur. `neighbours`: row m holds three distinct blocks among m - 2, m - 1, m + 1, m + 2 modulo 32.
All inputs are finite; a program needn't handle non-finite values.
Results may differ from a plain program's by a relative error of at most 0.015.
Values may be sent and summed in bfloat16 or wider, within the bound.
No kernel may reach another device: no remote copies, remote signals or barrier semaphores. Data moves between devices by JAX's collectives and lax.ppermute only.
A program may use at most 64 MiB of HBM per device.

v0:
```python
import jax
import jax.numpy as jnp
from jax import lax
from jax.sharding import PartitionSpec as P

HD = 128


def passed_along(block, axis, distance):
    devices = range(lax.axis_size(axis))
    route = [((i - distance) % len(devices), i) for i in devices]
    return lax.ppermute(block, axis, route)


def feed(rows, first, second):
    hidden = jnp.dot(rows, first, preferred_element_type=jnp.float32)
    active = jax.nn.silu(hidden).astype(jnp.bfloat16)
    return (
        rows.astype(jnp.float32) + jnp.dot(active, second, preferred_element_type=jnp.float32)
    ).astype(jnp.bfloat16)


def absorb(owners, weights, blocks, target):
    picked = (owners == target).astype(jnp.float32)[:, None] * weights
    return jnp.sum(picked[:, :, None] * blocks.astype(jnp.float32), axis=0)


def on_device(
    grid,
    g2m_owner,
    g2m_weight,
    m2g_owner,
    m2g_weight,
    mesh_feat,
    neighbours,
    enc_w1,
    enc_w2,
    attn_gain,
    w_qkv,
    w_out,
    dec_w1,
    dec_w2,
):
    mine = lax.axis_index(("tile", "sub"))
    count = lax.axis_size(("tile", "sub"))
    rows = mesh_feat.shape[0]
    depth = mesh_feat.shape[1]
    nblocks = g2m_owner.shape[0]
    heads = attn_gain.shape[1] // HD
    encoded = feed(grid, enc_w1, enc_w2)
    enc_blocks = encoded.reshape(nblocks, rows, depth)
    in_weights = g2m_weight.reshape(nblocks, rows)
    state = mesh_feat.astype(jnp.float32) + absorb(g2m_owner, in_weights, enc_blocks, mine)
    for delta in (-2, -1, 1, 2):
        target = (mine + delta) % count
        partial_sum = absorb(g2m_owner, in_weights, enc_blocks, target)
        state = state + passed_along(
            partial_sum.astype(jnp.bfloat16), ("tile", "sub"), delta
        ).astype(partial_sum.dtype)
    listed = (neighbours[0] - mine + 2) % count
    mean_sq = jnp.mean(state * state, axis=-1, keepdims=True)
    normed = (state * lax.rsqrt(mean_sq + 1e-06) * attn_gain[0]).astype(jnp.bfloat16)
    qkv = jnp.dot(normed, w_qkv[0], preferred_element_type=jnp.float32).astype(jnp.bfloat16)
    query = qkv[:, :depth]
    own_kv = qkv[:, depth:]
    nearby = {}
    for delta in (2, 1, -1, -2):
        nearby[delta] = passed_along(own_kv, ("tile", "sub"), delta)
    stacked = jnp.stack([nearby[2], nearby[1], own_kv, nearby[-1], nearby[-2]])
    far_kv = stacked[listed]
    all_kv = jnp.concatenate([own_kv[None], far_kv], axis=0).reshape(4 * rows, 2 * depth)
    keys = all_kv[:, :depth].reshape(4 * rows, heads, HD)
    values = all_kv[:, depth:].reshape(4 * rows, heads, HD)
    queries = query.reshape(rows, heads, HD)
    scores = jnp.einsum(
        "qhd,khd->hqk", queries, keys, preferred_element_type=jnp.float32
    ) / jnp.sqrt(jnp.float32(HD))
    probs = jax.nn.softmax(scores, axis=-1).astype(jnp.bfloat16)
    mixed = jnp.einsum("hqk,khd->qhd", probs, values, preferred_element_type=jnp.float32)
    attended = mixed.astype(jnp.bfloat16).reshape(rows, depth)
    state = state + jnp.dot(attended, w_out[0], preferred_element_type=jnp.float32)
    mesh_out = state.astype(jnp.bfloat16)
    beside_all = {}
    for delta in (2, 1, -1, -2):
        beside_all[delta] = passed_along(mesh_out, ("tile", "sub"), delta)
    candidates = jnp.stack([beside_all[2], beside_all[1], mesh_out, beside_all[-1], beside_all[-2]])
    reading = (m2g_owner - mine + 2) % count
    picked = candidates[reading].reshape(nblocks * rows, depth)
    dec_in = (
        encoded.astype(jnp.float32) + m2g_weight[:, None] * picked.astype(jnp.float32)
    ).astype(jnp.bfloat16)
    decoded = feed(dec_in, dec_w1, dec_w2)
    return (decoded, mesh_out)


def solution(mesh):
    in_specs = (
        P(("tile", "sub"), None),
        P(("tile", "sub")),
        P(("tile", "sub")),
        P(("tile", "sub")),
        P(("tile", "sub")),
        P(("tile", "sub"), None),
        P(("tile", "sub"), None),
        P(),
        P(),
        P(),
        P(),
        P(),
        P(),
        P(),
    )
    out_specs = (P(("tile", "sub"), None), P(("tile", "sub"), None))
    return jax.shard_map(
        on_device, mesh=mesh, in_specs=in_specs, out_specs=out_specs, check_vma=False
    )
```

profile of v0, /device:TPU:0, one launch (start us, length us, event | category | flops | bytes accessed | tf_op | source)
XLA Modules:
  0.0 88.0 jit_solution(167716245490597620)
XLA Ops:
  0.7 1.5 %copy-done = bf16[2048,512]{1,0:T(8,128)(2,1)S(1)} copy-done((bf16[2048,512]{1,0:T(8,128)(2,1)S(1)}, bf16[2048,512]{1,0:T(8,128)(2,1)}, u32[]{:S(2)}) %copy-start) | copy-done | bytes 2097176
  2.2 8.5 %fusion.11 = f32[1024,512]{1,0:T(8,128)} fusion(bf16[2048,512]{1,0:T(8,128)(2,1)S(1)} %copy-done, bf16[1024,512]{1,0:T(8,128)(2,1)} %param.14, bf16[512,2048]{1,0:T(8,128)(2,1)} %param.21), kind=kOutput, calls=%fused_computation.22 | convolution fusion | flops 4307550208 | bytes 7340032 | tf_op jit(solution)/shard_map/dot_general | solution.py:19
  10.8 2.4 %multiply_reduce_fusion.4 = (f32[128,512]{1,0:T(8,128)S(1)}, bf16[128,512]{1,0:T(8,128)(2,1)S(1)}, bf16[128,512]{1,0:T(8,128)(2,1)S(1)}, bf16[128,512]{1,0:T(8,128)(2,1)S(1)}, bf16[128,512]{1,0:T(8,128)(2,1)S(1)}) fusion(f32[8,128,512]{2,1,0:T(8,128)} %bitcast.72, f32[8,128]{1,0:T(8,128)S(1)} %get-tuple-element.17, f32[8,128]{1,0:T(8,128)S(1)} %get-tuple-element.16, ...), kind=kLoop, calls=%fused_computation.18 | loop fusion | flops 4915200 | bytes 2904064 | tf_op jit(solution)/shard_map/reduce_sum | solution.py:25
  13.2 7.0 %collective-permute-start = (bf16[128,512]{1,0:T(8,128)(2,1)S(1)}, bf16[128,512]{1,0:T(8,128)(2,1)S(1)}, u32[]{:S(2)}, u32[]{:S(2)}) collective-permute-start(bf16[128,512]{1,0:T(8,128)(2,1)S(1)} %get-tuple-element.6), channel_id=1, source_target_pairs={{2,0},{3,1},{4,2},{5,3},{6,4},{7,5},{8,6},{9,7},{10,8},{11,9},{12,... | collective-permute-start | bytes 393224 | tf_op jit(solution)/shard_map/ppermute | solution.py:12
  20.7 0.7 collective-permute-start.3
  21.4 1.5 %collective-permute-done = bf16[128,512]{1,0:T(8,128)(2,1)S(1)} collective-permute-done((bf16[128,512]{1,0:T(8,128)(2,1)S(1)}, bf16[128,512]{1,0:T(8,128)(2,1)S(1)}, u32[]{:S(2)}, u32[]{:S(2)}) %collective-permute-start) | collective-permute-done | bytes 131104 | tf_op jit(solution)/shard_map/ppermute | solution.py:12
  22.9 1.4 %collective-permute-done.1 = bf16[128,512]{1,0:T(8,128)(2,1)S(1)} collective-permute-done((bf16[128,512]{1,0:T(8,128)(2,1)S(1)}, bf16[128,512]{1,0:T(8,128)(2,1)S(1)}, u32[]{:S(2)}, u32[]{:S(2)}) %collective-permute-start.1) | collective-permute-done | bytes 131104 | tf_op jit(solution)/shard_map/ppermute | solution.py:12
  24.3 4.1 %collective-permute-done.2 = bf16[128,512]{1,0:T(8,128)(2,1)S(1)} collective-permute-done((bf16[128,512]{1,0:T(8,128)(2,1)S(1)}, bf16[128,512]{1,0:T(8,128)(2,1)S(1)}, u32[]{:S(2)}, u32[]{:S(2)}) %collective-permute-start.2) | collective-permute-done | bytes 131104 | tf_op jit(solution)/shard_map/ppermute | solution.py:12
  28.5 2.2 %collective-permute-done.3 = bf16[128,512]{1,0:T(8,128)(2,1)S(1)} collective-permute-done((bf16[128,512]{1,0:T(8,128)(2,1)S(1)}, bf16[128,512]{1,0:T(8,128)(2,1)S(1)}, u32[]{:S(2)}, u32[]{:S(2)}) %collective-permute-start.3) | collective-permute-done | bytes 131104 | tf_op jit(solution)/shard_map/ppermute | solution.py:12
  31.3 0.7 slice_bitcast_fusion.1
  32.3 5.2 %collective-permute-start.6 = (bf16[128,1024]{1,0:T(8,128)(2,1)S(1)}, bf16[128,1024]{1,0:T(8,128)(2,1)S(1)}, u32[]{:S(2)}, u32[]{:S(2)}) collective-permute-start(bf16[128,1024]{1,0:T(8,128)(2,1)S(1)} %get-tuple-element.12), channel_id=1, source_target_pairs={{1,0},{2,1},{3,2},{4,3},{5,4},{6,5},{7,6},{8,7},{9,8},{10,9},{11,1... | collective-permute-start | bytes 786440 | tf_op jit(solution)/shard_map/ppermute | solution.py:12
  37.5 2.0 %collective-permute-start.7 = (bf16[128,1024]{1,0:T(8,128)(2,1)S(1)}, bf16[128,1024]{1,0:T(8,128)(2,1)S(1)}, u32[]{:S(2)}, u32[]{:S(2)}) collective-permute-start(bf16[128,1024]{1,0:T(8,128)(2,1)S(1)} %get-tuple-element.12), channel_id=1, source_target_pairs={{2,0},{3,1},{4,2},{5,3},{6,4},{7,5},{8,6},{9,7},{10,8},{11,9},{12,... | collective-permute-start | bytes 786440 | tf_op jit(solution)/shard_map/ppermute | solution.py:12
  39.5 7.6 %collective-permute-done.4 = bf16[128,1024]{1,0:T(8,128)(2,1)S(1)} collective-permute-done((bf16[128,1024]{1,0:T(8,128)(2,1)S(1)}, bf16[128,1024]{1,0:T(8,128)(2,1)S(1)}, u32[]{:S(2)}, u32[]{:S(2)}) %collective-permute-start.4) | collective-permute-done | bytes 262176 | tf_op jit(solution)/shard_map/ppermute | solution.py:12
  47.1 0.7 bitcast_dynamic-update-slice_fusion.3
  47.9 0.7 bitcast_dynamic-update-slice_fusion.2
  48.6 0.7 constant_dynamic-update-slice_fusion
  49.3 0.7 bitcast_dynamic-update-slice_fusion.1
  50.1 0.7 bitcast_dynamic-update-slice_fusion
  50.8 1.9 %gather_fusion = bf16[3,128,1024]{2,1,0:T(8,128)(2,1)S(1)} fusion(bf16[5,128,1024]{2,1,0:T(8,128)(2,1)} %bitcast_dynamic-update-slice_fusion, s32[1024]{0:T(1024)S(1)} %pad_clamp_fusion.1), kind=kCustom, calls=%fused_computation | custom fusion | bytes 1572876 | tf_op jit(solution)/shard_map/gather | solution.py:70
  52.7 1.0 %pad_maximum_fusion = bf16[4,128,1024]{2,1,0:T(8,128)(2,1)S(1)} fusion(bf16[3,128,1024]{2,1,0:T(8,128)(2,1)S(1)} %gather_fusion, bf16[1,128,1024]{2,1,0:T(8,128)(2,1)} %get-tuple-element.11), kind=kLoop, calls=%fused_computation.28 | loop fusion | flops 524288 | bytes 2097152 | tf_op jit(solution)/shard_map/concatenate | solution.py:71
  53.8 1.0 %fusion.32 = (bf16[512,512]{1,0:T(8,128)(2,1)}, bf16[512,512]{1,0:T(8,128)(2,1)}) fusion(bf16[512,1024]{1,0:T(8,128)(2,1)S(1)} %bitcast.71), kind=kLoop, calls=%fused_computation.79 | loop fusion | bytes 2097152 | tf_op jit(solution)/shard_map/slice | solution.py:72
  54.8 1.3 %copy.23 = bf16[512,512]{0,1:T(8,128)(2,1)S(1)} copy(bf16[512,512]{1,0:T(8,128)(2,1)} %get-tuple-element.9) | data formatting | bytes 1048576
  56.0 1.3 %convolution_multiply_fusion = f32[4,128,512]{2,1,0:T(8,128)} fusion(bf16[512,4,128]{0,2,1:T(8,128)(2,1)S(1)} %bitcast.73, bf16[128,1536]{1,0:T(8,128)(2,1)S(1)} %convolution_convert_fusion), kind=kOutput, calls=%fused_computation.24 | convolution fusion | flops 67371008 | bytes 1703936 | tf_op jit(solution)/shard_map/qhd,khd->hqk/dot_general | solution.py:75
  57.8 1.3 %copy.18 = bf16[512,512]{0,1:T(8,128)(2,1)S(1)} copy(bf16[512,512]{1,0:T(8,128)(2,1)} %get-tuple-element.10) | data formatting | bytes 1048576 | tf_op jit(solution)/shard_map/slice | solution.py:73
  59.1 2.7 %convolution_convert_fusion.1 = bf16[4,128,128]{2,1,0:T(8,128)(2,1)S(1)} fusion(bf16[512,4,128]{0,2,1:T(8,128)(2,1)S(1)} %bitcast.76, f32[4,128]{1,0:T(4,128)S(1)} %fusion.33, f32[4,128,512]{2,1,0:T(8,128)} %convolution_multiply_fusion), kind=kOutput, calls=%fused_computation.27 | convolution fusion | flops 67961856 | bytes 1705984 | tf_op jit(solution)/shard_map/hqk,khd->qhd/dot_general | solution.py:79
  62.1 4.1 %collective-permute-start.8 = (bf16[128,512]{1,0:T(8,128)(2,1)S(1)}, bf16[128,512]{1,0:T(8,128)(2,1)S(1)}, u32[]{:S(2)}, u32[]{:S(2)}) collective-permute-start(bf16[128,512]{1,0:T(8,128)(2,1)S(1)} %fusion.13), channel_id=1, source_target_pairs={{30,0},{31,1},{0,2},{1,3},{2,4},{3,5},{4,6},{5,7},{6,8},{7,9},{8,1... | collective-permute-start | bytes 393224 | tf_op jit(solution)/shard_map/ppermute | solution.py:12
  66.3 5.3 %collective-permute-start.10 = (bf16[128,512]{1,0:T(8,128)(2,1)S(1)}, bf16[128,512]{1,0:T(8,128)(2,1)S(1)}, u32[]{:S(2)}, u32[]{:S(2)}) collective-permute-start(bf16[128,512]{1,0:T(8,128)(2,1)S(1)} %fusion.13), channel_id=1, source_target_pairs={{1,0},{2,1},{3,2},{4,3},{5,4},{6,5},{7,6},{8,7},{9,8},{10,9},{11,1... | collective-permute-start | bytes 393224 | tf_op jit(solution)/shard_map/ppermute | solution.py:12
  71.6 2.2 %collective-permute-done.8 = bf16[128,512]{1,0:T(8,128)(2,1)S(1)} collective-permute-done((bf16[128,512]{1,0:T(8,128)(2,1)S(1)}, bf16[128,512]{1,0:T(8,128)(2,1)S(1)}, u32[]{:S(2)}, u32[]{:S(2)}) %collective-permute-start.8) | collective-permute-done | bytes 131104 | tf_op jit(solution)/shard_map/ppermute | solution.py:12
  74.4 0.6 collective-permute-done.10
  75.0 1.6 %collective-permute-done.11 = bf16[128,512]{1,0:T(8,128)(2,1)S(1)} collective-permute-done((bf16[128,512]{1,0:T(8,128)(2,1)S(1)}, bf16[128,512]{1,0:T(8,128)(2,1)S(1)}, u32[]{:S(2)}, u32[]{:S(2)}) %collective-permute-start.11) | collective-permute-done | bytes 131104 | tf_op jit(solution)/shard_map/ppermute | solution.py:12
  76.6 1.6 %gather_fusion.1 = bf16[8,128,512]{2,1,0:T(8,128)(2,1)} fusion(bf16[5,128,512]{2,1,0:T(8,128)(2,1)S(1)} %bitcast_dynamic-update-slice_fusion.4, s32[1024]{0:T(1024)S(1)} %pad_clamp_fusion), kind=kCustom, calls=%fused_computation.1 | custom fusion | bytes 2097184 | tf_op jit(solution)/shard_map/gather | solution.py:88
  78.2 9.7 %add_convert_fusion = bf16[1024,512]{1,0:T(8,128)(2,1)} fusion(bf16[2048,512]{1,0:T(8,128)(2,1)} %param.27, bf16[512,2048]{1,0:T(8,128)(2,1)} %param.26, f32[1024,512]{1,0:T(8,128)} %fusion.11, bf16[1024,512]{1,0:T(8,128)(2,1)} %bitcast.75, f32[1024]{0:T(1024)S(1)} %copy-done.8), kind=kOutput, calls=%fused_computation.13 | convolution fusion | flops 4311220224 | bytes 8392704 | tf_op jit(solution)/shard_map/dot_general | solution.py:19
  (47 shorter events, 2.9 us)
Async XLA Ops:
  0.6 1.6 %copy-start = (bf16[2048,512]{1,0:T(8,128)(2,1)S(1)}, bf16[2048,512]{1,0:T(8,128)(2,1)}, u32[]{:S(2)}) copy-start(bf16[2048,512]{1,0:T(8,128)(2,1)} %param.22) | copy-start | bytes 6291460
  2.2 8.5 %copy-start.7 = (s32[8]{0:T(128)S(1)}, s32[8]{0:T(128)}, u32[]{:S(2)}) copy-start(s32[8]{0:T(128)} %param.15) | copy-start | bytes 100
  2.2 8.5 %copy-start.5 = (f32[1024]{0:T(1024)S(1)}, f32[1024]{0:T(1024)}, u32[]{:S(2)}) copy-start(f32[1024]{0:T(1024)} %param.16) | copy-start | bytes 12292
  10.7 20.0 %copy-start.4 = (bf16[128,512]{1,0:T(8,128)(2,1)S(1)}, bf16[128,512]{1,0:T(8,128)(2,1)}, u32[]{:S(2)}) copy-start(bf16[128,512]{1,0:T(8,128)(2,1)} %param.19) | copy-start | bytes 393220
  10.7 20.2 %copy-start.1 = (bf16[1,512,1536]{2,1,0:T(8,128)(2,1)S(1)}, bf16[1,512,1536]{2,1,0:T(8,128)(2,1)}, u32[]{:S(2)}) copy-start(bf16[1,512,1536]{2,1,0:T(8,128)(2,1)} %param.24) | copy-start | bytes 4718596
  10.7 20.2 %copy-start.6 = (f32[1,512]{1,0:T(1,128)S(1)}, f32[1,512]{1,0:T(1,128)}, u32[]{:S(2)}) copy-start(f32[1,512]{1,0:T(1,128)} %param.23) | copy-start | bytes 6148
  13.2 9.7 %collective-permute-start = (bf16[128,512]{1,0:T(8,128)(2,1)S(1)}, bf16[128,512]{1,0:T(8,128)(2,1)S(1)}, u32[]{:S(2)}, u32[]{:S(2)}) collective-permute-start(bf16[128,512]{1,0:T(8,128)(2,1)S(1)} %get-tuple-element.6), channel_id=1, source_target_pairs={{2,0},{3,1},{4,2},{5,3},{6,4},{7,5},{8,6},{9,7},{10,8},{11,9},{12,... | collective-permute-start | bytes 393224 | tf_op jit(solution)/shard_map/ppermute | solution.py:12
  20.2 4.2 %collective-permute-start.1 = (bf16[128,512]{1,0:T(8,128)(2,1)S(1)}, bf16[128,512]{1,0:T(8,128)(2,1)S(1)}, u32[]{:S(2)}, u32[]{:S(2)}) collective-permute-start(bf16[128,512]{1,0:T(8,128)(2,1)S(1)} %get-tuple-element.5), channel_id=1, source_target_pairs={{1,0},{2,1},{3,2},{4,3},{5,4},{6,5},{7,6},{8,7},{9,8},{10,9},{11,1... | collective-permute-start | bytes 393224 | tf_op jit(solution)/shard_map/ppermute | solution.py:12
  20.2 8.3 %collective-permute-start.2 = (bf16[128,512]{1,0:T(8,128)(2,1)S(1)}, bf16[128,512]{1,0:T(8,128)(2,1)S(1)}, u32[]{:S(2)}, u32[]{:S(2)}) collective-permute-start(bf16[128,512]{1,0:T(8,128)(2,1)S(1)} %get-tuple-element.4), channel_id=1, source_target_pairs={{31,0},{0,1},{1,2},{2,3},{3,4},{4,5},{5,6},{6,7},{7,8},{8,9},{9,10... | collective-permute-start | bytes 393224 | tf_op jit(solution)/shard_map/ppermute | solution.py:12
  20.7 10.0 %collective-permute-start.3 = (bf16[128,512]{1,0:T(8,128)(2,1)S(1)}, bf16[128,512]{1,0:T(8,128)(2,1)S(1)}, u32[]{:S(2)}, u32[]{:S(2)}) collective-permute-start(bf16[128,512]{1,0:T(8,128)(2,1)S(1)} %get-tuple-element.3), channel_id=1, source_target_pairs={{30,0},{31,1},{0,2},{1,3},{2,4},{3,5},{4,6},{5,7},{6,8},{7,9},{8,1... | collective-permute-start | bytes 393224 | tf_op jit(solution)/shard_map/ppermute | solution.py:12
  30.7 1.4 %copy-start.9 = (s32[1,3]{1,0:T(1,128)S(1)}, s32[1,3]{1,0:T(1,128)}, u32[]{:S(2)}) copy-start(s32[1,3]{1,0:T(1,128)} %param.20) | copy-start | bytes 40
  32.1 15.1 %collective-permute-start.4 = (bf16[128,1024]{1,0:T(8,128)(2,1)S(1)}, bf16[128,1024]{1,0:T(8,128)(2,1)S(1)}, u32[]{:S(2)}, u32[]{:S(2)}) collective-permute-start(bf16[128,1024]{1,0:T(8,128)(2,1)S(1)} %get-tuple-element.12), channel_id=1, source_target_pairs={{30,0},{31,1},{0,2},{1,3},{2,4},{3,5},{4,6},{5,7},{6,8},{7,9},{8,1... | collective-permute-start | bytes 786440 | tf_op jit(solution)/shard_map/ppermute | solution.py:12
  32.1 15.8 %collective-permute-start.5 = (bf16[128,1024]{1,0:T(8,128)(2,1)S(1)}, bf16[128,1024]{1,0:T(8,128)(2,1)S(1)}, u32[]{:S(2)}, u32[]{:S(2)}) collective-permute-start(bf16[128,1024]{1,0:T(8,128)(2,1)S(1)} %get-tuple-element.12), channel_id=1, source_target_pairs={{31,0},{0,1},{1,2},{2,3},{3,4},{4,5},{5,6},{6,7},{7,8},{8,9},{9,10... | collective-permute-start | bytes 786440 | tf_op jit(solution)/shard_map/ppermute | solution.py:12
  32.3 17.1 %collective-permute-start.6 = (bf16[128,1024]{1,0:T(8,128)(2,1)S(1)}, bf16[128,1024]{1,0:T(8,128)(2,1)S(1)}, u32[]{:S(2)}, u32[]{:S(2)}) collective-permute-start(bf16[128,1024]{1,0:T(8,128)(2,1)S(1)} %get-tuple-element.12), channel_id=1, source_target_pairs={{1,0},{2,1},{3,2},{4,3},{5,4},{6,5},{7,6},{8,7},{9,8},{10,9},{11,1... | collective-permute-start | bytes 786440 | tf_op jit(solution)/shard_map/ppermute | solution.py:12
  37.5 12.6 %collective-permute-start.7 = (bf16[128,1024]{1,0:T(8,128)(2,1)S(1)}, bf16[128,1024]{1,0:T(8,128)(2,1)S(1)}, u32[]{:S(2)}, u32[]{:S(2)}) collective-permute-start(bf16[128,1024]{1,0:T(8,128)(2,1)S(1)} %get-tuple-element.12), channel_id=1, source_target_pairs={{2,0},{3,1},{4,2},{5,3},{6,4},{7,5},{8,6},{9,7},{10,8},{11,9},{12,... | collective-permute-start | bytes 786440 | tf_op jit(solution)/shard_map/ppermute | solution.py:12
  59.1 2.7 %copy-start.2 = (bf16[1,512,512]{2,1,0:T(8,128)(2,1)S(1)}, bf16[1,512,512]{2,1,0:T(8,128)(2,1)}, u32[]{:S(2)}) copy-start(bf16[1,512,512]{2,1,0:T(8,128)(2,1)} %param.25) | copy-start | bytes 1572868
  59.1 7.1 %copy-start.10 = (s32[8]{0:T(128)S(1)}, s32[8]{0:T(128)}, u32[]{:S(2)}) copy-start(s32[8]{0:T(128)} %param.17) | copy-start | bytes 100
  61.8 16.4 %copy-start.8 = (f32[1024]{0:T(1024)S(1)}, f32[1024]{0:T(1024)}, u32[]{:S(2)}) copy-start(f32[1024]{0:T(1024)} %param.18) | copy-start | bytes 12292
  62.1 25.9 %copy-start.3 = (bf16[128,512]{1,0:T(8,128)(2,1)}, bf16[128,512]{1,0:T(8,128)(2,1)S(1)}, u32[]{:S(2)}) copy-start(bf16[128,512]{1,0:T(8,128)(2,1)S(1)} %fusion.13) | copy-start | bytes 393220
  62.1 11.8 %collective-permute-start.8 = (bf16[128,512]{1,0:T(8,128)(2,1)S(1)}, bf16[128,512]{1,0:T(8,128)(2,1)S(1)}, u32[]{:S(2)}, u32[]{:S(2)}) collective-permute-start(bf16[128,512]{1,0:T(8,128)(2,1)S(1)} %fusion.13), channel_id=1, source_target_pairs={{30,0},{31,1},{0,2},{1,3},{2,4},{3,5},{4,6},{5,7},{6,8},{7,9},{8,1... | collective-permute-start | bytes 393224 | tf_op jit(solution)/shard_map/ppermute | solution.py:12
  66.2 8.1 %collective-permute-start.9 = (bf16[128,512]{1,0:T(8,128)(2,1)S(1)}, bf16[128,512]{1,0:T(8,128)(2,1)S(1)}, u32[]{:S(2)}, u32[]{:S(2)}) collective-permute-start(bf16[128,512]{1,0:T(8,128)(2,1)S(1)} %fusion.13), channel_id=1, source_target_pairs={{31,0},{0,1},{1,2},{2,3},{3,4},{4,5},{5,6},{6,7},{7,8},{8,9},{9,10... | collective-permute-start | bytes 393224 | tf_op jit(solution)/shard_map/ppermute | solution.py:12
  66.3 8.7 %collective-permute-start.10 = (bf16[128,512]{1,0:T(8,128)(2,1)S(1)}, bf16[128,512]{1,0:T(8,128)(2,1)S(1)}, u32[]{:S(2)}, u32[]{:S(2)}) collective-permute-start(bf16[128,512]{1,0:T(8,128)(2,1)S(1)} %fusion.13), channel_id=1, source_target_pairs={{1,0},{2,1},{3,2},{4,3},{5,4},{6,5},{7,6},{8,7},{9,8},{10,9},{11,1... | collective-permute-start | bytes 393224 | tf_op jit(solution)/shard_map/ppermute | solution.py:12
  71.6 5.0 %collective-permute-start.11 = (bf16[128,512]{1,0:T(8,128)(2,1)S(1)}, bf16[128,512]{1,0:T(8,128)(2,1)S(1)}, u32[]{:S(2)}, u32[]{:S(2)}) collective-permute-start(bf16[128,512]{1,0:T(8,128)(2,1)S(1)} %fusion.13), channel_id=1, source_target_pairs={{2,0},{3,1},{4,2},{5,3},{6,4},{7,5},{8,6},{9,7},{10,8},{11,9},{12,... | collective-permute-start | bytes 393224 | tf_op jit(solution)/shard_map/ppermute | solution.py:12
where the time goes:
time: 88.3 us; the launch traced here: 88 us
  starting transfers between devices  25.1 us (28%)
  matrix products  23.3 us (26%)
  waiting for transfers between devices  21.8 us (25%)
  local copies, waits for them, and re-layouts  13.1 us (15%)
  other arithmetic  3.75 us (4%)
    ppermute x12, starting transfers between devices, passed_along(): return lax.ppermute(block, axis, route)  25.1 us
    ppermute x12, waiting for transfers between devices, passed_along(): return lax.ppermute(block, axis, route)  21.8 us
    dot_general x2, matrix products, feed(): jnp.dot(active, second, preferred_element_type=jnp.float32)  18.2 us
    unnamed x31, local copies, waits for them, and re-layouts  5.81 us
    dot_general x1, matrix products, on_device(): jnp.einsum('hqk,khd->qhd', probs, values, preferred_element_type=jnp.floa...  2.71 us
    reduce_sum x1, other arithmetic, absorb(): return jnp.sum(picked[:, :, None] * blocks.astype(jnp.float32), axis=0)  2.38 us
    gather x1, local copies, waits for them, and re-layouts, on_device(): far_kv = stacked[listed]  1.91 us
  transfers between devices with their start and end apart: 12, of which 9 were waited for; matrix products, arithmetic and copies ran while one was open for 3% of the time, Pallas kernels for 0%

commit v1 on v0

v1 whole, which is shorter than its diff:
```python
import functools

import jax
import jax.numpy as jnp
from jax import lax
from jax.experimental import pallas as pl
from jax.experimental.pallas import tpu as pltpu
from jax.sharding import PartitionSpec as P

HD = 128
REACH = 2
EXTRA = 16
AXES = ("tile", "sub")
BF16 = jnp.bfloat16
F32 = jnp.float32
VMEM = pl.BlockSpec(memory_space=pltpu.VMEM)
SMEM = pl.BlockSpec(memory_space=pltpu.SMEM)
ANY = pl.BlockSpec(memory_space=pl.ANY)


def swapped(block):
    count = lax.axis_size(AXES)
    return lax.ppermute(block, AXES, [(i, i ^ 1) for i in range(count)])


def from_outward(block, chips):
    count = lax.axis_size(AXES)
    route = []
    for i in range(count):
        step = 2 * chips - 1
        route.append((i, (i + step if i % 2 else i - step) % count))
    return lax.ppermute(block, AXES, route)


def tiles_of(rows, columns):
    return min(rows, 256), min(columns, 512)


def weight_copies(first_hbm, second_hbm, first, second, sems, part):
    parts = first.shape[1] // part
    ones, twos = [], []
    for j in range(parts):
        cut = pl.ds(j * part, part)
        ones.append(pltpu.make_async_copy(first_hbm.at[:, cut], first.at[:, cut], sems.at[0, j]))
        twos.append(pltpu.make_async_copy(second_hbm.at[cut], second.at[cut], sems.at[1, j]))
    return ones, twos


def hidden_layer(x_ref, first, act, ones, tile, part, arrive):
    for j, copy in enumerate(ones):
        copy.wait()
        cols = slice(j * part, (j + 1) * part)
        for r in range(x_ref.shape[0] // tile):
            if j == 0:
                arrive(r)
            cut = slice(r * tile, (r + 1) * tile)
            half = jnp.dot(x_ref[cut, :] * BF16(0.5), first[:, cols], preferred_element_type=F32)
            act[cut, cols] = (half * jnp.tanh(half) + half).astype(BF16)


def encode_kernel(
    slots, code, weight_ref, feat_ref, x_hbm, first_hbm, second_hbm,
    enc_hbm, msg_ref, base_ref, loc_ref,
    x_ref, first, second, act, total, sems, io_sems,
):
    rows = feat_ref.shape[0]
    depth = feat_ref.shape[1]
    tile, part = tiles_of(x_ref.shape[0], first.shape[1])
    tiles = x_ref.shape[0] // tile
    ones, twos = weight_copies(first_hbm, second_hbm, first, second, sems, part)
    loads = [
        pltpu.make_async_copy(x_hbm.at[pl.ds(r * tile, tile)], x_ref.at[pl.ds(r * tile, tile)], io_sems.at[0, r])
        for r in range(tiles)
    ]
    loads[0].start()
    ones[0].start()
    for copy in loads[1:] + ones[1:] + twos:
        copy.start()
    total[...] = jnp.zeros_like(total)
    columns = jnp.transpose(weight_ref[...])
    hidden_layer(x_ref, first, act, ones, tile, part, lambda r: loads[r].wait())
    for copy in twos:
        copy.wait()
    stores = []
    for r in range(tiles):
        cut = slice(r * tile, (r + 1) * tile)
        out = jnp.dot(act[cut, :], second[...], preferred_element_type=F32)
        x_ref[cut, :] = (x_ref[cut, :].astype(F32) + out).astype(BF16)
        copy = pltpu.make_async_copy(x_ref.at[pl.ds(r * tile, tile)], enc_hbm.at[pl.ds(r * tile, tile)], io_sems.at[1, r])
        copy.start()
        stores.append(copy)
        for b in range(r * tile // rows, (r + 1) * tile // rows):
            slot = slots[b]
            block = x_ref[b * rows:(b + 1) * rows, :].astype(F32)
            total[slot] += columns[:, b:b + 1] * block
    spot = lax.broadcasted_iota(jnp.int32, (EXTRA, depth), 1)
    row = lax.broadcasted_iota(jnp.int32, (EXTRA, depth), 0)
    value = code[0].astype(F32)
    msg_ref[:rows, :] = total[0].astype(BF16)
    msg_ref[rows:, :] = jnp.where((spot == 1) & (row == 0), value, 0.0).astype(BF16)
    base_ref[:rows, :] = total[4].astype(BF16)
    base_ref[rows:2 * rows, :] = total[3].astype(BF16)
    base_ref[2 * rows:, :] = jnp.where((spot == 0) & (row == 0), value, 0.0).astype(BF16)
    loc_ref[:rows, :] = total[1]
    loc_ref[rows:, :] = total[2] + feat_ref[...].astype(F32)
    for copy in stores:
        copy.wait()


def encode(slots, code, weights, feat, grid, first, second):
    cells, depth = grid.shape
    hidden = first.shape[1]
    rows = feat.shape[0]
    tile, part = tiles_of(cells, hidden)
    return pl.pallas_call(
        encode_kernel,
        out_shape=(
            jax.ShapeDtypeStruct((cells, depth), BF16),
            pltpu.VMEM((rows + EXTRA, depth), BF16),
            pltpu.VMEM((2 * rows + EXTRA, depth), BF16),
            pltpu.VMEM((2 * rows, depth), F32),
        ),
        in_specs=[SMEM, SMEM, VMEM, VMEM, ANY, ANY, ANY],
        out_specs=(ANY, VMEM, VMEM, VMEM),
        scratch_shapes=[
            pltpu.VMEM((cells, depth), BF16),
            pltpu.VMEM((depth, hidden), BF16),
            pltpu.VMEM((hidden, depth), BF16),
            pltpu.VMEM((cells, hidden), BF16),
            pltpu.VMEM((2 * REACH + 1, rows, depth), F32),
            pltpu.SemaphoreType.DMA((2, hidden // part)),
            pltpu.SemaphoreType.DMA((2, cells // tile)),
        ],
        compiler_params=pltpu.CompilerParams(vmem_limit_bytes=32 << 20),
        cost_estimate=pl.CostEstimate(
            flops=4 * cells * depth * hidden, bytes_accessed=4 * (cells + hidden) * depth, transcendentals=cells * hidden
        ),
        name="encode",
    )(slots, code, weights, feat, grid, first, second)


def attend_kernel(
    dropped, own_ref, pair_ref, near_ref, far_ref, behind_ref, gain_ref, qkv_hbm, out_hbm,
    mesh_ref, ring_ref,
    w_qkv, w_out, normed, query, key_value, mixed, sems,
):
    rows, depth = own_ref.shape
    heads = depth // HD
    span = 2 * REACH + 1
    copies = [
        pltpu.make_async_copy(qkv_hbm, w_qkv, sems.at[0]),
        pltpu.make_async_copy(out_hbm, w_out, sems.at[1]),
    ]
    for copy in copies:
        copy.start()
    blocks = [
        behind_ref[...], pair_ref[:rows, :], pair_ref[rows:, :],
        near_ref[rows:, :], near_ref[:rows, :], far_ref[rows:, :], far_ref[:rows, :],
    ]
    for n, block in enumerate(blocks):
        state = block.astype(F32)
        scale = lax.rsqrt(jnp.mean(state * state, axis=-1, keepdims=True) + 1e-6)
        normed[n * rows:(n + 1) * rows, :] = (state * scale * gain_ref[...]).astype(BF16)
    copies[0].wait()
    key_value[...] = jnp.dot(normed[...], w_qkv[:, depth:], preferred_element_type=F32).astype(BF16)
    query[...] = jnp.dot(
        normed[REACH * rows:(REACH + 3) * rows, :], w_qkv[:, :depth], preferred_element_type=F32
    ).astype(BF16)
    lane_block = lax.broadcasted_iota(jnp.int32, (rows, span * rows), 1) // rows
    for p in range(3):
        keep = lane_block != dropped[p]
        window = slice(p * rows, (p + span) * rows)
        for h in range(heads):
            cols = slice(h * HD, (h + 1) * HD)
            scores = lax.dot_general(
                query[p * rows:(p + 1) * rows, cols], key_value[window, cols],
                (((1,), (1,)), ((), ())), preferred_element_type=F32,
            ) * (HD ** -0.5)
            scores = jnp.where(keep, scores, -jnp.inf)
            grown = jnp.exp(scores - jnp.max(scores, axis=-1, keepdims=True))
            share = 1.0 / jnp.sum(grown, axis=-1, keepdims=True)
            value = key_value[window, depth + h * HD:depth + (h + 1) * HD]
            mixed[p * rows:(p + 1) * rows, cols] = (
                jnp.dot(grown.astype(BF16), value, preferred_element_type=F32) * share
            ).astype(BF16)
    copies[1].wait()
    added = jnp.dot(mixed[...], w_out[...], preferred_element_type=F32)
    mesh_own = (own_ref[...] + added[:rows, :]).astype(BF16)
    mesh_ref[...] = mesh_own
    ring_ref[:rows, :] = mesh_own
    ring_ref[rows:2 * rows, :] = (near_ref[rows:, :].astype(F32) + added[rows:2 * rows, :]).astype(BF16)
    ring_ref[2 * rows:, :] = (near_ref[:rows, :].astype(F32) + added[2 * rows:, :]).astype(BF16)


def attend(dropped, own, pair, near, far, behind, gain, w_qkv, w_out):
    rows, depth = own.shape
    count = 2 * REACH + 3
    return pl.pallas_call(
        attend_kernel,
        out_shape=(
            jax.ShapeDtypeStruct((rows, depth), BF16),
            pltpu.VMEM((3 * rows, depth), BF16),
        ),
        in_specs=[SMEM, VMEM, VMEM, VMEM, VMEM, VMEM, VMEM, ANY, ANY],
        out_specs=(VMEM, VMEM),
        scratch_shapes=[
            pltpu.VMEM(w_qkv.shape, BF16),
            pltpu.VMEM(w_out.shape, BF16),
            pltpu.VMEM((count * rows, depth), BF16),
            pltpu.VMEM((3 * rows, depth), BF16),
            pltpu.VMEM((count * rows, 2 * depth), BF16),
            pltpu.VMEM((3 * rows, depth), BF16),
            pltpu.SemaphoreType.DMA((2,)),
        ],
        compiler_params=pltpu.CompilerParams(vmem_limit_bytes=32 << 20),
        name="attend",
    )(dropped, own, pair, near, far, behind, gain, w_qkv, w_out)


def decode_kernel(
    slots, weight_ref, ring_ref, back_ref, enc_hbm, first_hbm, second_hbm,
    out_hbm,
    x_ref, first, second, act, mesh, sems, io_sems,
):
    rows = back_ref.shape[0] // 2
    tile, part = tiles_of(x_ref.shape[0], first.shape[1])
    tiles = x_ref.shape[0] // tile
    ones, twos = weight_copies(first_hbm, second_hbm, first, second, sems, part)
    loads = [
        pltpu.make_async_copy(enc_hbm.at[pl.ds(r * tile, tile)], x_ref.at[pl.ds(r * tile, tile)], io_sems.at[0, r])
        for r in range(tiles)
    ]
    loads[0].start()
    ones[0].start()
    for copy in loads[1:] + ones[1:] + twos:
        copy.start()
    mesh[0] = back_ref[rows:, :]
    mesh[1] = back_ref[:rows, :]
    for n in range(3):
        mesh[2 + n] = ring_ref[n * rows:(n + 1) * rows, :]
    columns = jnp.transpose(weight_ref[...])

    def arrive(r):
        loads[r].wait()
        for b in range(r * tile // rows, (r + 1) * tile // rows):
            cut = slice(b * rows, (b + 1) * rows)
            read = mesh[slots[b]].astype(F32)
            x_ref[cut, :] = (x_ref[cut, :].astype(F32) + columns[:, b:b + 1] * read).astype(BF16)

    hidden_layer(x_ref, first, act, ones, tile, part, arrive)
    for copy in twos:
        copy.wait()
    stores = []
    for r in range(tiles):
        cut = slice(r * tile, (r + 1) * tile)
        out = jnp.dot(act[cut, :], second[...], preferred_element_type=F32)
        x_ref[cut, :] = (x_ref[cut, :].astype(F32) + out).astype(BF16)
        copy = pltpu.make_async_copy(x_ref.at[pl.ds(r * tile, tile)], out_hbm.at[pl.ds(r * tile, tile)], io_sems.at[1, r])
        copy.start()
        stores.append(copy)
    for copy in stores:
        copy.wait()


def decode(slots, weights, ring, back, encoded, first, second):
    cells, depth = encoded.shape
    hidden = first.shape[1]
    rows = back.shape[0] // 2
    tile, part = tiles_of(cells, hidden)
    return pl.pallas_call(
        decode_kernel,
        out_shape=jax.ShapeDtypeStruct((cells, depth), BF16),
        in_specs=[SMEM, VMEM, VMEM, VMEM, ANY, ANY, ANY],
        out_specs=ANY,
        scratch_shapes=[
            pltpu.VMEM((cells, depth), BF16),
            pltpu.VMEM((depth, hidden), BF16),
            pltpu.VMEM((hidden, depth), BF16),
            pltpu.VMEM((cells, hidden), BF16),
            pltpu.VMEM((2 * REACH + 1, rows, depth), BF16),
            pltpu.SemaphoreType.DMA((2, hidden // part)),
            pltpu.SemaphoreType.DMA((2, cells // tile)),
        ],
        compiler_params=pltpu.CompilerParams(vmem_limit_bytes=32 << 20),
        cost_estimate=pl.CostEstimate(
            flops=4 * cells * depth * hidden, bytes_accessed=4 * (cells + hidden) * depth, transcendentals=cells * hidden
        ),
        name="decode",
    )(slots, weights, ring, back, encoded, first, second)


def on_device(
    grid, g2m_owner, g2m_weight, m2g_owner, m2g_weight, mesh_feat, neighbours,
    enc_w1, enc_w2, attn_gain, w_qkv, w_out, dec_w1, dec_w2,
):
    mine = lax.axis_index(AXES)
    count = lax.axis_size(AXES)
    rows, depth = mesh_feat.shape
    nblocks = g2m_owner.shape[0]
    outward = 2 * lax.axis_index("sub") - 1

    def offset(owner):
        return (owner - mine + REACH) % count - REACH

    absent = -jnp.sum(offset(neighbours[0]))
    loc_slots = outward * offset(g2m_owner) + REACH
    read_slots = outward * offset(m2g_owner) + REACH

    encoded, message, base, local = encode(
        loc_slots, absent[None], g2m_weight.reshape(nblocks, rows), mesh_feat, grid, enc_w1, enc_w2
    )
    arrived = swapped(message)
    outgoing = (
        base.astype(F32) + jnp.pad(arrived.astype(F32), ((rows, 0), (0, 0)))
    ).astype(BF16)
    arrived = from_outward(outgoing, 1)
    shares = local + arrived[:2 * rows].astype(F32)
    absents = arrived[2 * rows, :2].astype(F32).astype(jnp.int32)
    dropped = outward * jnp.concatenate([absent[None], absents]) + REACH
    halves = shares.reshape(2, rows, depth)
    other = swapped(halves[::-1].astype(BF16).reshape(2 * rows, depth))
    state = shares + other.astype(F32)
    pair = state.astype(BF16)
    near = from_outward(pair, 1)
    far = from_outward(pair, 2)
    behind = swapped(near[rows:])
    mesh_out, ring = attend(
        dropped, state[rows:], pair, near, far, behind, attn_gain, w_qkv[0], w_out[0]
    )
    back = swapped(ring[:2 * rows])
    decoded = decode(
        read_slots, m2g_weight.reshape(nblocks, rows), ring, back, encoded, dec_w1, dec_w2
    )
    return (decoded, mesh_out)


def solution(mesh):
    split = P(AXES, None)
    flat = P(AXES)
    in_specs = (split, flat, flat, flat, flat, split, split) + (P(),) * 7
    return jax.shard_map(
        on_device, mesh=mesh, in_specs=in_specs, out_specs=(split, split), check_vma=False
    )
```

time: 88.3 us -> 66.3 us (0.75)
  Pallas kernels: 0 us -> 23.7 us
  matrix products: 23.3 us -> 0 us
  starting transfers between devices: 25.1 us -> 13 us
  waiting for transfers between devices: 21.8 us -> 15.7 us
  local copies, waits for them, and re-layouts: 13.1 us -> 7.2 us
  other arithmetic: 3.75 us -> 4.78 us
    pallas_call x0 -> x3, Pallas kernels: none -> 23.7 us  [the longest x1 8.54 us: decode(): pl.pallas_call(decode_kernel, out_shape=jax.ShapeDtypeStruct((cells, dept...]
    dot_general x6 -> x0, matrix products: 22.8 us -> none  [the longest x2 18.2 us: feed(): jnp.dot(active, second, preferred_element_type=jnp.float32)]
    ppermute x12 -> x7, starting transfers between devices: 25.1 us -> 13 us  [the longest x3 12.3 us: from_outward(): return lax.ppermute(block, AXES, route)]
    ppermute x12 -> x7, waiting for transfers between devices: 21.8 us -> 15.7 us  [the longest x3 11.6 us: from_outward(): return lax.ppermute(block, AXES, route)]
    gather x2 -> x0, local copies, waits for them, and re-layouts: 3.53 us -> none  [the longest x1 1.91 us: on_device(): far_kv = stacked[listed]]
    slice x2 -> x3, local copies, waits for them, and re-layouts: 2.29 us -> 0.05 us  [the longest x1 0.02 us: on_device(): state[rows:]]
    convert_element_type x1 -> x3, other arithmetic: 0.01 us -> 1.84 us  [the longest x1 1.12 us: on_device(): pair = state.astype(BF16)]
    add x0 -> x4, other arithmetic: none -> 1.64 us  [the longest x1 0.87 us: on_device(): shares = local + arrived[:2 * rows].astype(F32)]
  transfers between devices with their start and end apart: 12 -> 7, of which waited for: 9 -> 6; matrix products, arithmetic and copies ran while one was open for 3% -> 1% of each run, Pallas kernels for 0% -> 0%
where the time goes in v1:
time: 66.3 us; the launch traced here: 65.9 us
  Pallas kernels  23.7 us (36%)
  waiting for transfers between devices  15.7 us (24%)
  starting transfers between devices  13 us (20%)
  local copies, waits for them, and re-layouts  7.2 us (11%)
  other arithmetic  4.78 us (7%)
  between operations  1.58 us (2%)
    ppermute x3, starting transfers between devices, from_outward(): return lax.ppermute(block, AXES, route)  12.3 us
    ppermute x3, waiting for transfers between devices, from_outward(): return lax.ppermute(block, AXES, route)  11.6 us
    pallas_call x1, Pallas kernels, decode(): pl.pallas_call(decode_kernel, out_shape=jax.ShapeDtypeStruct((cells, dept...  8.54 us
    pallas_call x1, Pallas kernels, encode(): pl.pallas_call(encode_kernel, out_shape=(jax.ShapeDtypeStruct((cells, dep...  8.08 us
    pallas_call x1, Pallas kernels, attend(): pl.pallas_call(attend_kernel, out_shape=(jax.ShapeDtypeStruct((rows, dept...  7.07 us
    unnamed x26, local copies, waits for them, and re-layouts  6.02 us
    ppermute x4, waiting for transfers between devices, swapped(): return lax.ppermute(block, AXES, [(i, i ^ 1) for i in range(count)])  4.03 us
  transfers between devices with their start and end apart: 7, of which 6 were waited for; matrix products, arithmetic and copies ran while one was open for 1% of the time, Pallas kernels for 0%

profile of v1, /device:TPU:0, one launch (start us, length us, event | category | flops | bytes accessed | tf_op | source)
XLA Modules:
  0.0 65.9 jit_solution(10541496951015982625)
XLA Ops:
  0.6 1.3 %fusion.4 = s32[]{:T(128)} fusion(s32[1,3]{1,0:T(1,128)} %param.20, s32[]{:T(128)S(6)} %add.55), kind=kLoop, calls=%fused_computation.17 | loop fusion | flops 44 | bytes 20 | tf_op jit(solution)/shard_map/reduce_sum | solution.py:305
  2.6 0.7 %fusion.7.slots = s32[8]{0:T(128)S(1)} fusion(s32[8]{0:T(128)} %param.15, s32[]{:T(128)S(6)} %add.55, s32[]{:T(128)S(6)} %sub.29), kind=kLoop, calls=%fused_computation.20 | loop fusion | flops 128 | bytes 72 | tf_op jit(solution)/shard_map/add | solution.py:306
  3.3 1.6 %copy-done.3 = bf16[512,2048]{1,0:T(8,128)(2,1)S(1)} copy-done((bf16[512,2048]{1,0:T(8,128)(2,1)S(1)}, bf16[512,2048]{1,0:T(8,128)(2,1)}, u32[]{:S(2)}) %copy-start.3) | copy-done | bytes 2097176
  4.9 1.6 %copy-done.4 = bf16[2048,512]{1,0:T(8,128)(2,1)S(1)} copy-done((bf16[2048,512]{1,0:T(8,128)(2,1)S(1)}, bf16[2048,512]{1,0:T(8,128)(2,1)}, u32[]{:S(2)}) %copy-start.4) | copy-done | bytes 2097176
  6.5 1.2 %copy-done.7 = bf16[1024,512]{1,0:T(8,128)(2,1)S(1)} copy-done((bf16[1024,512]{1,0:T(8,128)(2,1)S(1)}, bf16[1024,512]{1,0:T(8,128)(2,1)}, u32[]{:S(2)}) %copy-start.7) | copy-done | bytes 1048600
  7.7 0.9 %copy-done.8 = bf16[128,512]{1,0:T(8,128)(2,1)S(1)} copy-done((bf16[128,512]{1,0:T(8,128)(2,1)S(1)}, bf16[128,512]{1,0:T(8,128)(2,1)}, u32[]{:S(2)}) %copy-start.8) | copy-done | bytes 131096
  8.6 0.7 %copy-done.9 = f32[1024]{0:T(1024)S(1)} copy-done((f32[1024]{0:T(1024)S(1)}, f32[1024]{0:T(1024)}, u32[]{:S(2)}) %copy-start.9) | copy-done | bytes 4120
  9.3 8.1 %encode.1 = (bf16[1024,512]{1,0:T(8,128)(2,1)S(1)}, bf16[144,512]{1,0:T(8,128)(2,1)S(1)}, bf16[272,512]{1,0:T(8,128)(2,1)S(1)}, f32[256,512]{1,0:T(8,128)S(1)}) custom-call(s32[8]{0:T(128)S(1)} %fusion.7.slots, s32[1]{0:T(128)} %bitcast.2.code, f32[8,128]{1,0:T(8,128)S(1)} %bitcast.13, bf16[128,512]{1,0:T(8,128)(2,1)S(1)} %copy-done.8, ...), custom_call_target="tpu_custom_call" | custom-call | flops 4294967296 | bytes 6291456 | tf_op jit(solution)/shard_map/encode/pallas_call | solution.py:115
  17.4 0.5 collective-permute-start
  17.9 1.0 %collective-permute-done = bf16[144,512]{1,0:T(8,128)(2,1)S(1)} collective-permute-done((bf16[144,512]{1,0:T(8,128)(2,1)S(1)}, bf16[144,512]{1,0:T(8,128)(2,1)S(1)}, u32[]{:S(2)}, u32[]{:S(2)}) %collective-permute-start) | collective-permute-done | bytes 147488 | tf_op jit(solution)/shard_map/ppermute | solution.py:23
  18.9 6.7 %collective-permute-start.1 = (bf16[272,512]{1,0:T(8,128)(2,1)S(1)}, bf16[272,512]{1,0:T(8,128)(2,1)S(1)}, u32[]{:S(2)}, u32[]{:S(2)}) collective-permute-start(bf16[272,512]{1,0:T(8,128)(2,1)S(1)} %add_convert_fusion), channel_id=1, source_target_pairs={{0,31},{1,2},{2,1},{3,4},{4,3},{5,6},{6,5},{7,8},{8,7},{9,10},{10,... | collective-permute-start | bytes 835592 | tf_op jit(solution)/shard_map/ppermute | solution.py:32
  25.6 4.3 %collective-permute-done.1 = bf16[272,512]{1,0:T(8,128)(2,1)S(1)} collective-permute-done((bf16[272,512]{1,0:T(8,128)(2,1)S(1)}, bf16[272,512]{1,0:T(8,128)(2,1)S(1)}, u32[]{:S(2)}, u32[]{:S(2)}) %collective-permute-start.1) | collective-permute-done | bytes 278560 | tf_op jit(solution)/shard_map/ppermute | solution.py:32
  29.9 0.9 %convert_add_fusion.1 = f32[256,512]{1,0:T(8,128)} fusion(f32[256,512]{1,0:T(8,128)S(1)} %get-tuple-element.10, bf16[272,512]{1,0:T(8,128)(2,1)S(1)} %collective-permute-done.1), kind=kLoop, calls=%fused_computation.3 | loop fusion | flops 262144 | bytes 1310720 | tf_op jit(solution)/shard_map/add | solution.py:317
  30.8 0.0 copy-done.11
  30.8 1.1 %rev.5 = bf16[2,128,512]{2,1,0:T(8,128)(2,1)S(1)} reverse(f32[2,128,512]{2,1,0:T(8,128)} %bitcast.15), dimensions={0} | reverse | bytes 786432 | tf_op jit(solution)/shard_map/rev | solution.py:321
  31.9 0.1 collective-permute-start.2
  32.0 1.5 %collective-permute-done.2 = bf16[256,512]{1,0:T(8,128)(2,1)S(1)} collective-permute-done((bf16[256,512]{1,0:T(8,128)(2,1)S(1)}, bf16[256,512]{1,0:T(8,128)(2,1)S(1)}, u32[]{:S(2)}, u32[]{:S(2)}) %collective-permute-start.2) | collective-permute-done | bytes 262176 | tf_op jit(solution)/shard_map/ppermute | solution.py:23
  33.5 1.1 %fusion.14 = (bf16[256,512]{1,0:T(8,128)(2,1)S(1)}, f32[256,512]{1,0:T(8,128)S(1)}) fusion(f32[256,512]{1,0:T(8,128)} %convert_add_fusion.1, bf16[256,512]{1,0:T(8,128)(2,1)S(1)} %collective-permute-done.2), kind=kLoop, calls=%fused_computation.29 | loop fusion | flops 393216 | bytes 1572864 | tf_op jit(solution)/shard_map/convert_element_type | solution.py:323
  34.7 5.3 %collective-permute-start.3 = (bf16[256,512]{1,0:T(8,128)(2,1)S(1)}, bf16[256,512]{1,0:T(8,128)(2,1)S(1)}, u32[]{:S(2)}, u32[]{:S(2)}) collective-permute-start(bf16[256,512]{1,0:T(8,128)(2,1)S(1)} %get-tuple-element.14.pair_ref), channel_id=1, source_target_pairs={{0,31},{1,2},{2,1},{3,4},{4,3},{5,6},{6,5},{7,8},{8,7},{9,10},{10,... | collective-permute-start | bytes 786440 | tf_op jit(solution)/shard_map/ppermute | solution.py:32
  40.0 0.3 collective-permute-start.4
  40.3 4.0 %collective-permute-done.3.near_ref = bf16[256,512]{1,0:T(8,128)(2,1)S(1)} collective-permute-done((bf16[256,512]{1,0:T(8,128)(2,1)S(1)}, bf16[256,512]{1,0:T(8,128)(2,1)S(1)}, u32[]{:S(2)}, u32[]{:S(2)}) %collective-permute-start.3) | collective-permute-done | bytes 262176 | tf_op jit(solution)/shard_map/ppermute | solution.py:32
  44.2 0.1 collective-permute-start.5
  44.3 0.7 %fusion.12 = s32[2]{0:T(128)S(1)} fusion(bf16[272,512]{1,0:T(8,128)(2,1)} %copy-done.11), kind=kLoop, calls=%fused_computation.26 | loop fusion | flops 4 | bytes 12 | tf_op jit(solution)/shard_map/convert_element_type | solution.py:318
  45.0 0.1 fusion.13.dropped
  45.1 3.3 %collective-permute-done.4.far_ref = bf16[256,512]{1,0:T(8,128)(2,1)S(1)} collective-permute-done((bf16[256,512]{1,0:T(8,128)(2,1)S(1)}, bf16[256,512]{1,0:T(8,128)(2,1)S(1)}, u32[]{:S(2)}, u32[]{:S(2)}) %collective-permute-start.4) | collective-permute-done | bytes 262176 | tf_op jit(solution)/shard_map/ppermute | solution.py:32
  48.5 0.0 collective-permute-done.5.behind_ref
  48.5 0.0 copy-done
  48.5 0.0 copy-done.1
  48.5 7.1 %attend.1 = (bf16[128,512]{1,0:T(8,128)(2,1)}, bf16[384,512]{1,0:T(8,128)(2,1)S(1)}) custom-call(s32[3]{0:T(128)S(1)} %fusion.13.dropped, f32[128,512]{1,0:T(8,128)S(1)} %slice.22.own_ref, bf16[256,512]{1,0:T(8,128)(2,1)S(1)} %get-tuple-element.14.pair_ref, bf16[256,512]{1,0:T(8,128)(2,1)S(1)} %collective-permute-done.3.near_ref, ...), custom_call_target="tpu_custom_call" | custom-call | tf_op jit(solution)/shard_map/attend/pallas_call | solution.py:198
  55.6 0.1 collective-permute-start.6
  55.7 1.5 %collective-permute-done.6.back_ref = bf16[256,512]{1,0:T(8,128)(2,1)S(1)} collective-permute-done((bf16[256,512]{1,0:T(8,128)(2,1)S(1)}, bf16[256,512]{1,0:T(8,128)(2,1)S(1)}, u32[]{:S(2)}, u32[]{:S(2)}) %collective-permute-start.6) | collective-permute-done | bytes 262176 | tf_op jit(solution)/shard_map/ppermute | solution.py:23
  57.2 8.5 %decode.1 = bf16[1024,512]{1,0:T(8,128)(2,1)} custom-call(s32[8]{0:T(128)S(1)} %fusion.2.slots, f32[8,128]{1,0:T(8,128)S(1)} %bitcast.14, bf16[384,512]{1,0:T(8,128)(2,1)S(1)} %get-tuple-element.11.ring_ref, bf16[256,512]{1,0:T(8,128)(2,1)S(1)} %collective-permute-done.6.back_ref, bf16[1024,512]{1,0:T(8,128)(2,1)S(1)} %get-tuple-element.12.enc_hbm, ...), custom_call_target="tpu_custom_call" | custom-call | flops 4294967296 | bytes 6291456 | tf_op jit(solution)/shard_map/decode/pallas_call | solution.py:270
  (23 shorter events, 0.1 us)
Async XLA Ops:
  3.3 1.6 %copy-start.3 = (bf16[512,2048]{1,0:T(8,128)(2,1)S(1)}, bf16[512,2048]{1,0:T(8,128)(2,1)}, u32[]{:S(2)}) copy-start(bf16[512,2048]{1,0:T(8,128)(2,1)} %first_hbm.2) | copy-start | bytes 6291460
  4.9 1.6 %copy-start.4 = (bf16[2048,512]{1,0:T(8,128)(2,1)S(1)}, bf16[2048,512]{1,0:T(8,128)(2,1)}, u32[]{:S(2)}) copy-start(bf16[2048,512]{1,0:T(8,128)(2,1)} %second_hbm.2) | copy-start | bytes 6291460
  6.5 1.2 %copy-start.7 = (bf16[1024,512]{1,0:T(8,128)(2,1)S(1)}, bf16[1024,512]{1,0:T(8,128)(2,1)}, u32[]{:S(2)}) copy-start(bf16[1024,512]{1,0:T(8,128)(2,1)} %x_hbm.1) | copy-start | bytes 3145732
  7.7 0.9 %copy-start.8 = (bf16[128,512]{1,0:T(8,128)(2,1)S(1)}, bf16[128,512]{1,0:T(8,128)(2,1)}, u32[]{:S(2)}) copy-start(bf16[128,512]{1,0:T(8,128)(2,1)} %feat_ref.1) | copy-start | bytes 393220
  8.6 0.7 %copy-start.9 = (f32[1024]{0:T(1024)S(1)}, f32[1024]{0:T(1024)}, u32[]{:S(2)}) copy-start(f32[1024]{0:T(1024)} %param.16) | copy-start | bytes 12292
  17.4 1.5 %collective-permute-start = (bf16[144,512]{1,0:T(8,128)(2,1)S(1)}, bf16[144,512]{1,0:T(8,128)(2,1)S(1)}, u32[]{:S(2)}, u32[]{:S(2)}) collective-permute-start(bf16[144,512]{1,0:T(8,128)(2,1)S(1)} %get-tuple-element.9), channel_id=1, source_target_pairs={{0,1},{1,0},{2,3},{3,2},{4,5},{5,4},{6,7},{7,6},{8,9},{9,8},{10,11... | collective-permute-start | bytes 442376 | tf_op jit(solution)/shard_map/ppermute | solution.py:23
  18.9 11.0 %collective-permute-start.1 = (bf16[272,512]{1,0:T(8,128)(2,1)S(1)}, bf16[272,512]{1,0:T(8,128)(2,1)S(1)}, u32[]{:S(2)}, u32[]{:S(2)}) collective-permute-start(bf16[272,512]{1,0:T(8,128)(2,1)S(1)} %add_convert_fusion), channel_id=1, source_target_pairs={{0,31},{1,2},{2,1},{3,4},{4,3},{5,6},{6,5},{7,8},{8,7},{9,10},{10,... | collective-permute-start | bytes 835592 | tf_op jit(solution)/shard_map/ppermute | solution.py:32
  29.9 0.9 %copy-start.11 = (bf16[272,512]{1,0:T(8,128)(2,1)}, bf16[272,512]{1,0:T(8,128)(2,1)S(1)}, u32[]{:S(2)}) copy-start(bf16[272,512]{1,0:T(8,128)(2,1)S(1)} %collective-permute-done.1) | copy-start | bytes 835588
  29.9 18.5 %copy-start = (bf16[1,512,1536]{2,1,0:T(8,128)(2,1)S(1)}, bf16[1,512,1536]{2,1,0:T(8,128)(2,1)}, u32[]{:S(2)}) copy-start(bf16[1,512,1536]{2,1,0:T(8,128)(2,1)} %param.24) | copy-start | bytes 4718596
  29.9 18.5 %copy-start.1 = (bf16[1,512,512]{2,1,0:T(8,128)(2,1)S(1)}, bf16[1,512,512]{2,1,0:T(8,128)(2,1)}, u32[]{:S(2)}) copy-start(bf16[1,512,512]{2,1,0:T(8,128)(2,1)} %param.25) | copy-start | bytes 1572868
  29.9 18.5 %copy-start.2 = (f32[1,512]{1,0:T(1,128)S(1)}, f32[1,512]{1,0:T(1,128)}, u32[]{:S(2)}) copy-start(f32[1,512]{1,0:T(1,128)} %gain_ref.1) | copy-start | bytes 6148
  31.9 1.6 %collective-permute-start.2 = (bf16[256,512]{1,0:T(8,128)(2,1)S(1)}, bf16[256,512]{1,0:T(8,128)(2,1)S(1)}, u32[]{:S(2)}, u32[]{:S(2)}) collective-permute-start(bf16[256,512]{1,0:T(8,128)(2,1)S(1)} %bitcast.16), channel_id=1, source_target_pairs={{0,1},{1,0},{2,3},{3,2},{4,5},{5,4},{6,7},{7,6},{8,9},{9,8},{10,11... | collective-permute-start | bytes 786440 | tf_op jit(solution)/shard_map/ppermute | solution.py:23
  34.7 9.6 %collective-permute-start.3 = (bf16[256,512]{1,0:T(8,128)(2,1)S(1)}, bf16[256,512]{1,0:T(8,128)(2,1)S(1)}, u32[]{:S(2)}, u32[]{:S(2)}) collective-permute-start(bf16[256,512]{1,0:T(8,128)(2,1)S(1)} %get-tuple-element.14.pair_ref), channel_id=1, source_target_pairs={{0,31},{1,2},{2,1},{3,4},{4,3},{5,6},{6,5},{7,8},{8,7},{9,10},{10,... | collective-permute-start | bytes 786440 | tf_op jit(solution)/shard_map/ppermute | solution.py:32
  40.0 8.5 %collective-permute-start.4 = (bf16[256,512]{1,0:T(8,128)(2,1)S(1)}, bf16[256,512]{1,0:T(8,128)(2,1)S(1)}, u32[]{:S(2)}, u32[]{:S(2)}) collective-permute-start(bf16[256,512]{1,0:T(8,128)(2,1)S(1)} %get-tuple-element.14.pair_ref), channel_id=1, source_target_pairs={{0,29},{1,4},{2,31},{3,6},{4,1},{5,8},{6,3},{7,10},{8,5},{9,12},{1... | collective-permute-start | bytes 786440 | tf_op jit(solution)/shard_map/ppermute | solution.py:32
  44.2 4.2 %collective-permute-start.5 = (bf16[128,512]{1,0:T(8,128)(2,1)S(1)}, bf16[128,512]{1,0:T(8,128)(2,1)S(1)}, u32[]{:S(2)}, u32[]{:S(2)}) collective-permute-start(bf16[128,512]{1,0:T(8,128)(2,1)S(1)} %slice.23), channel_id=1, source_target_pairs={{0,1},{1,0},{2,3},{3,2},{4,5},{5,4},{6,7},{7,6},{8,9},{9,8},{10,11... | collective-permute-start | bytes 393224 | tf_op jit(solution)/shard_map/ppermute | solution.py:23
  45.1 10.6 %copy-start.12 = (s32[8]{0:T(128)S(1)}, s32[8]{0:T(128)}, u32[]{:S(2)}) copy-start(s32[8]{0:T(128)} %param.17) | copy-start | bytes 100
  45.1 12.1 %copy-start.5 = (bf16[512,2048]{1,0:T(8,128)(2,1)S(1)}, bf16[512,2048]{1,0:T(8,128)(2,1)}, u32[]{:S(2)}) copy-start(bf16[512,2048]{1,0:T(8,128)(2,1)} %first_hbm.3) | copy-start | bytes 6291460
  45.1 12.1 %copy-start.6 = (bf16[2048,512]{1,0:T(8,128)(2,1)S(1)}, bf16[2048,512]{1,0:T(8,128)(2,1)}, u32[]{:S(2)}) copy-start(bf16[2048,512]{1,0:T(8,128)(2,1)} %second_hbm.3) | copy-start | bytes 6291460
  45.1 12.1 %copy-start.10 = (f32[1024]{0:T(1024)S(1)}, f32[1024]{0:T(1024)}, u32[]{:S(2)}) copy-start(f32[1024]{0:T(1024)} %param.18) | copy-start | bytes 12292
  55.6 1.6 %collective-permute-start.6 = (bf16[256,512]{1,0:T(8,128)(2,1)S(1)}, bf16[256,512]{1,0:T(8,128)(2,1)S(1)}, u32[]{:S(2)}, u32[]{:S(2)}) collective-permute-start(bf16[256,512]{1,0:T(8,128)(2,1)S(1)} %slice.19), channel_id=1, source_target_pairs={{0,1},{1,0},{2,3},{3,2},{4,5},{5,4},{6,7},{7,6},{8,9},{9,8},{10,11... | collective-permute-start | bytes 786440 | tf_op jit(solution)/shard_map/ppermute | solution.py:23

commit v2 on v1

v2 whole, which is shorter than its diff:
```python
import functools

import jax
import jax.numpy as jnp
from jax import lax
from jax.experimental import pallas as pl
from jax.experimental.pallas import tpu as pltpu
from jax.sharding import PartitionSpec as P

HD = 128
REACH = 2
EXTRA = 16
AXES = ("tile", "sub")
BF16 = jnp.bfloat16
F32 = jnp.float32
VMEM = pl.BlockSpec(memory_space=pltpu.VMEM)
SMEM = pl.BlockSpec(memory_space=pltpu.SMEM)
ANY = pl.BlockSpec(memory_space=pl.ANY)


def swapped(block):
    count = lax.axis_size(AXES)
    return lax.ppermute(block, AXES, [(i, i ^ 1) for i in range(count)])


def from_outward(block, chips):
    count = lax.axis_size(AXES)
    route = []
    for i in range(count):
        step = 2 * chips - 1
        route.append((i, (i + step if i % 2 else i - step) % count))
    return lax.ppermute(block, AXES, route)


def tiles_of(rows, columns):
    return min(rows, 256), min(columns, 512)


def outward_of():
    return 2 * lax.axis_index("sub") - 1


def offset_of(owner, mine, count):
    return lax.rem(owner - mine + REACH + count, count) - REACH


def kept(shape, dtype=BF16):
    return pltpu.VMEM(shape, dtype)


def in_hbm(*arrays):
    return [pltpu.with_memory_space_constraint(a, pltpu.HBM) for a in arrays]


def hidden_layer(x_ref, first, act, tile, part, arrive, before):
    for j in range(first.shape[1] // part):
        before(j)
        cols = slice(j * part, (j + 1) * part)
        for r in range(x_ref.shape[0] // tile):
            if j == 0:
                arrive(r)
            cut = slice(r * tile, (r + 1) * tile)
            half = jnp.dot(x_ref[cut, :] * BF16(0.5), first[:, cols], preferred_element_type=F32)
            act[cut, cols] = (half * jnp.tanh(half) + half).astype(BF16)


def encode_kernel(
    owner, listed, weight_hbm, feat_hbm, x_hbm, first_hbm, second_hbm,
    enc_ref, msg_ref, base_ref, loc_ref,
    weight_ref, feat_ref, first, second, act, total, sems, io_sems,
):
    rows, depth = feat_ref.shape
    tile, part = tiles_of(enc_ref.shape[0], first.shape[1])
    tiles, parts = enc_ref.shape[0] // tile, first.shape[1] // part
    loads = [
        pltpu.make_async_copy(x_hbm.at[pl.ds(r * tile, tile)], enc_ref.at[pl.ds(r * tile, tile)], io_sems.at[r])
        for r in range(tiles)
    ]
    ones, twos = [], []
    for j in range(parts):
        cut = pl.ds(j * part, part)
        ones.append(pltpu.make_async_copy(first_hbm.at[:, cut], first.at[:, cut], sems.at[0, j]))
        twos.append(pltpu.make_async_copy(second_hbm.at[cut], second.at[cut], sems.at[1, j]))
    small = [
        pltpu.make_async_copy(weight_hbm, weight_ref, io_sems.at[tiles]),
        pltpu.make_async_copy(feat_hbm, feat_ref, io_sems.at[tiles + 1]),
    ]
    for copy in [loads[0], ones[0]] + loads[1:] + ones[1:] + twos + small:
        copy.start()
    mine, count = lax.axis_index(AXES), lax.axis_size(AXES)
    outward = outward_of()
    total[...] = jnp.zeros_like(total)
    hidden_layer(
        enc_ref, first, act, tile, part, lambda r: loads[r].wait(), lambda j: ones[j].wait()
    )
    for copy in twos + small:
        copy.wait()
    columns = jnp.transpose(weight_ref[...])
    for r in range(tiles):
        cut = slice(r * tile, (r + 1) * tile)
        out = jnp.dot(act[cut, :], second[...], preferred_element_type=F32)
        enc_ref[cut, :] = (enc_ref[cut, :].astype(F32) + out).astype(BF16)
        for b in range(r * tile // rows, (r + 1) * tile // rows):
            slot = outward * offset_of(owner[b], mine, count) + REACH
            block = enc_ref[b * rows:(b + 1) * rows, :].astype(F32)
            total[slot] += columns[:, b:b + 1] * block
    absent = sum(-offset_of(listed[0, n], mine, count) for n in range(listed.shape[1])).astype(F32)
    spot = lax.broadcasted_iota(jnp.int32, (EXTRA, depth), 1)
    msg_ref[:rows, :] = total[0].astype(BF16)
    msg_ref[rows:, :] = jnp.where(spot == 1, absent, 0.0).astype(BF16)
    base_ref[:rows, :] = total[4].astype(BF16)
    base_ref[rows:2 * rows, :] = total[3].astype(BF16)
    base_ref[2 * rows:, :] = jnp.where(spot == 0, absent, 0.0).astype(BF16)
    loc_ref[:rows, :] = total[1]
    loc_ref[rows:, :] = total[2] + feat_ref[...].astype(F32)


def encode(owner, listed, weights, feat, grid, first, second):
    cells, depth = grid.shape
    hidden = first.shape[1]
    rows = feat.shape[0]
    tile, part = tiles_of(cells, hidden)
    return pl.pallas_call(
        encode_kernel,
        out_shape=(
            kept((cells, depth)),
            kept((rows + EXTRA, depth)),
            kept((2 * rows + EXTRA, depth)),
            kept((2 * rows, depth), F32),
        ),
        in_specs=[SMEM, SMEM] + [ANY] * 5,
        out_specs=(VMEM,) * 4,
        scratch_shapes=[
            pltpu.VMEM(weights.shape, F32),
            pltpu.VMEM(feat.shape, BF16),
            pltpu.VMEM((depth, hidden), BF16),
            pltpu.VMEM((hidden, depth), BF16),
            pltpu.VMEM((cells, hidden), BF16),
            pltpu.VMEM((2 * REACH + 1, rows, depth), F32),
            pltpu.SemaphoreType.DMA((2, hidden // part)),
            pltpu.SemaphoreType.DMA((cells // tile + 2,)),
        ],
        compiler_params=pltpu.CompilerParams(vmem_limit_bytes=24 << 20),
        cost_estimate=pl.CostEstimate(
            flops=4 * cells * depth * hidden, bytes_accessed=4 * (cells + hidden) * depth, transcendentals=cells * hidden
        ),
        name="encode",
    )(owner, listed, *in_hbm(weights, feat, grid, first, second))


def outgoing_kernel(base_ref, arrived_ref, out_ref):
    rows = arrived_ref.shape[0] - EXTRA
    out_ref[:rows, :] = base_ref[:rows, :]
    out_ref[rows:, :] = (base_ref[rows:, :].astype(F32) + arrived_ref[...].astype(F32)).astype(BF16)


def outgoing_sums(base, arrived):
    return pl.pallas_call(
        outgoing_kernel, out_shape=kept(base.shape), in_specs=[VMEM] * 2, out_specs=VMEM, name="outgoing_sums"
    )(base, arrived)


def share_kernel(loc_ref, arrived_ref, share_ref, msg_ref):
    rows = loc_ref.shape[0] // 2
    share_ref[...] = loc_ref[...] + arrived_ref[:2 * rows, :].astype(F32)
    msg_ref[:rows, :] = share_ref[rows:, :].astype(BF16)
    msg_ref[rows:, :] = share_ref[:rows, :].astype(BF16)


def chip_share(local, arrived):
    return pl.pallas_call(
        share_kernel,
        out_shape=(kept(local.shape, F32), kept(local.shape)),
        in_specs=[VMEM] * 2,
        out_specs=(VMEM,) * 2,
        name="chip_share",
    )(local, arrived)


def state_kernel(share_ref, other_ref, own_ref, pair_ref):
    rows = own_ref.shape[0]
    own_ref[...] = share_ref[rows:, :] + other_ref[rows:, :].astype(F32)
    pair_ref[:rows, :] = (share_ref[:rows, :] + other_ref[:rows, :].astype(F32)).astype(BF16)
    pair_ref[rows:, :] = own_ref[...].astype(BF16)


def chip_states(share, other):
    rows, depth = share.shape[0] // 2, share.shape[1]
    return pl.pallas_call(
        state_kernel,
        out_shape=(kept((rows, depth), F32), kept(share.shape)),
        in_specs=[VMEM] * 2,
        out_specs=(VMEM,) * 2,
        name="chip_states",
    )(share, other)


def normal(block, gain):
    state = block.astype(F32)
    scale = lax.rsqrt(jnp.mean(state * state, axis=-1, keepdims=True) + 1e-6)
    return (state * scale * gain).astype(BF16)


def project_kernel(state_ref, gain_ref, w_qkv, out_ref):
    rows = normal(state_ref[...], gain_ref[...])
    out_ref[...] = jnp.dot(rows, w_qkv[...], preferred_element_type=F32).astype(BF16)


def project(states, gain, w_qkv):
    rows, depth = states.shape
    return pl.pallas_call(
        project_kernel,
        out_shape=kept((rows, w_qkv.shape[1])),
        in_specs=[VMEM] * 3,
        out_specs=VMEM,
        compiler_params=pltpu.CompilerParams(vmem_limit_bytes=16 << 20),
        cost_estimate=pl.CostEstimate(
            flops=2 * rows * depth * w_qkv.shape[1], bytes_accessed=2 * rows * depth, transcendentals=0
        ),
        name="project",
    )(states, gain, w_qkv)


def attend_kernel(
    listed, code_ref, own_ref, qkv_pair, near_ref, qkv_near, far_ref, behind_ref, gain_ref, w_qkv, w_out,
    ring_ref,
    kv_far, kv_behind, mixed,
):
    rows, depth = own_ref.shape
    heads = depth // HD
    span = 2 * REACH + 1
    mine, count = lax.axis_index(AXES), lax.axis_size(AXES)
    outward = outward_of()
    gain = gain_ref[...]
    kv_far[...] = jnp.dot(normal(far_ref[...], gain), w_qkv[:, depth:], preferred_element_type=F32).astype(BF16)
    kv_behind[...] = jnp.dot(normal(behind_ref[...], gain), w_qkv[:, depth:], preferred_element_type=F32).astype(BF16)
    window = [
        (kv_behind, 0, 0), (qkv_pair, 0, depth), (qkv_pair, 1, depth), (qkv_near, 1, depth),
        (qkv_near, 0, depth), (kv_far, 1, 0), (kv_far, 0, 0),
    ]
    absent = sum(-offset_of(listed[0, n], mine, count) for n in range(listed.shape[1]))
    dropped = [
        (outward * absent + REACH).astype(F32),
        outward.astype(F32) * code_ref[0:1, 0:1].astype(F32) + REACH,
        outward.astype(F32) * code_ref[0:1, 1:2].astype(F32) + REACH,
    ]
    lane_block = (lax.broadcasted_iota(jnp.int32, (rows, span * rows), 1) // rows).astype(F32)
    queries = [(qkv_pair, 1), (qkv_near, 1), (qkv_near, 0)]
    for p, (q_ref, q_block) in enumerate(queries):
        keep = lane_block != dropped[p]
        for h in range(heads):
            cols = slice(h * HD, (h + 1) * HD)
            query = q_ref[q_block * rows:(q_block + 1) * rows, cols]
            parts = []
            for ref, block, start in window[p:p + span]:
                key = ref[block * rows:(block + 1) * rows, start + h * HD:start + (h + 1) * HD]
                parts.append(lax.dot_general(
                    query, key, (((1,), (1,)), ((), ())), preferred_element_type=F32
                ))
            scores = jnp.concatenate(parts, axis=1) * (HD ** -0.5)
            scores = jnp.where(keep, scores, -jnp.inf)
            grown = jnp.exp(scores - jnp.max(scores, axis=-1, keepdims=True))
            share = 1.0 / jnp.sum(grown, axis=-1, keepdims=True)
            grown = grown.astype(BF16)
            taken = None
            for n, (ref, block, start) in enumerate(window[p:p + span]):
                left = start + depth + h * HD
                value = ref[block * rows:(block + 1) * rows, left:left + HD]
                term = jnp.dot(grown[:, n * rows:(n + 1) * rows], value, preferred_element_type=F32)
                taken = term if taken is None else taken + term
            mixed[p * rows:(p + 1) * rows, cols] = (taken * share).astype(BF16)
    added = jnp.dot(mixed[...], w_out[...], preferred_element_type=F32)
    ring_ref[:rows, :] = (own_ref[...] + added[:rows, :]).astype(BF16)
    ring_ref[rows:2 * rows, :] = (near_ref[rows:, :].astype(F32) + added[rows:2 * rows, :]).astype(BF16)
    ring_ref[2 * rows:, :] = (near_ref[:rows, :].astype(F32) + added[2 * rows:, :]).astype(BF16)


def attend(listed, codes, own, qkv_pair, near, qkv_near, far, behind, gain, w_qkv, w_out):
    rows, depth = own.shape
    return pl.pallas_call(
        attend_kernel,
        out_shape=kept((3 * rows, depth)),
        in_specs=[SMEM] + [VMEM] * 10,
        out_specs=VMEM,
        scratch_shapes=[
            pltpu.VMEM((2 * rows, 2 * depth), BF16),
            pltpu.VMEM((rows, 2 * depth), BF16),
            pltpu.VMEM((3 * rows, depth), BF16),
        ],
        compiler_params=pltpu.CompilerParams(vmem_limit_bytes=16 << 20),
        name="attend",
    )(listed, codes, own, qkv_pair, near, qkv_near, far, behind, gain, w_qkv, w_out)


def decode_kernel(
    owner, weight_ref, ring_ref, back_ref, enc_ref, first, second,
    out_hbm, mesh_hbm,
    x_ref, act, mesh, io_sems,
):
    rows = back_ref.shape[0] // 2
    tile, part = tiles_of(x_ref.shape[0], first.shape[1])
    tiles = x_ref.shape[0] // tile
    stores = [pltpu.make_async_copy(ring_ref.at[pl.ds(0, rows)], mesh_hbm, io_sems.at[tiles])]
    stores[0].start()
    mine, count = lax.axis_index(AXES), lax.axis_size(AXES)
    outward = outward_of()
    mesh[0] = back_ref[rows:, :]
    mesh[1] = back_ref[:rows, :]
    for n in range(3):
        mesh[2 + n] = ring_ref[n * rows:(n + 1) * rows, :]
    columns = jnp.transpose(weight_ref[...])

    def arrive(r):
        for b in range(r * tile // rows, (r + 1) * tile // rows):
            cut = slice(b * rows, (b + 1) * rows)
            slot = outward * offset_of(owner[b], mine, count) + REACH
            read = mesh[slot].astype(F32)
            x_ref[cut, :] = (enc_ref[cut, :].astype(F32) + columns[:, b:b + 1] * read).astype(BF16)

    hidden_layer(x_ref, first, act, tile, part, arrive, lambda j: None)
    for r in range(tiles):
        cut = slice(r * tile, (r + 1) * tile)
        out = jnp.dot(act[cut, :], second[...], preferred_element_type=F32)
        x_ref[cut, :] = (x_ref[cut, :].astype(F32) + out).astype(BF16)
        copy = pltpu.make_async_copy(x_ref.at[pl.ds(r * tile, tile)], out_hbm.at[pl.ds(r * tile, tile)], io_sems.at[r])
        copy.start()
        stores.append(copy)
    for copy in stores:
        copy.wait()


def decode(owner, weights, ring, back, encoded, first, second):
    cells, depth = encoded.shape
    hidden = first.shape[1]
    rows = back.shape[0] // 2
    tile, part = tiles_of(cells, hidden)
    return pl.pallas_call(
        decode_kernel,
        out_shape=(jax.ShapeDtypeStruct((cells, depth), BF16), jax.ShapeDtypeStruct((rows, depth), BF16)),
        in_specs=[SMEM] + [VMEM] * 6,
        out_specs=(ANY, ANY),
        scratch_shapes=[
            pltpu.VMEM((cells, depth), BF16),
            pltpu.VMEM((cells, hidden), BF16),
            pltpu.VMEM((2 * REACH + 1, rows, depth), BF16),
            pltpu.SemaphoreType.DMA((cells // tile + 1,)),
        ],
        compiler_params=pltpu.CompilerParams(vmem_limit_bytes=24 << 20),
        cost_estimate=pl.CostEstimate(
            flops=4 * cells * depth * hidden, bytes_accessed=4 * (cells + hidden) * depth, transcendentals=cells * hidden
        ),
        name="decode",
    )(owner, weights, ring, back, encoded, first, second)


def on_device(
    grid, g2m_owner, g2m_weight, m2g_owner, m2g_weight, mesh_feat, neighbours,
    enc_w1, enc_w2, attn_gain, w_qkv, w_out, dec_w1, dec_w2,
):
    rows = mesh_feat.shape[0]
    nblocks = g2m_owner.shape[0]
    encoded, message, base, local = encode(
        g2m_owner, neighbours, g2m_weight.reshape(nblocks, rows), mesh_feat, grid, enc_w1, enc_w2
    )
    sums = from_outward(outgoing_sums(base, swapped(message)), 1)
    share, message = chip_share(local, sums)
    own, pair = chip_states(share, swapped(message))
    near = from_outward(pair, 1)
    far = from_outward(pair, 2)
    behind = swapped(near[rows:])
    qkv_pair = project(pair, attn_gain, w_qkv[0])
    qkv_near = project(near, attn_gain, w_qkv[0])
    ring = attend(
        neighbours, sums[2 * rows:], own, qkv_pair, near, qkv_near, far, behind, attn_gain, w_qkv[0], w_out[0]
    )
    back = swapped(ring[:2 * rows])
    return decode(m2g_owner, m2g_weight.reshape(nblocks, rows), ring, back, encoded, dec_w1, dec_w2)


def solution(mesh):
    split = P(AXES, None)
    flat = P(AXES)
    in_specs = (split, flat, flat, flat, flat, split, split) + (P(),) * 7
    return jax.shard_map(
        on_device, mesh=mesh, in_specs=in_specs, out_specs=(split, split), check_vma=False
    )
```

time: 66.3 us -> 59.6 us (0.90)
  other arithmetic: 4.78 us -> 0 us
  Pallas kernels: 23.7 us -> 25.2 us
  local copies, waits for them, and re-layouts: 7.2 us -> 5.74 us
  waiting for transfers between devices: 15.7 us -> 14.6 us
    convert_element_type x3 -> x0, other arithmetic: 1.84 us -> none  [the longest x1 1.12 us: on_device(): pair = state.astype(BF16)]
    add x4 -> x0, other arithmetic: 1.64 us -> none  [the longest x1 0.87 us: on_device(): shares = local + arrived[:2 * rows].astype(F32)]
    pallas_call x3 -> x8, Pallas kernels: 23.7 us -> 25.2 us  [the longest x1 8.08 us: encode(): pl.pallas_call(encode_kernel, out_shape=(kept((cells, depth)), kept((rows...]
    reduce_sum x1 -> x0, other arithmetic: 1.3 us -> none  [on_device(): absent = -jnp.sum(offset(neighbours[0]))]
    rev x1 -> x0, local copies, waits for them, and re-layouts: 1.13 us -> none  [on_device(): other = swapped(halves[::-1].astype(BF16).reshape(2 * rows, depth))]
    ppermute x3, waiting for transfers between devices: 11.6 us -> 10.5 us  [from_outward(): return lax.ppermute(block, AXES, route)]
    unnamed x26 -> x30, local copies, waits for them, and re-layouts: 6.02 us -> 4.99 us
    slice x1, local copies, waits for them, and re-layouts: 0.02 us -> 0.72 us  [on_device(): sums[2 * rows:]]
  transfers between devices with their start and end apart: 7 -> 7, of which waited for: 6 -> 6; matrix products, arithmetic and copies ran while one was open for 1% -> 1% of each run, Pallas kernels for 0% -> 2%
where the time goes in v2:
time: 59.6 us; the launch traced here: 59.4 us
  Pallas kernels  25.2 us (42%)
  waiting for transfers between devices  14.6 us (24%)
  starting transfers between devices  12.9 us (22%)
  local copies, waits for them, and re-layouts  5.74 us (10%)
  between operations  0.95 us (2%)
    ppermute x3, starting transfers between devices, from_outward(): return lax.ppermute(block, AXES, route)  12.3 us
    ppermute x3, waiting for transfers between devices, from_outward(): return lax.ppermute(block, AXES, route)  10.5 us
    pallas_call x1, Pallas kernels, encode(): pl.pallas_call(encode_kernel, out_shape=(kept((cells, depth)), kept((rows...  8.08 us
    pallas_call x1, Pallas kernels, decode(): pl.pallas_call(decode_kernel, out_shape=(jax.ShapeDtypeStruct((cells, dep...  6.46 us
    pallas_call x1, Pallas kernels, attend(): pl.pallas_call(attend_kernel, out_shape=kept((3 * rows, depth)), in_specs...  6 us
    unnamed x30, local copies, waits for them, and re-layouts  4.99 us
    ppermute x4, waiting for transfers between devices, swapped(): return lax.ppermute(block, AXES, [(i, i ^ 1) for i in range(count)])  4.06 us
    pallas_call x2, Pallas kernels, project(): pl.pallas_call(project_kernel, out_shape=kept((rows, w_qkv.shape[1])), in...  1.26 us
  transfers between devices with their start and end apart: 7, of which 6 were waited for; matrix products, arithmetic and copies ran while one was open for 1% of the time, Pallas kernels for 2%

profile of v2, /device:TPU:0, one launch (start us, length us, event | category | flops | bytes accessed | tf_op | source)
XLA Modules:
  0.0 59.4 jit_solution(477005834939565070)
XLA Ops:
  0.6 0.6 %copy-done.6 = s32[1,3]{1,0:T(1,128)S(1)} copy-done((s32[1,3]{1,0:T(1,128)S(1)}, s32[1,3]{1,0:T(1,128)}, u32[]{:S(2)}) %copy-start.6) | copy-done | bytes 36
  1.3 0.7 %copy-done.11 = s32[8]{0:T(128)S(1)} copy-done((s32[8]{0:T(128)S(1)}, s32[8]{0:T(128)}, u32[]{:S(2)}) %copy-start.11) | copy-done | bytes 56
  1.9 8.1 %encode.1 = (bf16[1024,512]{1,0:T(8,128)(2,1)S(1)}, bf16[144,512]{1,0:T(8,128)(2,1)S(1)}, bf16[272,512]{1,0:T(8,128)(2,1)S(1)}, f32[256,512]{1,0:T(8,128)S(1)}) custom-call(s32[8]{0:T(128)S(1)} %copy-done.11, s32[1,3]{1,0:T(1,128)S(1)} %copy-done.6, f32[8,128]{1,0:T(8,128)} %bitcast.9, bf16[128,512]{1,0:T(8,128)(2,1)} %feat_hbm.1, bf16[1024,512]{1,0:T(8,128)(2,1)} %x_hbm.1, ...), custom_call_target="tpu_custom_call" | custom-call | flops 4294967296 | bytes 6291456 | tf_op jit(solution)/shard_map/encode/pallas_call | solution.py:123
  10.0 0.8 %copy-done.3 = f32[256,512]{1,0:T(8,128)} copy-done((f32[256,512]{1,0:T(8,128)}, f32[256,512]{1,0:T(8,128)S(1)}, u32[]{:S(2)}) %copy-start.3) | copy-done | bytes 524312
  10.8 0.7 %copy-done.4 = bf16[272,512]{1,0:T(8,128)(2,1)} copy-done((bf16[272,512]{1,0:T(8,128)(2,1)}, bf16[272,512]{1,0:T(8,128)(2,1)S(1)}, u32[]{:S(2)}) %copy-start.4) | copy-done | bytes 278552
  11.6 0.5 collective-permute-start
  12.0 1.0 %collective-permute-done.arrived_ref = bf16[144,512]{1,0:T(8,128)(2,1)S(1)} collective-permute-done((bf16[144,512]{1,0:T(8,128)(2,1)S(1)}, bf16[144,512]{1,0:T(8,128)(2,1)S(1)}, u32[]{:S(2)}, u32[]{:S(2)}) %collective-permute-start) | collective-permute-done | bytes 147488 | tf_op jit(solution)/shard_map/ppermute | solution.py:23
  13.0 0.6 %copy-done.14 = bf16[144,512]{1,0:T(8,128)(2,1)} copy-done((bf16[144,512]{1,0:T(8,128)(2,1)}, bf16[144,512]{1,0:T(8,128)(2,1)S(1)}, u32[]{:S(2)}) %copy-start.14) | copy-done | bytes 147480
  13.7 1.0 %outgoing_sums.1 = bf16[272,512]{1,0:T(8,128)(2,1)S(1)} custom-call(bf16[272,512]{1,0:T(8,128)(2,1)} %copy-done.4, bf16[144,512]{1,0:T(8,128)(2,1)} %copy-done.14), custom_call_target="tpu_custom_call" | custom-call | tf_op jit(solution)/shard_map/outgoing_sums/pallas_call | solution.py:158
  14.7 6.7 %collective-permute-start.1 = (bf16[272,512]{1,0:T(8,128)(2,1)S(1)}, bf16[272,512]{1,0:T(8,128)(2,1)}, u32[]{:S(2)}, u32[]{:S(2)}) collective-permute-start(bf16[272,512]{1,0:T(8,128)(2,1)S(1)} %outgoing_sums.1), channel_id=1, source_target_pairs={{0,31},{1,2},{2,1},{3,4},{4,3},{5,6},{6,5},{7,8},{8,7},{9,10},{10,... | collective-permute-start | bytes 835592 | tf_op jit(solution)/shard_map/ppermute | solution.py:32
  21.4 4.4 %collective-permute-done.1.arrived_ref = bf16[272,512]{1,0:T(8,128)(2,1)} collective-permute-done((bf16[272,512]{1,0:T(8,128)(2,1)S(1)}, bf16[272,512]{1,0:T(8,128)(2,1)}, u32[]{:S(2)}, u32[]{:S(2)}) %collective-permute-start.1) | collective-permute-done | bytes 278560 | tf_op jit(solution)/shard_map/ppermute | solution.py:32
  25.8 1.2 %chip_share.1 = (f32[256,512]{1,0:T(8,128)S(1)}, bf16[256,512]{1,0:T(8,128)(2,1)S(1)}) custom-call(f32[256,512]{1,0:T(8,128)} %copy-done.3, bf16[272,512]{1,0:T(8,128)(2,1)} %collective-permute-done.1.arrived_ref), custom_call_target="tpu_custom_call" | custom-call | tf_op jit(solution)/shard_map/chip_share/pallas_call | solution.py:171
  27.0 0.0 copy-start.2
  27.0 0.8 %copy-done.2 = f32[256,512]{1,0:T(8,128)} copy-done((f32[256,512]{1,0:T(8,128)}, f32[256,512]{1,0:T(8,128)S(1)}, u32[]{:S(2)}) %copy-start.2) | copy-done | bytes 524312
  27.8 1.5 %collective-permute-done.2.other_ref = bf16[256,512]{1,0:T(8,128)(2,1)S(1)} collective-permute-done((bf16[256,512]{1,0:T(8,128)(2,1)S(1)}, bf16[256,512]{1,0:T(8,128)(2,1)S(1)}, u32[]{:S(2)}, u32[]{:S(2)}) %collective-permute-start.2) | collective-permute-done | bytes 262176 | tf_op jit(solution)/shard_map/ppermute | solution.py:23
  29.4 0.7 %copy-done.13 = bf16[256,512]{1,0:T(8,128)(2,1)} copy-done((bf16[256,512]{1,0:T(8,128)(2,1)}, bf16[256,512]{1,0:T(8,128)(2,1)S(1)}, u32[]{:S(2)}) %copy-start.13) | copy-done | bytes 262168
  30.1 1.2 %chip_states.1 = (f32[128,512]{1,0:T(8,128)S(1)}, bf16[256,512]{1,0:T(8,128)(2,1)S(1)}) custom-call(f32[256,512]{1,0:T(8,128)} %copy-done.2, bf16[256,512]{1,0:T(8,128)(2,1)} %copy-done.13), custom_call_target="tpu_custom_call" | custom-call | tf_op jit(solution)/shard_map/chip_states/pallas_call | solution.py:189
  31.2 5.3 %collective-permute-start.3 = (bf16[256,512]{1,0:T(8,128)(2,1)S(1)}, bf16[256,512]{1,0:T(8,128)(2,1)S(1)}, u32[]{:S(2)}, u32[]{:S(2)}) collective-permute-start(bf16[256,512]{1,0:T(8,128)(2,1)S(1)} %get-tuple-element.16.state_ref), channel_id=1, source_target_pairs={{0,31},{1,2},{2,1},{3,4},{4,3},{5,6},{6,5},{7,8},{8,7},{9,10},{10,... | collective-permute-start | bytes 786440 | tf_op jit(solution)/shard_map/ppermute | solution.py:32
  36.5 0.3 collective-permute-start.4
  36.8 4.0 %collective-permute-done.3.state_ref.near_ref = bf16[256,512]{1,0:T(8,128)(2,1)S(1)} collective-permute-done((bf16[256,512]{1,0:T(8,128)(2,1)S(1)}, bf16[256,512]{1,0:T(8,128)(2,1)S(1)}, u32[]{:S(2)}, u32[]{:S(2)}) %collective-permute-start.3) | collective-permute-done | bytes 262176 | tf_op jit(solution)/shard_map/ppermute | solution.py:32
  40.8 0.1 collective-permute-start.5
  40.9 0.7 %slice.12.code_ref = bf16[16,512]{1,0:T(8,128)(2,1)S(1)} slice(bf16[272,512]{1,0:T(8,128)(2,1)} %collective-permute-done.1.arrived_ref), slice={[256:272], [0:512]} | slice | bytes 32768 | tf_op jit(solution)/shard_map/slice | solution.py:374
  41.6 0.0 copy-start.7
  41.7 0.6 %project.2.qkv_pair = bf16[256,1536]{1,0:T(8,128)(2,1)S(1)} custom-call(bf16[256,512]{1,0:T(8,128)(2,1)S(1)} %get-tuple-element.16.state_ref, f32[1,512]{1,0:T(1,128)S(1)} %copy-done.5, bf16[512,1536]{1,0:T(8,128)(2,1)S(1)} %bitcast.4), custom_call_target="tpu_custom_call" | custom-call | flops 402653184 | bytes 262144 | tf_op jit(solution)/shard_map/project/pallas_call | solution.py:211
  42.3 0.6 %project.3.qkv_near = bf16[256,1536]{1,0:T(8,128)(2,1)S(1)} custom-call(bf16[256,512]{1,0:T(8,128)(2,1)S(1)} %collective-permute-done.3.state_ref.near_ref, f32[1,512]{1,0:T(1,128)S(1)} %copy-done.5, bf16[512,1536]{1,0:T(8,128)(2,1)S(1)} %bitcast.5), custom_call_target="tpu_custom_call" | custom-call | flops 402653184 | bytes 262144 | tf_op jit(solution)/shard_map/project/pallas_call | solution.py:211
  42.9 2.1 %collective-permute-done.4.far_ref = bf16[256,512]{1,0:T(8,128)(2,1)S(1)} collective-permute-done((bf16[256,512]{1,0:T(8,128)(2,1)S(1)}, bf16[256,512]{1,0:T(8,128)(2,1)S(1)}, u32[]{:S(2)}, u32[]{:S(2)}) %collective-permute-start.4) | collective-permute-done | bytes 262176 | tf_op jit(solution)/shard_map/ppermute | solution.py:32
  45.1 0.0 copy-start.9
  45.1 0.0 copy-start.10
  45.1 6.0 %attend.1.ring_ref = bf16[384,512]{1,0:T(8,128)(2,1)S(1)} custom-call(s32[1,3]{1,0:T(1,128)S(1)} %copy-done.7, bf16[16,512]{1,0:T(8,128)(2,1)S(1)} %slice.12.code_ref, f32[128,512]{1,0:T(8,128)S(1)} %get-tuple-element.15.own_ref, bf16[256,1536]{1,0:T(8,128)(2,1)S(1)} %project.2.qkv_pair, bf16[256,512]{1,0:T(8,128)(2,1)S(1)} %collective-permute-done.3.state_ref.near_ref, ...), custom_call_target="tpu_custom_call" | custom-call | tf_op jit(solution)/shard_map/attend/pallas_call | solution.py:280
  51.1 0.1 collective-permute-start.6
  51.2 1.5 %collective-permute-done.6.back_ref = bf16[256,512]{1,0:T(8,128)(2,1)S(1)} collective-permute-done((bf16[256,512]{1,0:T(8,128)(2,1)S(1)}, bf16[256,512]{1,0:T(8,128)(2,1)S(1)}, u32[]{:S(2)}, u32[]{:S(2)}) %collective-permute-start.6) | collective-permute-done | bytes 262176 | tf_op jit(solution)/shard_map/ppermute | solution.py:23
  52.8 6.5 %decode.1 = (bf16[1024,512]{1,0:T(8,128)(2,1)}, bf16[128,512]{1,0:T(8,128)(2,1)}) custom-call(s32[8]{0:T(128)S(1)} %copy-done.12, f32[8,128]{1,0:T(8,128)S(1)} %bitcast.8, bf16[384,512]{1,0:T(8,128)(2,1)S(1)} %attend.1.ring_ref, bf16[256,512]{1,0:T(8,128)(2,1)S(1)} %collective-permute-done.6.back_ref, bf16[1024,512]{1,0:T(8,128)(2,1)S(1)} %get-tuple-element.17.enc_ref, ...), custom_call_target="tpu_custom_call" | custom-call | flops 4294967296 | bytes 6291456 | tf_op jit(solution)/shard_map/decode/pallas_call | solution.py:337
  (23 shorter events, 0.1 us)
Async XLA Ops:
  0.6 0.7 %copy-start.6 = (s32[1,3]{1,0:T(1,128)S(1)}, s32[1,3]{1,0:T(1,128)}, u32[]{:S(2)}) copy-start(s32[1,3]{1,0:T(1,128)} %listed.3) | copy-start | bytes 40
  1.3 0.7 %copy-start.11 = (s32[8]{0:T(128)S(1)}, s32[8]{0:T(128)}, u32[]{:S(2)}) copy-start(s32[8]{0:T(128)} %owner.2) | copy-start | bytes 100
  10.0 0.8 %copy-start.3 = (f32[256,512]{1,0:T(8,128)}, f32[256,512]{1,0:T(8,128)S(1)}, u32[]{:S(2)}) copy-start(f32[256,512]{1,0:T(8,128)S(1)} %get-tuple-element.12.loc_ref) | copy-start | bytes 1572868
  10.8 0.7 %copy-start.4 = (bf16[272,512]{1,0:T(8,128)(2,1)}, bf16[272,512]{1,0:T(8,128)(2,1)S(1)}, u32[]{:S(2)}) copy-start(bf16[272,512]{1,0:T(8,128)(2,1)S(1)} %get-tuple-element.10.base_ref) | copy-start | bytes 835588
  11.5 30.1 %copy-start = (bf16[1,512,1536]{2,1,0:T(8,128)(2,1)S(1)}, bf16[1,512,1536]{2,1,0:T(8,128)(2,1)}, u32[]{:S(2)}) copy-start(bf16[1,512,1536]{2,1,0:T(8,128)(2,1)} %param.24) | copy-start | bytes 4718596
  11.5 30.1 %copy-start.5 = (f32[1,512]{1,0:T(1,128)S(1)}, f32[1,512]{1,0:T(1,128)}, u32[]{:S(2)}) copy-start(f32[1,512]{1,0:T(1,128)} %gain_ref.5) | copy-start | bytes 6148
  11.6 1.5 %collective-permute-start = (bf16[144,512]{1,0:T(8,128)(2,1)S(1)}, bf16[144,512]{1,0:T(8,128)(2,1)S(1)}, u32[]{:S(2)}, u32[]{:S(2)}) collective-permute-start(bf16[144,512]{1,0:T(8,128)(2,1)S(1)} %get-tuple-element.11), channel_id=1, source_target_pairs={{0,1},{1,0},{2,3},{3,2},{4,5},{5,4},{6,7},{7,6},{8,9},{9,8},{10,11... | collective-permute-start | bytes 442376 | tf_op jit(solution)/shard_map/ppermute | solution.py:23
  13.0 0.7 %copy-start.14 = (bf16[144,512]{1,0:T(8,128)(2,1)}, bf16[144,512]{1,0:T(8,128)(2,1)S(1)}, u32[]{:S(2)}) copy-start(bf16[144,512]{1,0:T(8,128)(2,1)S(1)} %collective-permute-done.arrived_ref) | copy-start | bytes 442372
  14.7 11.1 %collective-permute-start.1 = (bf16[272,512]{1,0:T(8,128)(2,1)S(1)}, bf16[272,512]{1,0:T(8,128)(2,1)}, u32[]{:S(2)}, u32[]{:S(2)}) collective-permute-start(bf16[272,512]{1,0:T(8,128)(2,1)S(1)} %outgoing_sums.1), channel_id=1, source_target_pairs={{0,31},{1,2},{2,1},{3,4},{4,3},{5,6},{6,5},{7,8},{8,7},{9,10},{10,... | collective-permute-start | bytes 835592 | tf_op jit(solution)/shard_map/ppermute | solution.py:32
  27.0 0.8 %copy-start.2 = (f32[256,512]{1,0:T(8,128)}, f32[256,512]{1,0:T(8,128)S(1)}, u32[]{:S(2)}) copy-start(f32[256,512]{1,0:T(8,128)S(1)} %get-tuple-element.13.share_ref) | copy-start | bytes 1572868
  27.8 1.5 %collective-permute-start.2 = (bf16[256,512]{1,0:T(8,128)(2,1)S(1)}, bf16[256,512]{1,0:T(8,128)(2,1)S(1)}, u32[]{:S(2)}, u32[]{:S(2)}) collective-permute-start(bf16[256,512]{1,0:T(8,128)(2,1)S(1)} %get-tuple-element.14), channel_id=1, source_target_pairs={{0,1},{1,0},{2,3},{3,2},{4,5},{5,4},{6,7},{7,6},{8,9},{9,8},{10,11... | collective-permute-start | bytes 786440 | tf_op jit(solution)/shard_map/ppermute | solution.py:23
  29.4 0.7 %copy-start.13 = (bf16[256,512]{1,0:T(8,128)(2,1)}, bf16[256,512]{1,0:T(8,128)(2,1)S(1)}, u32[]{:S(2)}) copy-start(bf16[256,512]{1,0:T(8,128)(2,1)S(1)} %collective-permute-done.2.other_ref) | copy-start | bytes 786436
  31.2 9.6 %collective-permute-start.3 = (bf16[256,512]{1,0:T(8,128)(2,1)S(1)}, bf16[256,512]{1,0:T(8,128)(2,1)S(1)}, u32[]{:S(2)}, u32[]{:S(2)}) collective-permute-start(bf16[256,512]{1,0:T(8,128)(2,1)S(1)} %get-tuple-element.16.state_ref), channel_id=1, source_target_pairs={{0,31},{1,2},{2,1},{3,4},{4,3},{5,6},{6,5},{7,8},{8,7},{9,10},{10,... | collective-permute-start | bytes 786440 | tf_op jit(solution)/shard_map/ppermute | solution.py:32
  36.5 8.5 %collective-permute-start.4 = (bf16[256,512]{1,0:T(8,128)(2,1)S(1)}, bf16[256,512]{1,0:T(8,128)(2,1)S(1)}, u32[]{:S(2)}, u32[]{:S(2)}) collective-permute-start(bf16[256,512]{1,0:T(8,128)(2,1)S(1)} %get-tuple-element.16.state_ref), channel_id=1, source_target_pairs={{0,29},{1,4},{2,31},{3,6},{4,1},{5,8},{6,3},{7,10},{8,5},{9,12},{1... | collective-permute-start | bytes 786440 | tf_op jit(solution)/shard_map/ppermute | solution.py:32
  40.8 4.2 %collective-permute-start.5 = (bf16[128,512]{1,0:T(8,128)(2,1)S(1)}, bf16[128,512]{1,0:T(8,128)(2,1)S(1)}, u32[]{:S(2)}, u32[]{:S(2)}) collective-permute-start(bf16[128,512]{1,0:T(8,128)(2,1)S(1)} %slice.13), channel_id=1, source_target_pairs={{0,1},{1,0},{2,3},{3,2},{4,5},{5,4},{6,7},{7,6},{8,9},{9,8},{10,11... | collective-permute-start | bytes 393224 | tf_op jit(solution)/shard_map/ppermute | solution.py:23
  41.6 3.4 %copy-start.1 = (bf16[1,512,512]{2,1,0:T(8,128)(2,1)S(1)}, bf16[1,512,512]{2,1,0:T(8,128)(2,1)}, u32[]{:S(2)}) copy-start(bf16[1,512,512]{2,1,0:T(8,128)(2,1)} %param.25) | copy-start | bytes 1572868
  41.6 3.4 %copy-start.7 = (s32[1,3]{1,0:T(1,128)S(1)}, s32[1,3]{1,0:T(1,128)}, u32[]{:S(2)}) copy-start(s32[1,3]{1,0:T(1,128)} %listed.3) | copy-start | bytes 40
  45.0 7.7 %copy-start.8 = (bf16[512,2048]{1,0:T(8,128)(2,1)S(1)}, bf16[512,2048]{1,0:T(8,128)(2,1)}, u32[]{:S(2)}) copy-start(bf16[512,2048]{1,0:T(8,128)(2,1)} %first.1) | copy-start | bytes 6291460
  45.1 7.7 %copy-start.9 = (bf16[2048,512]{1,0:T(8,128)(2,1)S(1)}, bf16[2048,512]{1,0:T(8,128)(2,1)}, u32[]{:S(2)}) copy-start(bf16[2048,512]{1,0:T(8,128)(2,1)} %second.1) | copy-start | bytes 6291460
  45.1 7.7 %copy-start.10 = (f32[1024]{0:T(1024)S(1)}, f32[1024]{0:T(1024)}, u32[]{:S(2)}) copy-start(f32[1024]{0:T(1024)} %param.18) | copy-start | bytes 12292
  45.1 7.7 %copy-start.12 = (s32[8]{0:T(128)S(1)}, s32[8]{0:T(128)}, u32[]{:S(2)}) copy-start(s32[8]{0:T(128)} %owner.3) | copy-start | bytes 100
  51.1 1.6 %collective-permute-start.6 = (bf16[256,512]{1,0:T(8,128)(2,1)S(1)}, bf16[256,512]{1,0:T(8,128)(2,1)S(1)}, u32[]{:S(2)}, u32[]{:S(2)}) collective-permute-start(bf16[256,512]{1,0:T(8,128)(2,1)S(1)} %slice.14), channel_id=1, source_target_pairs={{0,1},{1,0},{2,3},{3,2},{4,5},{5,4},{6,7},{7,6},{8,9},{9,8},{10,11... | collective-permute-start | bytes 786440 | tf_op jit(solution)/shard_map/ppermute | solution.py:23

commit v3 on v2

--- a/solution.py
+++ b/solution.py
@@ -156,7 +156,8 @@
 
 def outgoing_sums(base, arrived):
     return pl.pallas_call(
-        outgoing_kernel, out_shape=kept(base.shape), in_specs=[VMEM] * 2, out_specs=VMEM, name="outgoing_sums"
+        outgoing_kernel, out_shape=kept(base.shape), in_specs=[VMEM] * 2, out_specs=VMEM,
+        compiler_params=pltpu.CompilerParams(vmem_limit_bytes=4 << 20), name="outgoing_sums"
     )(base, arrived)
 
 
@@ -173,6 +174,7 @@
         out_shape=(kept(local.shape, F32), kept(local.shape)),
         in_specs=[VMEM] * 2,
         out_specs=(VMEM,) * 2,
+        compiler_params=pltpu.CompilerParams(vmem_limit_bytes=4 << 20),
         name="chip_share",
     )(local, arrived)
 
@@ -191,6 +193,7 @@
         out_shape=(kept((rows, depth), F32), kept(share.shape)),
         in_specs=[VMEM] * 2,
         out_specs=(VMEM,) * 2,
+        compiler_params=pltpu.CompilerParams(vmem_limit_bytes=4 << 20),
         name="chip_states",
     )(share, other)
 

time: 59.6 us -> 52.7 us (0.88)
  local copies, waits for them, and re-layouts: 5.74 us -> 1.38 us
  Pallas kernels: 25.2 us -> 22 us
  waiting for transfers between devices: 14.6 us -> 15.2 us
    unnamed x30 -> x18, local copies, waits for them, and re-layouts: 4.99 us -> 1.34 us
    pallas_call x1, Pallas kernels: 1.21 us -> 0.1 us  [chip_share(): pl.pallas_call(share_kernel, out_shape=(kept(local.shape, F32), kept(loca...]
    pallas_call x1, Pallas kernels: 1.19 us -> 0.08 us  [chip_states(): pl.pallas_call(state_kernel, out_shape=(kept((rows, depth), F32), kept(sh...]
    pallas_call x1, Pallas kernels: 1.04 us -> 0.04 us  [outgoing_sums(): pl.pallas_call(outgoing_kernel, out_shape=kept(base.shape), in_specs=[VME...]
    slice x1, local copies, waits for them, and re-layouts: 0.72 us -> 0.01 us  [on_device(): sums[2 * rows:]]
  transfers between devices with their start and end apart: 7 -> 7, of which waited for: 6 -> 6; matrix products, arithmetic and copies ran while one was open for 1% -> 0% of each run, Pallas kernels for 2% -> 2%
where the time goes in v3:
time: 52.7 us; the launch traced here: 52.5 us
  Pallas kernels  22 us (42%)
  waiting for transfers between devices  15.2 us (29%)
  starting transfers between devices  13 us (25%)
  local copies, waits for them, and re-layouts  1.38 us (3%)
  between operations  0.97 us (2%)
    ppermute x3, starting transfers between devices, from_outward(): return lax.ppermute(block, AXES, route)  12.3 us
    ppermute x3, waiting for transfers between devices, from_outward(): return lax.ppermute(block, AXES, route)  11.1 us
    pallas_call x1, Pallas kernels, encode(): pl.pallas_call(encode_kernel, out_shape=(kept((cells, depth)), kept((rows...  8.1 us
    pallas_call x1, Pallas kernels, decode(): pl.pallas_call(decode_kernel, out_shape=(jax.ShapeDtypeStruct((cells, dep...  6.45 us
    pallas_call x1, Pallas kernels, attend(): pl.pallas_call(attend_kernel, out_shape=kept((3 * rows, depth)), in_specs...  6 us
    ppermute x4, waiting for transfers between devices, swapped(): return lax.ppermute(block, AXES, [(i, i ^ 1) for i in range(count)])  4.05 us
    unnamed x18, local copies, waits for them, and re-layouts  1.34 us
    pallas_call x2, Pallas kernels, project(): pl.pallas_call(project_kernel, out_shape=kept((rows, w_qkv.shape[1])), in...  1.26 us
  transfers between devices with their start and end apart: 7, of which 6 were waited for; matrix products, arithmetic and copies ran while one was open for 0% of the time, Pallas kernels for 2%

profile of v3, /device:TPU:0, one launch (start us, length us, event | category | flops | bytes accessed | tf_op | source)
XLA Modules:
  0.0 52.5 jit_solution(13513400098540074768)
XLA Ops:
  0.6 0.0 copy-start.3
  0.6 0.6 %copy-done.3 = s32[1,3]{1,0:T(1,128)S(1)} copy-done((s32[1,3]{1,0:T(1,128)S(1)}, s32[1,3]{1,0:T(1,128)}, u32[]{:S(2)}) %copy-start.3) | copy-done | bytes 36
  1.3 0.7 %copy-done.7 = s32[8]{0:T(128)S(1)} copy-done((s32[8]{0:T(128)S(1)}, s32[8]{0:T(128)}, u32[]{:S(2)}) %copy-start.7) | copy-done | bytes 56
  1.9 8.1 %encode.1 = (bf16[1024,512]{1,0:T(8,128)(2,1)S(1)}, bf16[144,512]{1,0:T(8,128)(2,1)S(1)}, bf16[272,512]{1,0:T(8,128)(2,1)S(1)}, f32[256,512]{1,0:T(8,128)S(1)}) custom-call(s32[8]{0:T(128)S(1)} %copy-done.7, s32[1,3]{1,0:T(1,128)S(1)} %copy-done.3, f32[8,128]{1,0:T(8,128)} %bitcast.9, bf16[128,512]{1,0:T(8,128)(2,1)} %feat_hbm.1, bf16[1024,512]{1,0:T(8,128)(2,1)} %x_hbm.1, ...), custom_call_target="tpu_custom_call" | custom-call | flops 4294967296 | bytes 6291456 | tf_op jit(solution)/shard_map/encode/pallas_call | solution.py:123
  10.1 0.0 copy-start
  10.1 0.0 copy-start.2
  10.1 0.5 %collective-permute-start = (bf16[144,512]{1,0:T(8,128)(2,1)S(1)}, bf16[144,512]{1,0:T(8,128)(2,1)S(1)}, u32[]{:S(2)}, u32[]{:S(2)}) collective-permute-start(bf16[144,512]{1,0:T(8,128)(2,1)S(1)} %get-tuple-element.11), channel_id=1, source_target_pairs={{0,1},{1,0},{2,3},{3,2},{4,5},{5,4},{6,7},{7,6},{8,9},{9,8},{10,11... | collective-permute-start | bytes 442376 | tf_op jit(solution)/shard_map/ppermute | solution.py:23
  10.6 1.0 %collective-permute-done.arrived_ref = bf16[144,512]{1,0:T(8,128)(2,1)S(1)} collective-permute-done((bf16[144,512]{1,0:T(8,128)(2,1)S(1)}, bf16[144,512]{1,0:T(8,128)(2,1)S(1)}, u32[]{:S(2)}, u32[]{:S(2)}) %collective-permute-start) | collective-permute-done | bytes 147488 | tf_op jit(solution)/shard_map/ppermute | solution.py:23
  11.7 6.7 %collective-permute-start.1 = (bf16[272,512]{1,0:T(8,128)(2,1)S(1)}, bf16[272,512]{1,0:T(8,128)(2,1)S(1)}, u32[]{:S(2)}, u32[]{:S(2)}) collective-permute-start(bf16[272,512]{1,0:T(8,128)(2,1)S(1)} %outgoing_sums.1), channel_id=1, source_target_pairs={{0,31},{1,2},{2,1},{3,4},{4,3},{5,6},{6,5},{7,8},{8,7},{9,10},{10,... | collective-permute-start | bytes 835592 | tf_op jit(solution)/shard_map/ppermute | solution.py:32
  18.3 4.3 %collective-permute-done.1.arrived_ref = bf16[272,512]{1,0:T(8,128)(2,1)S(1)} collective-permute-done((bf16[272,512]{1,0:T(8,128)(2,1)S(1)}, bf16[272,512]{1,0:T(8,128)(2,1)S(1)}, u32[]{:S(2)}, u32[]{:S(2)}) %collective-permute-start.1) | collective-permute-done | bytes 278560 | tf_op jit(solution)/shard_map/ppermute | solution.py:32
  22.7 0.1 chip_share.1
  22.8 0.1 collective-permute-start.2
  22.8 1.5 %collective-permute-done.2.other_ref = bf16[256,512]{1,0:T(8,128)(2,1)S(1)} collective-permute-done((bf16[256,512]{1,0:T(8,128)(2,1)S(1)}, bf16[256,512]{1,0:T(8,128)(2,1)S(1)}, u32[]{:S(2)}, u32[]{:S(2)}) %collective-permute-start.2) | collective-permute-done | bytes 262176 | tf_op jit(solution)/shard_map/ppermute | solution.py:23
  24.4 0.1 chip_states.1
  24.4 5.3 %collective-permute-start.3 = (bf16[256,512]{1,0:T(8,128)(2,1)S(1)}, bf16[256,512]{1,0:T(8,128)(2,1)S(1)}, u32[]{:S(2)}, u32[]{:S(2)}) collective-permute-start(bf16[256,512]{1,0:T(8,128)(2,1)S(1)} %get-tuple-element.16.state_ref), channel_id=1, source_target_pairs={{0,31},{1,2},{2,1},{3,4},{4,3},{5,6},{6,5},{7,8},{8,7},{9,10},{10,... | collective-permute-start | bytes 786440 | tf_op jit(solution)/shard_map/ppermute | solution.py:32
  29.7 0.3 collective-permute-start.4
  30.0 4.0 %collective-permute-done.3.state_ref.near_ref = bf16[256,512]{1,0:T(8,128)(2,1)S(1)} collective-permute-done((bf16[256,512]{1,0:T(8,128)(2,1)S(1)}, bf16[256,512]{1,0:T(8,128)(2,1)S(1)}, u32[]{:S(2)}, u32[]{:S(2)}) %collective-permute-start.3) | collective-permute-done | bytes 262176 | tf_op jit(solution)/shard_map/ppermute | solution.py:32
  34.0 0.1 collective-permute-start.5
  34.1 0.0 copy-done
  34.1 0.0 copy-done.2
  34.1 0.0 copy-start.1
  34.1 0.6 %project.2.qkv_pair = bf16[256,1536]{1,0:T(8,128)(2,1)S(1)} custom-call(bf16[256,512]{1,0:T(8,128)(2,1)S(1)} %get-tuple-element.16.state_ref, f32[1,512]{1,0:T(1,128)S(1)} %copy-done.2, bf16[512,1536]{1,0:T(8,128)(2,1)S(1)} %bitcast.4), custom_call_target="tpu_custom_call" | custom-call | flops 402653184 | bytes 262144 | tf_op jit(solution)/shard_map/project/pallas_call | solution.py:214
  34.8 0.6 %project.3.qkv_near = bf16[256,1536]{1,0:T(8,128)(2,1)S(1)} custom-call(bf16[256,512]{1,0:T(8,128)(2,1)S(1)} %collective-permute-done.3.state_ref.near_ref, f32[1,512]{1,0:T(1,128)S(1)} %copy-done.2, bf16[512,1536]{1,0:T(8,128)(2,1)S(1)} %bitcast.5), custom_call_target="tpu_custom_call" | custom-call | flops 402653184 | bytes 262144 | tf_op jit(solution)/shard_map/project/pallas_call | solution.py:214
  35.4 2.8 %collective-permute-done.4.far_ref = bf16[256,512]{1,0:T(8,128)(2,1)S(1)} collective-permute-done((bf16[256,512]{1,0:T(8,128)(2,1)S(1)}, bf16[256,512]{1,0:T(8,128)(2,1)S(1)}, u32[]{:S(2)}, u32[]{:S(2)}) %collective-permute-start.4) | collective-permute-done | bytes 262176 | tf_op jit(solution)/shard_map/ppermute | solution.py:32
  38.2 0.0 collective-permute-done.5.behind_ref
  38.2 0.0 copy-start.5
  38.3 0.0 copy-start.6
  38.3 0.0 copy-start.8
  38.3 6.0 %attend.1.ring_ref = bf16[384,512]{1,0:T(8,128)(2,1)S(1)} custom-call(s32[1,3]{1,0:T(1,128)S(1)} %copy-done.3, bf16[16,512]{1,0:T(8,128)(2,1)S(1)} %slice.12.code_ref, f32[128,512]{1,0:T(8,128)S(1)} %get-tuple-element.15.own_ref, bf16[256,1536]{1,0:T(8,128)(2,1)S(1)} %project.2.qkv_pair, bf16[256,512]{1,0:T(8,128)(2,1)S(1)} %collective-permute-done.3.state_ref.near_ref, ...), custom_call_target="tpu_custom_call" | custom-call | tf_op jit(solution)/shard_map/attend/pallas_call | solution.py:283
  44.3 0.1 collective-permute-start.6
  44.4 1.5 %collective-permute-done.6.back_ref = bf16[256,512]{1,0:T(8,128)(2,1)S(1)} collective-permute-done((bf16[256,512]{1,0:T(8,128)(2,1)S(1)}, bf16[256,512]{1,0:T(8,128)(2,1)S(1)}, u32[]{:S(2)}, u32[]{:S(2)}) %collective-permute-start.6) | collective-permute-done | bytes 262176 | tf_op jit(solution)/shard_map/ppermute | solution.py:23
  45.9 6.4 %decode.1 = (bf16[1024,512]{1,0:T(8,128)(2,1)}, bf16[128,512]{1,0:T(8,128)(2,1)}) custom-call(s32[8]{0:T(128)S(1)} %copy-done.8, f32[8,128]{1,0:T(8,128)S(1)} %bitcast.8, bf16[384,512]{1,0:T(8,128)(2,1)S(1)} %attend.1.ring_ref, bf16[256,512]{1,0:T(8,128)(2,1)S(1)} %collective-permute-done.6.back_ref, bf16[1024,512]{1,0:T(8,128)(2,1)S(1)} %get-tuple-element.17.enc_ref, ...), custom_call_target="tpu_custom_call" | custom-call | flops 4294967296 | bytes 6291456 | tf_op jit(solution)/shard_map/decode/pallas_call | solution.py:340
  (11 shorter events, 0.1 us)
Async XLA Ops:
  0.6 0.7 %copy-start.3 = (s32[1,3]{1,0:T(1,128)S(1)}, s32[1,3]{1,0:T(1,128)}, u32[]{:S(2)}) copy-start(s32[1,3]{1,0:T(1,128)} %listed.3) | copy-start | bytes 40
  1.3 0.7 %copy-start.7 = (s32[8]{0:T(128)S(1)}, s32[8]{0:T(128)}, u32[]{:S(2)}) copy-start(s32[8]{0:T(128)} %owner.2) | copy-start | bytes 100
  10.1 24.1 %copy-start = (bf16[1,512,1536]{2,1,0:T(8,128)(2,1)S(1)}, bf16[1,512,1536]{2,1,0:T(8,128)(2,1)}, u32[]{:S(2)}) copy-start(bf16[1,512,1536]{2,1,0:T(8,128)(2,1)} %param.24) | copy-start | bytes 4718596
  10.1 24.1 %copy-start.2 = (f32[1,512]{1,0:T(1,128)S(1)}, f32[1,512]{1,0:T(1,128)}, u32[]{:S(2)}) copy-start(f32[1,512]{1,0:T(1,128)} %gain_ref.5) | copy-start | bytes 6148
  10.1 1.5 %collective-permute-start = (bf16[144,512]{1,0:T(8,128)(2,1)S(1)}, bf16[144,512]{1,0:T(8,128)(2,1)S(1)}, u32[]{:S(2)}, u32[]{:S(2)}) collective-permute-start(bf16[144,512]{1,0:T(8,128)(2,1)S(1)} %get-tuple-element.11), channel_id=1, source_target_pairs={{0,1},{1,0},{2,3},{3,2},{4,5},{5,4},{6,7},{7,6},{8,9},{9,8},{10,11... | collective-permute-start | bytes 442376 | tf_op jit(solution)/shard_map/ppermute | solution.py:23
  11.7 11.0 %collective-permute-start.1 = (bf16[272,512]{1,0:T(8,128)(2,1)S(1)}, bf16[272,512]{1,0:T(8,128)(2,1)S(1)}, u32[]{:S(2)}, u32[]{:S(2)}) collective-permute-start(bf16[272,512]{1,0:T(8,128)(2,1)S(1)} %outgoing_sums.1), channel_id=1, source_target_pairs={{0,31},{1,2},{2,1},{3,4},{4,3},{5,6},{6,5},{7,8},{8,7},{9,10},{10,... | collective-permute-start | bytes 835592 | tf_op jit(solution)/shard_map/ppermute | solution.py:32
  22.8 1.6 %collective-permute-start.2 = (bf16[256,512]{1,0:T(8,128)(2,1)S(1)}, bf16[256,512]{1,0:T(8,128)(2,1)S(1)}, u32[]{:S(2)}, u32[]{:S(2)}) collective-permute-start(bf16[256,512]{1,0:T(8,128)(2,1)S(1)} %get-tuple-element.14), channel_id=1, source_target_pairs={{0,1},{1,0},{2,3},{3,2},{4,5},{5,4},{6,7},{7,6},{8,9},{9,8},{10,11... | collective-permute-start | bytes 786440 | tf_op jit(solution)/shard_map/ppermute | solution.py:23
  24.4 9.6 %collective-permute-start.3 = (bf16[256,512]{1,0:T(8,128)(2,1)S(1)}, bf16[256,512]{1,0:T(8,128)(2,1)S(1)}, u32[]{:S(2)}, u32[]{:S(2)}) collective-permute-start(bf16[256,512]{1,0:T(8,128)(2,1)S(1)} %get-tuple-element.16.state_ref), channel_id=1, source_target_pairs={{0,31},{1,2},{2,1},{3,4},{4,3},{5,6},{6,5},{7,8},{8,7},{9,10},{10,... | collective-permute-start | bytes 786440 | tf_op jit(solution)/shard_map/ppermute | solution.py:32
  29.7 8.5 %collective-permute-start.4 = (bf16[256,512]{1,0:T(8,128)(2,1)S(1)}, bf16[256,512]{1,0:T(8,128)(2,1)S(1)}, u32[]{:S(2)}, u32[]{:S(2)}) collective-permute-start(bf16[256,512]{1,0:T(8,128)(2,1)S(1)} %get-tuple-element.16.state_ref), channel_id=1, source_target_pairs={{0,29},{1,4},{2,31},{3,6},{4,1},{5,8},{6,3},{7,10},{8,5},{9,12},{1... | collective-permute-start | bytes 786440 | tf_op jit(solution)/shard_map/ppermute | solution.py:32
  34.0 4.2 %collective-permute-start.5 = (bf16[128,512]{1,0:T(8,128)(2,1)S(1)}, bf16[128,512]{1,0:T(8,128)(2,1)S(1)}, u32[]{:S(2)}, u32[]{:S(2)}) collective-permute-start(bf16[128,512]{1,0:T(8,128)(2,1)S(1)} %slice.13), channel_id=1, source_target_pairs={{0,1},{1,0},{2,3},{3,2},{4,5},{5,4},{6,7},{7,6},{8,9},{9,8},{10,11... | collective-permute-start | bytes 393224 | tf_op jit(solution)/shard_map/ppermute | solution.py:23
  34.1 4.1 %copy-start.1 = (bf16[1,512,512]{2,1,0:T(8,128)(2,1)S(1)}, bf16[1,512,512]{2,1,0:T(8,128)(2,1)}, u32[]{:S(2)}) copy-start(bf16[1,512,512]{2,1,0:T(8,128)(2,1)} %param.25) | copy-start | bytes 1572868
  38.2 7.7 %copy-start.4 = (bf16[512,2048]{1,0:T(8,128)(2,1)S(1)}, bf16[512,2048]{1,0:T(8,128)(2,1)}, u32[]{:S(2)}) copy-start(bf16[512,2048]{1,0:T(8,128)(2,1)} %first.1) | copy-start | bytes 6291460
  38.2 7.7 %copy-start.5 = (bf16[2048,512]{1,0:T(8,128)(2,1)S(1)}, bf16[2048,512]{1,0:T(8,128)(2,1)}, u32[]{:S(2)}) copy-start(bf16[2048,512]{1,0:T(8,128)(2,1)} %second.1) | copy-start | bytes 6291460
  38.3 7.7 %copy-start.6 = (f32[1024]{0:T(1024)S(1)}, f32[1024]{0:T(1024)}, u32[]{:S(2)}) copy-start(f32[1024]{0:T(1024)} %param.18) | copy-start | bytes 12292
  38.3 7.7 %copy-start.8 = (s32[8]{0:T(128)S(1)}, s32[8]{0:T(128)}, u32[]{:S(2)}) copy-start(s32[8]{0:T(128)} %owner.3) | copy-start | bytes 100
  44.3 1.6 %collective-permute-start.6 = (bf16[256,512]{1,0:T(8,128)(2,1)S(1)}, bf16[256,512]{1,0:T(8,128)(2,1)S(1)}, u32[]{:S(2)}, u32[]{:S(2)}) collective-permute-start(bf16[256,512]{1,0:T(8,128)(2,1)S(1)} %slice.14), channel_id=1, source_target_pairs={{0,1},{1,0},{2,3},{3,2},{4,5},{5,4},{6,7},{7,6},{8,9},{9,8},{10,11... | collective-permute-start | bytes 786440 | tf_op jit(solution)/shard_map/ppermute | solution.py:23

commit v4 on v3

v4 whole, which is shorter than its diff:
```python
import functools

import jax
import jax.numpy as jnp
from jax import lax
from jax.experimental import pallas as pl
from jax.experimental.pallas import tpu as pltpu
from jax.sharding import PartitionSpec as P

HD = 128
REACH = 2
EXTRA = 16
AXES = ("tile", "sub")
BF16 = jnp.bfloat16
F32 = jnp.float32
VMEM = pl.BlockSpec(memory_space=pltpu.VMEM)
SMEM = pl.BlockSpec(memory_space=pltpu.SMEM)
ANY = pl.BlockSpec(memory_space=pl.ANY)


def swapped(block):
    count = lax.axis_size(AXES)
    return lax.ppermute(block, AXES, [(i, i ^ 1) for i in range(count)])


def from_outward(block, chips):
    count = lax.axis_size(AXES)
    route = []
    for i in range(count):
        step = 2 * chips - 1
        route.append((i, (i + step if i % 2 else i - step) % count))
    return lax.ppermute(block, AXES, route)


def tiles_of(rows, columns):
    return min(rows, 512), min(columns, 1024)


def outward_of():
    return 2 * lax.axis_index("sub") - 1


def offset_of(owner, mine, count):
    return lax.rem(owner - mine + REACH + count, count) - REACH


def kept(shape, dtype=BF16):
    return pltpu.VMEM(shape, dtype)


def in_hbm(*arrays):
    return [pltpu.with_memory_space_constraint(a, pltpu.HBM) for a in arrays]


def hidden_layer(x_ref, first, act, tile, part, arrive, before):
    for j in range(first.shape[1] // part):
        before(j)
        cols = slice(j * part, (j + 1) * part)
        for r in range(x_ref.shape[0] // tile):
            if j == 0:
                arrive(r)
            cut = slice(r * tile, (r + 1) * tile)
            half = jnp.dot(x_ref[cut, :] * BF16(0.5), first[:, cols], preferred_element_type=F32)
            act[cut, cols] = (half * jnp.tanh(half) + half).astype(BF16)


def encode_kernel(
    owner_hbm, listed_hbm, weight_hbm, feat_hbm, x_hbm, first_hbm, second_hbm,
    enc_ref, msg_ref, base_ref, loc_ref,
    owner, listed, weight_ref, feat_ref, first, second, act, total, sems, io_sems,
):
    rows, depth = feat_ref.shape
    tile, part = tiles_of(enc_ref.shape[0], first.shape[1])
    tiles, parts = enc_ref.shape[0] // tile, first.shape[1] // part
    loads = [
        pltpu.make_async_copy(x_hbm.at[pl.ds(r * tile, tile)], enc_ref.at[pl.ds(r * tile, tile)], io_sems.at[r])
        for r in range(tiles)
    ]
    ones, twos = [], []
    for j in range(parts):
        cut = pl.ds(j * part, part)
        ones.append(pltpu.make_async_copy(first_hbm.at[:, cut], first.at[:, cut], sems.at[0, j]))
        twos.append(pltpu.make_async_copy(second_hbm.at[cut], second.at[cut], sems.at[1, j]))
    small = [
        pltpu.make_async_copy(weight_hbm, weight_ref, io_sems.at[tiles]),
        pltpu.make_async_copy(feat_hbm, feat_ref, io_sems.at[tiles + 1]),
        pltpu.make_async_copy(owner_hbm, owner, io_sems.at[tiles + 2]),
        pltpu.make_async_copy(listed_hbm, listed, io_sems.at[tiles + 3]),
    ]
    for copy in loads + ones:
        copy.start()

    def arrive(r):
        if r == 0:
            for copy in loads:
                copy.wait()
            for copy in twos + small:
                copy.start()

    mine, count = lax.axis_index(AXES), lax.axis_size(AXES)
    outward = outward_of()
    total[...] = jnp.zeros_like(total)
    hidden_layer(enc_ref, first, act, tile, part, arrive, lambda j: ones[j].wait())
    for copy in twos + small:
        copy.wait()
    columns = jnp.transpose(weight_ref[...])
    for r in range(tiles):
        cut = slice(r * tile, (r + 1) * tile)
        out = jnp.dot(act[cut, :], second[...], preferred_element_type=F32)
        enc_ref[cut, :] = (enc_ref[cut, :].astype(F32) + out).astype(BF16)
        for b in range(r * tile // rows, (r + 1) * tile // rows):
            slot = outward * offset_of(owner[b], mine, count) + REACH
            block = enc_ref[b * rows:(b + 1) * rows, :].astype(F32)
            total[slot] += columns[:, b:b + 1] * block
    absent = sum(-offset_of(listed[0, n], mine, count) for n in range(listed.shape[1])).astype(F32)
    spot = lax.broadcasted_iota(jnp.int32, (EXTRA, depth), 1)
    msg_ref[:rows, :] = total[0].astype(BF16)
    msg_ref[rows:, :] = jnp.where(spot == 1, absent, 0.0).astype(BF16)
    base_ref[:rows, :] = total[4].astype(BF16)
    base_ref[rows:2 * rows, :] = total[3].astype(BF16)
    base_ref[2 * rows:, :] = jnp.where(spot == 0, absent, 0.0).astype(BF16)
    loc_ref[:rows, :] = total[1]
    loc_ref[rows:, :] = total[2] + feat_ref[...].astype(F32)


def encode(owner, listed, weights, feat, grid, first, second):
    cells, depth = grid.shape
    hidden = first.shape[1]
    rows = feat.shape[0]
    tile, part = tiles_of(cells, hidden)
    return pl.pallas_call(
        encode_kernel,
        out_shape=(
            kept((cells, depth)),
            kept((rows + EXTRA, depth)),
            kept((2 * rows + EXTRA, depth)),
            kept((2 * rows, depth), F32),
        ),
        in_specs=[ANY] * 7,
        out_specs=(VMEM,) * 4,
        scratch_shapes=[
            pltpu.SMEM(owner.shape, jnp.int32),
            pltpu.SMEM(listed.shape, jnp.int32),
            pltpu.VMEM(weights.shape, F32),
            pltpu.VMEM(feat.shape, BF16),
            pltpu.VMEM((depth, hidden), BF16),
            pltpu.VMEM((hidden, depth), BF16),
            pltpu.VMEM((cells, hidden), BF16),
            pltpu.VMEM((2 * REACH + 1, rows, depth), F32),
            pltpu.SemaphoreType.DMA((2, hidden // part)),
            pltpu.SemaphoreType.DMA((cells // tile + 4,)),
        ],
        compiler_params=pltpu.CompilerParams(vmem_limit_bytes=24 << 20),
        cost_estimate=pl.CostEstimate(
            flops=4 * cells * depth * hidden, bytes_accessed=4 * (cells + hidden) * depth, transcendentals=cells * hidden
        ),
        name="encode",
    )(*in_hbm(owner, listed, weights, feat, grid, first, second))


def outgoing_kernel(base_ref, arrived_ref, out_ref):
    rows = arrived_ref.shape[0] - EXTRA
    out_ref[:rows, :] = base_ref[:rows, :]
    out_ref[rows:, :] = (base_ref[rows:, :].astype(F32) + arrived_ref[...].astype(F32)).astype(BF16)


def outgoing_sums(base, arrived):
    return pl.pallas_call(
        outgoing_kernel, out_shape=kept(base.shape), in_specs=[VMEM] * 2, out_specs=VMEM,
        compiler_params=pltpu.CompilerParams(vmem_limit_bytes=4 << 20), name="outgoing_sums"
    )(base, arrived)


def share_kernel(loc_ref, arrived_ref, after, share_ref, msg_ref):
    del after
    rows = loc_ref.shape[0] // 2
    share_ref[...] = loc_ref[...] + arrived_ref[:2 * rows, :].astype(F32)
    msg_ref[:rows, :] = share_ref[rows:, :].astype(BF16)
    msg_ref[rows:, :] = share_ref[:rows, :].astype(BF16)


def chip_share(local, arrived, after):
    return pl.pallas_call(
        share_kernel,
        out_shape=(kept(local.shape, F32), kept(local.shape)),
        in_specs=[VMEM] * 2 + [ANY],
        out_specs=(VMEM,) * 2,
        compiler_params=pltpu.CompilerParams(vmem_limit_bytes=4 << 20),
        name="chip_share",
    )(local, arrived, after)


def state_kernel(share_ref, other_ref, own_ref, pair_ref, msg_ref):
    rows = own_ref.shape[0]
    own_ref[...] = share_ref[rows:, :] + other_ref[rows:, :].astype(F32)
    pair_ref[:rows, :] = (share_ref[:rows, :] + other_ref[:rows, :].astype(F32)).astype(BF16)
    pair_ref[rows:, :] = own_ref[...].astype(BF16)
    msg_ref[:rows, :] = pair_ref[rows:, :]
    msg_ref[rows:, :] = pair_ref[:rows, :]


def chip_states(share, other):
    rows, depth = share.shape[0] // 2, share.shape[1]
    return pl.pallas_call(
        state_kernel,
        out_shape=(kept((rows, depth), F32), kept(share.shape), kept(share.shape)),
        in_specs=[VMEM] * 2,
        out_specs=(VMEM,) * 3,
        compiler_params=pltpu.CompilerParams(vmem_limit_bytes=4 << 20),
        name="chip_states",
    )(share, other)


def normal(block, gain):
    state = block.astype(F32)
    scale = lax.rsqrt(jnp.mean(state * state, axis=-1, keepdims=True) + 1e-6)
    return (state * scale * gain).astype(BF16)


def project_kernel(pair_ref, near_ref, gain_ref, w_qkv, query_ref, kv_ref, normed):
    rows, depth = pair_ref.shape[0] // 2, pair_ref.shape[1]
    gain = gain_ref[...]
    normed[:2 * rows, :] = normal(pair_ref[...], gain)
    normed[2 * rows:, :] = normal(near_ref[...], gain)
    kv_ref[...] = jnp.dot(normed[...], w_qkv[:, depth:], preferred_element_type=F32).astype(BF16)
    query_ref[...] = jnp.dot(normed[rows:, :], w_qkv[:, :depth], preferred_element_type=F32).astype(BF16)


def project(pair, near, gain, w_qkv):
    rows, depth = pair.shape[0] // 2, pair.shape[1]
    return pl.pallas_call(
        project_kernel,
        out_shape=(kept((3 * rows, depth)), kept((4 * rows, 2 * depth))),
        in_specs=[VMEM] * 4,
        out_specs=(VMEM,) * 2,
        scratch_shapes=[pltpu.VMEM((4 * rows, depth), BF16)],
        compiler_params=pltpu.CompilerParams(vmem_limit_bytes=8 << 20),
        cost_estimate=pl.CostEstimate(
            flops=22 * rows * depth * depth, bytes_accessed=2 * rows * depth, transcendentals=0
        ),
        name="project",
    )(pair, near, gain, w_qkv)


def attention(query, window, keep):
    depth = query.shape[1]
    heads = []
    for h in range(depth // HD):
        cols = slice(h * HD, (h + 1) * HD)
        value_cols = slice(depth + h * HD, depth + (h + 1) * HD)
        scores = jnp.concatenate([
            lax.dot_general(
                query[:, cols], ref[first:first + size, cols], (((1,), (1,)), ((), ())), preferred_element_type=F32
            )
            for ref, first, size in window
        ], axis=1)
        scores = jnp.where(keep, scores, -jnp.inf) * (HD ** -0.5)
        grown = jnp.exp(scores - jnp.max(scores, axis=-1, keepdims=True))
        share = 1.0 / jnp.sum(grown, axis=-1, keepdims=True)
        grown = grown.astype(BF16)
        start, taken = 0, None
        for ref, first, size in window:
            term = jnp.dot(
                grown[:, start:start + size], ref[first:first + size, value_cols], preferred_element_type=F32
            )
            taken = term if taken is None else taken + term
            start += size
        heads.append((taken * share).astype(BF16))
    return jnp.concatenate(heads, axis=1)


def kept_lanes(rows, absent):
    block = (lax.broadcasted_iota(jnp.int32, (rows, (2 * REACH + 1) * rows), 1) // rows).astype(F32)
    return block != outward_of().astype(F32) * absent.astype(F32) + REACH


def attend_own_kernel(base_ref, own_ref, query_ref, kv_ref, behind_ref, gain_ref, w_qkv, w_out, ring_ref, kv_behind):
    rows, depth = own_ref.shape
    kv_behind[...] = jnp.dot(
        normal(behind_ref[...], gain_ref[...]), w_qkv[:, depth:], preferred_element_type=F32
    ).astype(BF16)
    keep = kept_lanes(rows, base_ref[2 * rows:2 * rows + 1, 0:1])
    mixed = attention(query_ref[:rows, :], [(kv_behind, 0, rows), (kv_ref, 0, 4 * rows)], keep)
    ring_ref[...] = (own_ref[...] + jnp.dot(mixed, w_out[...], preferred_element_type=F32)).astype(BF16)


def attend_near_kernel(
    sums_ref, near_ref, query_ref, kv_ref, far_ref, gain_ref, w_qkv, w_out, after, ring_ref, kv_far, mixed
):
    del after
    rows, depth = near_ref.shape[0] // 2, near_ref.shape[1]
    kv_far[...] = jnp.dot(
        normal(far_ref[...], gain_ref[...]), w_qkv[:, depth:], preferred_element_type=F32
    ).astype(BF16)
    windows = [
        [(kv_ref, 0, 4 * rows), (kv_far, 0, rows)],
        [(kv_ref, rows, 3 * rows), (kv_far, 0, 2 * rows)],
    ]
    for n, window in enumerate(windows):
        keep = kept_lanes(rows, sums_ref[2 * rows:2 * rows + 1, n:n + 1])
        mixed[n * rows:(n + 1) * rows, :] = attention(query_ref[(n + 1) * rows:(n + 2) * rows, :], window, keep)
    added = jnp.dot(mixed[...], w_out[...], preferred_element_type=F32)
    ring_ref[...] = (near_ref[...].astype(F32) + added).astype(BF16)


def attend_own(base, own, query, kv, behind, gain, w_qkv, w_out):
    rows, depth = own.shape
    return pl.pallas_call(
        attend_own_kernel,
        out_shape=kept((rows, depth)),
        in_specs=[VMEM] * 8,
        out_specs=VMEM,
        scratch_shapes=[pltpu.VMEM((rows, 2 * depth), BF16)],
        compiler_params=pltpu.CompilerParams(vmem_limit_bytes=12 << 20),
        cost_estimate=pl.CostEstimate(
            flops=20 * rows * depth * depth, bytes_accessed=2 * rows * depth, transcendentals=0
        ),
        name="attend_own",
    )(base, own, query, kv, behind, gain, w_qkv, w_out)


def attend_near(sums, near, query, kv, far, gain, w_qkv, w_out, after):
    rows, depth = near.shape[0] // 2, near.shape[1]
    return pl.pallas_call(
        attend_near_kernel,
        out_shape=kept((2 * rows, depth)),
        in_specs=[VMEM] * 8 + [ANY],
        out_specs=VMEM,
        scratch_shapes=[pltpu.VMEM((2 * rows, 2 * depth), BF16), pltpu.VMEM((2 * rows, depth), BF16)],
        compiler_params=pltpu.CompilerParams(vmem_limit_bytes=12 << 20),
        cost_estimate=pl.CostEstimate(
            flops=40 * rows * depth * depth, bytes_accessed=2 * rows * depth, transcendentals=0
        ),
        name="attend_near",
    )(sums, near, query, kv, far, gain, w_qkv, w_out, after)


def halved(rows, first):
    return jnp.dot(rows * BF16(0.5), first, preferred_element_type=F32)


def grid_hidden_kernel(enc_ref, first, after, out_ref):
    del after
    tile, part = tiles_of(*out_ref.shape)
    for j in range(out_ref.shape[1] // part):
        cols = slice(j * part, (j + 1) * part)
        for r in range(out_ref.shape[0] // tile):
            cut = slice(r * tile, (r + 1) * tile)
            out_ref[cut, cols] = halved(enc_ref[cut, :], first[:, cols]).astype(BF16)


def grid_hidden(encoded, first, after):
    cells, depth = encoded.shape
    hidden = first.shape[1]
    return pl.pallas_call(
        grid_hidden_kernel,
        out_shape=kept((cells, hidden)),
        in_specs=[VMEM] * 2 + [ANY],
        out_specs=VMEM,
        compiler_params=pltpu.CompilerParams(vmem_limit_bytes=12 << 20),
        cost_estimate=pl.CostEstimate(
            flops=2 * cells * depth * hidden, bytes_accessed=2 * (cells + hidden) * depth, transcendentals=0
        ),
        name="grid_hidden",
    )(encoded, first, after)


def mesh_hidden_kernel(ring_own, ring_near, first, out_ref):
    rows = ring_own.shape[0]
    out_ref[REACH * rows:(REACH + 1) * rows, :] = halved(ring_own[...], first[...])
    out_ref[(REACH + 1) * rows:, :] = halved(ring_near[...], first[...])


def mesh_hidden(ring_own, ring_near, first):
    rows, depth = ring_own.shape
    return pl.pallas_call(
        mesh_hidden_kernel,
        out_shape=kept(((2 * REACH + 1) * rows, first.shape[1]), F32),
        in_specs=[VMEM] * 3,
        out_specs=VMEM,
        compiler_params=pltpu.CompilerParams(vmem_limit_bytes=12 << 20),
        cost_estimate=pl.CostEstimate(
            flops=6 * rows * depth * first.shape[1], bytes_accessed=2 * rows * depth, transcendentals=0
        ),
        name="mesh_hidden",
    )(ring_own, ring_near, first)


def decode_kernel(
    owner, weight_ref, ring_own, ring_near, back_own, back_near, grid_ref, mesh_in, enc_ref, first, second,
    out_hbm, mesh_hbm, mesh_ref,
    x_ref, act, ring, io_sems,
):
    del mesh_in
    rows = ring_own.shape[0]
    tile, part = tiles_of(x_ref.shape[0], first.shape[1])
    tile = min(tile, 256)
    tiles, parts = x_ref.shape[0] // tile, first.shape[1] // part
    stores = [pltpu.make_async_copy(ring_own, mesh_hbm, io_sems.at[tiles])]
    stores[0].start()
    mine, count = lax.axis_index(AXES), lax.axis_size(AXES)
    outward = outward_of()
    mesh_ref[:rows, :] = halved(back_near[...], first[...])
    mesh_ref[rows:2 * rows, :] = halved(back_own[...], first[...])
    ring[:rows, :] = back_near[...]
    ring[rows:2 * rows, :] = back_own[...]
    ring[2 * rows:3 * rows, :] = ring_own[...]
    ring[3 * rows:, :] = ring_near[...]
    columns = jnp.transpose(weight_ref[...])
    for r in range(tiles):
        cut = slice(r * tile, (r + 1) * tile)
        for b in range(r * tile // rows, (r + 1) * tile // rows):
            slot = outward * offset_of(owner[b], mine, count) + REACH
            lines = pl.ds(pl.multiple_of(slot * rows, rows), rows)
            block = slice(b * rows, (b + 1) * rows)
            weight = columns[:, b:b + 1]
            for j in range(parts):
                cols = slice(j * part, (j + 1) * part)
                half = grid_ref[block, cols].astype(F32) + weight * mesh_ref[lines, cols]
                act[block, cols] = (half * jnp.tanh(half) + half).astype(BF16)
            x_ref[block, :] = (enc_ref[block, :].astype(F32) + weight * ring[lines, :].astype(F32)).astype(BF16)
        out = jnp.dot(act[cut, :], second[...], preferred_element_type=F32)
        x_ref[cut, :] = (x_ref[cut, :].astype(F32) + out).astype(BF16)
        copy = pltpu.make_async_copy(x_ref.at[pl.ds(r * tile, tile)], out_hbm.at[pl.ds(r * tile, tile)], io_sems.at[r])
        copy.start()
        stores.append(copy)
    for copy in stores:
        copy.wait()


def decode(owner, weights, ring_own, ring_near, back_own, back_near, grid_part, mesh_part, encoded, first, second):
    cells, depth = encoded.shape
    hidden = first.shape[1]
    rows = ring_own.shape[0]
    return pl.pallas_call(
        decode_kernel,
        out_shape=(
            jax.ShapeDtypeStruct((cells, depth), BF16),
            jax.ShapeDtypeStruct((rows, depth), BF16),
            kept(mesh_part.shape, F32),
        ),
        in_specs=[SMEM] + [VMEM] * 10,
        out_specs=(ANY, ANY, VMEM),
        input_output_aliases={7: 2},
        scratch_shapes=[
            pltpu.VMEM((cells, depth), BF16),
            pltpu.VMEM((cells, hidden), BF16),
            pltpu.VMEM(((2 * REACH + 1) * rows, depth), BF16),
            pltpu.SemaphoreType.DMA((cells // min(cells, 256) + 1,)),
        ],
        compiler_params=pltpu.CompilerParams(vmem_limit_bytes=16 << 20),
        cost_estimate=pl.CostEstimate(
            flops=2 * cells * depth * hidden, bytes_accessed=4 * (cells + hidden) * depth, transcendentals=cells * hidden
        ),
        name="decode",
    )(owner, weights, ring_own, ring_near, back_own, back_near, grid_part, mesh_part, encoded, first, second)[:2]


def on_device(
    grid, g2m_owner, g2m_weight, m2g_owner, m2g_weight, mesh_feat, neighbours,
    enc_w1, enc_w2, attn_gain, w_qkv, w_out, dec_w1, dec_w2,
):
    rows = mesh_feat.shape[0]
    nblocks = g2m_owner.shape[0]
    encoded, message, base, local = encode(
        g2m_owner, neighbours, g2m_weight.reshape(nblocks, rows), mesh_feat, grid, enc_w1, enc_w2
    )
    outgoing = outgoing_sums(base, swapped(message))
    sums = from_outward(outgoing, 1)
    grid_part = grid_hidden(encoded, dec_w1, outgoing)
    share, message = chip_share(local, sums, grid_part)
    own, pair, message = chip_states(share, swapped(message))
    near = from_outward(message, 1)
    far = from_outward(message, 2)
    behind = swapped(near[:rows])
    query, kv = project(pair, near, attn_gain, w_qkv[0])
    ring_own = attend_own(base, own, query, kv, behind, attn_gain, w_qkv[0], w_out[0])
    ring_near = attend_near(sums, near, query, kv, far, attn_gain, w_qkv[0], w_out[0], ring_own)
    back_own = swapped(ring_own)
    back_near = swapped(ring_near[:rows])
    mesh_part = mesh_hidden(ring_own, ring_near, dec_w1)
    return decode(
        m2g_owner, m2g_weight.reshape(nblocks, rows), ring_own, ring_near, back_own, back_near,
        grid_part, mesh_part, encoded, dec_w1, dec_w2,
    )


def solution(mesh):
    split = P(AXES, None)
    flat = P(AXES)
    in_specs = (split, flat, flat, flat, flat, split, split) + (P(),) * 7
    return jax.shard_map(
        on_device, mesh=mesh, in_specs=in_specs, out_specs=(split, split), check_vma=False
    )
```

time: 52.7 us -> 45.9 us (0.87)
  waiting for transfers between devices: 15.2 us -> 9.75 us
  local copies, waits for them, and re-layouts: 1.38 us -> 0.06 us
  Pallas kernels: 22 us -> 21.4 us
    ppermute x3, waiting for transfers between devices: 11.1 us -> 6.88 us  [from_outward(): return lax.ppermute(block, AXES, route)]
    pallas_call x3 -> x5, Pallas kernels: 7.26 us -> 9.4 us  [the longest x1 3.22 us: attend_near(): pl.pallas_call(attend_near_kernel, out_shape=kept((2 * rows, depth)), in_...]
    pallas_call x1, Pallas kernels: 6.45 us -> 4.88 us  [decode(): pl.pallas_call(decode_kernel, out_shape=(jax.ShapeDtypeStruct((cells, dep...]
    unnamed x18 -> x14, local copies, waits for them, and re-layouts: 1.34 us -> 0.04 us
    ppermute x4 -> x5, waiting for transfers between devices: 4.05 us -> 2.87 us  [swapped(): return lax.ppermute(block, AXES, [(i, i ^ 1) for i in range(count)])]
    pallas_call x1, Pallas kernels: 8.1 us -> 6.94 us  [encode(): pl.pallas_call(encode_kernel, out_shape=(kept((cells, depth)), kept((rows...]
    ppermute x4 -> x5, starting transfers between devices: 0.74 us -> 1.22 us  [swapped(): return lax.ppermute(block, AXES, [(i, i ^ 1) for i in range(count)])]
  transfers between devices with their start and end apart: 7 -> 8, of which waited for: 6 -> 6; matrix products, arithmetic and copies ran while one was open for 0% -> 0% of each run, Pallas kernels for 2% -> 14%
where the time goes in v4:
time: 45.9 us; the launch traced here: 45.7 us
  Pallas kernels  21.4 us (47%)
  starting transfers between devices  13.5 us (29%)
  waiting for transfers between devices  9.75 us (21%)
  between operations  0.97 us (2%)
    ppermute x3, starting transfers between devices, from_outward(): return lax.ppermute(block, AXES, route)  12.3 us
    pallas_call x1, Pallas kernels, encode(): pl.pallas_call(encode_kernel, out_shape=(kept((cells, depth)), kept((rows...  6.94 us
    ppermute x3, waiting for transfers between devices, from_outward(): return lax.ppermute(block, AXES, route)  6.88 us
    pallas_call x1, Pallas kernels, decode(): pl.pallas_call(decode_kernel, out_shape=(jax.ShapeDtypeStruct((cells, dep...  4.88 us
    pallas_call x1, Pallas kernels, attend_near(): pl.pallas_call(attend_near_kernel, out_shape=kept((2 * rows, depth)), in_...  3.22 us
    ppermute x5, waiting for transfers between devices, swapped(): return lax.ppermute(block, AXES, [(i, i ^ 1) for i in range(count)])  2.87 us
    pallas_call x1, Pallas kernels, grid_hidden(): pl.pallas_call(grid_hidden_kernel, out_shape=kept((cells, hidden)), in_sp...  2.35 us
    pallas_call x1, Pallas kernels, attend_own(): pl.pallas_call(attend_own_kernel, out_shape=kept((rows, depth)), in_specs...  1.86 us
  transfers between devices with their start and end apart: 8, of which 6 were waited for; matrix products, arithmetic and copies ran while one was open for 0% of the time, Pallas kernels for 14%

profile of v4, /device:TPU:0, one launch (start us, length us, event | category | flops | bytes accessed | tf_op | source)
XLA Modules:
  0.0 45.7 jit_solution(11956551169409710996)
XLA Ops:
  0.6 6.9 %encode.1 = (bf16[1024,512]{1,0:T(8,128)(2,1)S(1)}, bf16[144,512]{1,0:T(8,128)(2,1)S(1)}, bf16[272,512]{1,0:T(8,128)(2,1)S(1)}, f32[256,512]{1,0:T(8,128)S(1)}) custom-call(s32[8]{0:T(128)} %owner_hbm.1, s32[1,3]{1,0:T(1,128)} %listed_hbm.1, f32[8,128]{1,0:T(8,128)} %bitcast.10, bf16[128,512]{1,0:T(8,128)(2,1)} %feat_hbm.1, bf16[1024,512]{1,0:T(8,128)(2,1)} %x_hbm.1, ...), custom_call_target="tpu_custom_call" | custom-call | flops 4294967296 | bytes 6291456 | tf_op jit(solution)/shard_map/encode/pallas_call | solution.py:131
  7.6 0.5 %collective-permute-start = (bf16[144,512]{1,0:T(8,128)(2,1)S(1)}, bf16[144,512]{1,0:T(8,128)(2,1)S(1)}, u32[]{:S(2)}, u32[]{:S(2)}) collective-permute-start(bf16[144,512]{1,0:T(8,128)(2,1)S(1)} %get-tuple-element.17), channel_id=1, source_target_pairs={{0,1},{1,0},{2,3},{3,2},{4,5},{5,4},{6,7},{7,6},{8,9},{9,8},{10,11... | collective-permute-start | bytes 442376 | tf_op jit(solution)/shard_map/ppermute | solution.py:23
  8.1 1.0 %collective-permute-done.arrived_ref = bf16[144,512]{1,0:T(8,128)(2,1)S(1)} collective-permute-done((bf16[144,512]{1,0:T(8,128)(2,1)S(1)}, bf16[144,512]{1,0:T(8,128)(2,1)S(1)}, u32[]{:S(2)}, u32[]{:S(2)}) %collective-permute-start) | collective-permute-done | bytes 147488 | tf_op jit(solution)/shard_map/ppermute | solution.py:23
  9.2 6.7 %collective-permute-start.1 = (bf16[272,512]{1,0:T(8,128)(2,1)S(1)}, bf16[272,512]{1,0:T(8,128)(2,1)S(1)}, u32[]{:S(2)}, u32[]{:S(2)}) collective-permute-start(bf16[272,512]{1,0:T(8,128)(2,1)S(1)} %outgoing_sums.1.after), channel_id=1, source_target_pairs={{0,31},{1,2},{2,1},{3,4},{4,3},{5,6},{6,5},{7,8},{8,7},{9,10},{10,... | collective-permute-start | bytes 835592 | tf_op jit(solution)/shard_map/ppermute | solution.py:32
  15.8 2.3 %grid_hidden.1.after.grid_ref = bf16[1024,2048]{1,0:T(8,128)(2,1)S(1)} custom-call(bf16[1024,512]{1,0:T(8,128)(2,1)S(1)} %get-tuple-element.18.enc_ref, bf16[512,2048]{1,0:T(8,128)(2,1)S(1)} %copy-done, bf16[272,512]{1,0:T(8,128)(2,1)S(1)} %outgoing_sums.1.after), custom_call_target="tpu_custom_call" | custom-call | flops 2147483648 | bytes 3145728 | tf_op jit(solution)/shard_map/grid_hidden/pallas_call | solution.py:355
  18.2 2.0 %collective-permute-done.1.arrived_ref.sums_ref = bf16[272,512]{1,0:T(8,128)(2,1)S(1)} collective-permute-done((bf16[272,512]{1,0:T(8,128)(2,1)S(1)}, bf16[272,512]{1,0:T(8,128)(2,1)S(1)}, u32[]{:S(2)}, u32[]{:S(2)}) %collective-permute-start.1) | collective-permute-done | bytes 278560 | tf_op jit(solution)/shard_map/ppermute | solution.py:32
  20.2 0.1 chip_share.1
  20.3 0.0 copy-start.3
  20.3 0.1 collective-permute-start.2
  20.4 1.5 %collective-permute-done.2.other_ref = bf16[256,512]{1,0:T(8,128)(2,1)S(1)} collective-permute-done((bf16[256,512]{1,0:T(8,128)(2,1)S(1)}, bf16[256,512]{1,0:T(8,128)(2,1)S(1)}, u32[]{:S(2)}, u32[]{:S(2)}) %collective-permute-start.2) | collective-permute-done | bytes 262176 | tf_op jit(solution)/shard_map/ppermute | solution.py:23
  21.9 0.1 chip_states.1
  22.0 5.3 %collective-permute-start.3 = (bf16[256,512]{1,0:T(8,128)(2,1)S(1)}, bf16[256,512]{1,0:T(8,128)(2,1)S(1)}, u32[]{:S(2)}, u32[]{:S(2)}) collective-permute-start(bf16[256,512]{1,0:T(8,128)(2,1)S(1)} %get-tuple-element.23), channel_id=1, source_target_pairs={{0,31},{1,2},{2,1},{3,4},{4,3},{5,6},{6,5},{7,8},{8,7},{9,10},{10,... | collective-permute-start | bytes 786440 | tf_op jit(solution)/shard_map/ppermute | solution.py:32
  27.3 0.3 collective-permute-start.5
  27.6 4.0 %collective-permute-done.3.near_ref = bf16[256,512]{1,0:T(8,128)(2,1)S(1)} collective-permute-done((bf16[256,512]{1,0:T(8,128)(2,1)S(1)}, bf16[256,512]{1,0:T(8,128)(2,1)S(1)}, u32[]{:S(2)}, u32[]{:S(2)}) %collective-permute-start.3) | collective-permute-done | bytes 262176 | tf_op jit(solution)/shard_map/ppermute | solution.py:32
  31.6 0.1 collective-permute-start.4
  31.6 0.0 copy-done.2
  31.7 0.0 copy-done.5
  31.7 1.0 %project.1 = (bf16[384,512]{1,0:T(8,128)(2,1)S(1)}, bf16[512,1024]{1,0:T(8,128)(2,1)S(1)}) custom-call(bf16[256,512]{1,0:T(8,128)(2,1)S(1)} %get-tuple-element.22.pair_ref, bf16[256,512]{1,0:T(8,128)(2,1)S(1)} %collective-permute-done.3.near_ref, f32[1,512]{1,0:T(1,128)S(1)} %copy-done.5, bf16[512,1536]{1,0:T(8,128)(2,1)S(1)} %bitcast.4), custom_call_target="tpu_custom_call" | custom-call | flops 738197504 | bytes 131072 | tf_op jit(solution)/shard_map/project/pallas_call | solution.py:231
  32.7 0.3 collective-permute-done.4.behind_ref
  33.0 0.0 copy-done.3
  33.0 1.9 %attend_own.1.after.ring_own = bf16[128,512]{1,0:T(8,128)(2,1)S(1)} custom-call(bf16[272,512]{1,0:T(8,128)(2,1)S(1)} %get-tuple-element.15.base_ref, f32[128,512]{1,0:T(8,128)S(1)} %get-tuple-element.21.own_ref, bf16[384,512]{1,0:T(8,128)(2,1)S(1)} %get-tuple-element.24.query_ref, bf16[512,1024]{1,0:T(8,128)(2,1)S(1)} %get-tuple-element.25.kv_ref, ...), custom_call_target="tpu_custom_call" | custom-call | flops 671088640 | bytes 131072 | tf_op jit(solution)/shard_map/attend_own/pallas_call | solution.py:308
  34.9 0.9 %collective-permute-done.5.far_ref = bf16[256,512]{1,0:T(8,128)(2,1)S(1)} collective-permute-done((bf16[256,512]{1,0:T(8,128)(2,1)S(1)}, bf16[256,512]{1,0:T(8,128)(2,1)S(1)}, u32[]{:S(2)}, u32[]{:S(2)}) %collective-permute-start.5) | collective-permute-done | bytes 262176 | tf_op jit(solution)/shard_map/ppermute | solution.py:32
  35.8 3.2 %attend_near.1.ring_near = bf16[256,512]{1,0:T(8,128)(2,1)S(1)} custom-call(bf16[272,512]{1,0:T(8,128)(2,1)S(1)} %collective-permute-done.1.arrived_ref.sums_ref, bf16[256,512]{1,0:T(8,128)(2,1)S(1)} %collective-permute-done.3.near_ref, bf16[384,512]{1,0:T(8,128)(2,1)S(1)} %get-tuple-element.24.query_ref, bf16[512,1024]{1,0:T(8,128)(2,1)S(1)} %get-tuple-element.25.kv_ref, ...), custom_call_target="tpu_custom_call" | custom-call | flops 1342177280 | bytes 131072 | tf_op jit(solution)/shard_map/attend_near/pallas_call | solution.py:324
  39.0 0.0 copy-start.1
  39.0 0.0 copy-start.4
  39.0 0.0 copy-start.6
  39.1 0.1 collective-permute-start.7
  39.1 0.5 %collective-permute-start.6 = (bf16[128,512]{1,0:T(8,128)(2,1)S(1)}, bf16[128,512]{1,0:T(8,128)(2,1)S(1)}, u32[]{:S(2)}, u32[]{:S(2)}) collective-permute-start(bf16[128,512]{1,0:T(8,128)(2,1)S(1)} %attend_own.1.after.ring_own), channel_id=1, source_target_pairs={{0,1},{1,0},{2,3},{3,2},{4,5},{5,4},{6,7},{7,6},{8,9},{9,8},{10,11... | collective-permute-start | bytes 393224 | tf_op jit(solution)/shard_map/ppermute | solution.py:23
  39.6 1.0 %mesh_hidden.1.mesh_in = f32[640,2048]{1,0:T(8,128)S(1)} custom-call(bf16[128,512]{1,0:T(8,128)(2,1)S(1)} %attend_own.1.after.ring_own, bf16[256,512]{1,0:T(8,128)(2,1)S(1)} %attend_near.1.ring_near, bf16[512,2048]{1,0:T(8,128)(2,1)S(1)} %copy-done), custom_call_target="tpu_custom_call" | custom-call | flops 805306368 | bytes 131072 | tf_op jit(solution)/shard_map/mesh_hidden/pallas_call | solution.py:376
  40.6 0.0 collective-permute-done.7.back_near
  40.6 0.0 collective-permute-done.6.back_own
  40.7 4.9 %decode.1 = (bf16[1024,512]{1,0:T(8,128)(2,1)}, bf16[128,512]{1,0:T(8,128)(2,1)}, f32[640,2048]{1,0:T(8,128)S(1)}) custom-call(s32[8]{0:T(128)S(1)} %copy-done.6, f32[8,128]{1,0:T(8,128)S(1)} %bitcast.9, bf16[128,512]{1,0:T(8,128)(2,1)S(1)} %attend_own.1.after.ring_own, bf16[256,512]{1,0:T(8,128)(2,1)S(1)} %attend_near.1.ring_near, ...), custom_call_target="tpu_custom_call", output_to_operand_aliasing={{2}: (7, {})} | custom-call | flops 2147483648 | bytes 6291456 | tf_op jit(solution)/shard_map/decode/pallas_call | solution.py:435
  (10 shorter events, 0.1 us)
Async XLA Ops:
  0.6 15.2 %copy-start = (bf16[512,2048]{1,0:T(8,128)(2,1)S(1)}, bf16[512,2048]{1,0:T(8,128)(2,1)}, u32[]{:S(2)}) copy-start(bf16[512,2048]{1,0:T(8,128)(2,1)} %first.5) | copy-start | bytes 6291460
  7.6 1.5 %collective-permute-start = (bf16[144,512]{1,0:T(8,128)(2,1)S(1)}, bf16[144,512]{1,0:T(8,128)(2,1)S(1)}, u32[]{:S(2)}, u32[]{:S(2)}) collective-permute-start(bf16[144,512]{1,0:T(8,128)(2,1)S(1)} %get-tuple-element.17), channel_id=1, source_target_pairs={{0,1},{1,0},{2,3},{3,2},{4,5},{5,4},{6,7},{7,6},{8,9},{9,8},{10,11... | collective-permute-start | bytes 442376 | tf_op jit(solution)/shard_map/ppermute | solution.py:23
  9.2 11.0 %collective-permute-start.1 = (bf16[272,512]{1,0:T(8,128)(2,1)S(1)}, bf16[272,512]{1,0:T(8,128)(2,1)S(1)}, u32[]{:S(2)}, u32[]{:S(2)}) collective-permute-start(bf16[272,512]{1,0:T(8,128)(2,1)S(1)} %outgoing_sums.1.after), channel_id=1, source_target_pairs={{0,31},{1,2},{2,1},{3,4},{4,3},{5,6},{6,5},{7,8},{8,7},{9,10},{10,... | collective-permute-start | bytes 835592 | tf_op jit(solution)/shard_map/ppermute | solution.py:32
  20.2 11.5 %copy-start.2 = (bf16[1,512,1536]{2,1,0:T(8,128)(2,1)S(1)}, bf16[1,512,1536]{2,1,0:T(8,128)(2,1)}, u32[]{:S(2)}) copy-start(bf16[1,512,1536]{2,1,0:T(8,128)(2,1)} %param.24) | copy-start | bytes 4718596
  20.2 11.5 %copy-start.5 = (f32[1,512]{1,0:T(1,128)S(1)}, f32[1,512]{1,0:T(1,128)}, u32[]{:S(2)}) copy-start(f32[1,512]{1,0:T(1,128)} %gain_ref.5) | copy-start | bytes 6148
  20.3 12.7 %copy-start.3 = (bf16[1,512,512]{2,1,0:T(8,128)(2,1)S(1)}, bf16[1,512,512]{2,1,0:T(8,128)(2,1)}, u32[]{:S(2)}) copy-start(bf16[1,512,512]{2,1,0:T(8,128)(2,1)} %param.25) | copy-start | bytes 1572868
  20.3 1.6 %collective-permute-start.2 = (bf16[256,512]{1,0:T(8,128)(2,1)S(1)}, bf16[256,512]{1,0:T(8,128)(2,1)S(1)}, u32[]{:S(2)}, u32[]{:S(2)}) collective-permute-start(bf16[256,512]{1,0:T(8,128)(2,1)S(1)} %get-tuple-element.20), channel_id=1, source_target_pairs={{0,1},{1,0},{2,3},{3,2},{4,5},{5,4},{6,7},{7,6},{8,9},{9,8},{10,11... | collective-permute-start | bytes 786440 | tf_op jit(solution)/shard_map/ppermute | solution.py:23
  22.0 9.6 %collective-permute-start.3 = (bf16[256,512]{1,0:T(8,128)(2,1)S(1)}, bf16[256,512]{1,0:T(8,128)(2,1)S(1)}, u32[]{:S(2)}, u32[]{:S(2)}) collective-permute-start(bf16[256,512]{1,0:T(8,128)(2,1)S(1)} %get-tuple-element.23), channel_id=1, source_target_pairs={{0,31},{1,2},{2,1},{3,4},{4,3},{5,6},{6,5},{7,8},{8,7},{9,10},{10,... | collective-permute-start | bytes 786440 | tf_op jit(solution)/shard_map/ppermute | solution.py:32
  27.3 8.5 %collective-permute-start.5 = (bf16[256,512]{1,0:T(8,128)(2,1)S(1)}, bf16[256,512]{1,0:T(8,128)(2,1)S(1)}, u32[]{:S(2)}, u32[]{:S(2)}) collective-permute-start(bf16[256,512]{1,0:T(8,128)(2,1)S(1)} %get-tuple-element.23), channel_id=1, source_target_pairs={{0,29},{1,4},{2,31},{3,6},{4,1},{5,8},{6,3},{7,10},{8,5},{9,12},{1... | collective-permute-start | bytes 786440 | tf_op jit(solution)/shard_map/ppermute | solution.py:32
  31.6 1.4 %collective-permute-start.4 = (bf16[128,512]{1,0:T(8,128)(2,1)S(1)}, bf16[128,512]{1,0:T(8,128)(2,1)S(1)}, u32[]{:S(2)}, u32[]{:S(2)}) collective-permute-start(bf16[128,512]{1,0:T(8,128)(2,1)S(1)} %slice.8), channel_id=1, source_target_pairs={{0,1},{1,0},{2,3},{3,2},{4,5},{5,4},{6,7},{7,6},{8,9},{9,8},{10,11... | collective-permute-start | bytes 393224 | tf_op jit(solution)/shard_map/ppermute | solution.py:23
  39.0 1.6 %copy-start.1 = (bf16[2048,512]{1,0:T(8,128)(2,1)S(1)}, bf16[2048,512]{1,0:T(8,128)(2,1)}, u32[]{:S(2)}) copy-start(bf16[2048,512]{1,0:T(8,128)(2,1)} %second.1) | copy-start | bytes 6291460
  39.0 1.6 %copy-start.4 = (f32[1024]{0:T(1024)S(1)}, f32[1024]{0:T(1024)}, u32[]{:S(2)}) copy-start(f32[1024]{0:T(1024)} %param.18) | copy-start | bytes 12292
  39.0 1.6 %copy-start.6 = (s32[8]{0:T(128)S(1)}, s32[8]{0:T(128)}, u32[]{:S(2)}) copy-start(s32[8]{0:T(128)} %owner.1) | copy-start | bytes 100
  39.1 1.6 %collective-permute-start.7 = (bf16[128,512]{1,0:T(8,128)(2,1)S(1)}, bf16[128,512]{1,0:T(8,128)(2,1)S(1)}, u32[]{:S(2)}, u32[]{:S(2)}) collective-permute-start(bf16[128,512]{1,0:T(8,128)(2,1)S(1)} %slice.9), channel_id=1, source_target_pairs={{0,1},{1,0},{2,3},{3,2},{4,5},{5,4},{6,7},{7,6},{8,9},{9,8},{10,11... | collective-permute-start | bytes 393224 | tf_op jit(solution)/shard_map/ppermute | solution.py:23
  39.1 1.5 %collective-permute-start.6 = (bf16[128,512]{1,0:T(8,128)(2,1)S(1)}, bf16[128,512]{1,0:T(8,128)(2,1)S(1)}, u32[]{:S(2)}, u32[]{:S(2)}) collective-permute-start(bf16[128,512]{1,0:T(8,128)(2,1)S(1)} %attend_own.1.after.ring_own), channel_id=1, source_target_pairs={{0,1},{1,0},{2,3},{3,2},{4,5},{5,4},{6,7},{7,6},{8,9},{9,8},{10,11... | collective-permute-start | bytes 393224 | tf_op jit(solution)/shard_map/ppermute | solution.py:23

commit v5 on v4

--- a/solution.py
+++ b/solution.py
@@ -104,7 +104,8 @@
     for copy in twos + small:
         copy.wait()
     columns = jnp.transpose(weight_ref[...])
-    for r in range(tiles):
+    tile = min(tile, 256)
+    for r in range(enc_ref.shape[0] // tile):
         cut = slice(r * tile, (r + 1) * tile)
         out = jnp.dot(act[cut, :], second[...], preferred_element_type=F32)
         enc_ref[cut, :] = (enc_ref[cut, :].astype(F32) + out).astype(BF16)
@@ -254,18 +255,16 @@
             )
             for ref, first, size in window
         ], axis=1)
-        scores = jnp.where(keep, scores, -jnp.inf) * (HD ** -0.5)
-        grown = jnp.exp(scores - jnp.max(scores, axis=-1, keepdims=True))
-        share = 1.0 / jnp.sum(grown, axis=-1, keepdims=True)
-        grown = grown.astype(BF16)
+        scores = jnp.where(keep, scores, -jnp.inf)
+        below = (scores - jnp.max(scores, axis=-1, keepdims=True)) * (HD ** -0.5)
+        grown = jnp.exp(below.astype(BF16))
         start, taken = 0, None
         for ref, first, size in window:
-            term = jnp.dot(
-                grown[:, start:start + size], ref[first:first + size, value_cols], preferred_element_type=F32
-            )
+            value = jnp.concatenate([ref[first:first + size, value_cols], jnp.ones((size, HD), BF16)], axis=1)
+            term = jnp.dot(grown[:, start:start + size], value, preferred_element_type=F32)
             taken = term if taken is None else taken + term
             start += size
-        heads.append((taken * share).astype(BF16))
+        heads.append((taken[:, :HD] / taken[:, HD:]).astype(BF16))
     return jnp.concatenate(heads, axis=1)
 
 
@@ -367,15 +366,15 @@
 
 def mesh_hidden_kernel(ring_own, ring_near, first, out_ref):
     rows = ring_own.shape[0]
-    out_ref[REACH * rows:(REACH + 1) * rows, :] = halved(ring_own[...], first[...])
-    out_ref[(REACH + 1) * rows:, :] = halved(ring_near[...], first[...])
+    out_ref[REACH * rows:(REACH + 1) * rows, :] = halved(ring_own[...], first[...]).astype(BF16)
+    out_ref[(REACH + 1) * rows:, :] = halved(ring_near[...], first[...]).astype(BF16)
 
 
 def mesh_hidden(ring_own, ring_near, first):
     rows, depth = ring_own.shape
     return pl.pallas_call(
         mesh_hidden_kernel,
-        out_shape=kept(((2 * REACH + 1) * rows, first.shape[1]), F32),
+        out_shape=kept(((2 * REACH + 1) * rows, first.shape[1])),
         in_specs=[VMEM] * 3,
         out_specs=VMEM,
         compiler_params=pltpu.CompilerParams(vmem_limit_bytes=12 << 20),
@@ -400,8 +399,8 @@
     stores[0].start()
     mine, count = lax.axis_index(AXES), lax.axis_size(AXES)
     outward = outward_of()
-    mesh_ref[:rows, :] = halved(back_near[...], first[...])
-    mesh_ref[rows:2 * rows, :] = halved(back_own[...], first[...])
+    mesh_ref[:rows, :] = halved(back_near[...], first[...]).astype(BF16)
+    mesh_ref[rows:2 * rows, :] = halved(back_own[...], first[...]).astype(BF16)
     ring[:rows, :] = back_near[...]
     ring[rows:2 * rows, :] = back_own[...]
     ring[2 * rows:3 * rows, :] = ring_own[...]
@@ -414,10 +413,11 @@
             lines = pl.ds(pl.multiple_of(slot * rows, rows), rows)
             block = slice(b * rows, (b + 1) * rows)
             weight = columns[:, b:b + 1]
+            narrow = weight.astype(BF16)
             for j in range(parts):
                 cols = slice(j * part, (j + 1) * part)
-                half = grid_ref[block, cols].astype(F32) + weight * mesh_ref[lines, cols]
-                act[block, cols] = (half * jnp.tanh(half) + half).astype(BF16)
+                half = grid_ref[block, cols] + narrow * mesh_ref[lines, cols]
+                act[block, cols] = half * jnp.tanh(half) + half
             x_ref[block, :] = (enc_ref[block, :].astype(F32) + weight * ring[lines, :].astype(F32)).astype(BF16)
         out = jnp.dot(act[cut, :], second[...], preferred_element_type=F32)
         x_ref[cut, :] = (x_ref[cut, :].astype(F32) + out).astype(BF16)
@@ -437,7 +437,7 @@
         out_shape=(
             jax.ShapeDtypeStruct((cells, depth), BF16),
             jax.ShapeDtypeStruct((rows, depth), BF16),
-            kept(mesh_part.shape, F32),
+            kept(mesh_part.shape),
         ),
         in_specs=[SMEM] + [VMEM] * 10,
         out_specs=(ANY, ANY, VMEM),

time: 45.9 us -> 44.2 us (0.963)
  Pallas kernels: 21.4 us -> 19.5 us
    pallas_call x1, Pallas kernels: 3.22 us -> 1.98 us  [attend_near(): pl.pallas_call(attend_near_kernel, out_shape=kept((2 * rows, depth)), in_...]
    pallas_call x1, Pallas kernels: 1.86 us -> 1.37 us  [attend_own(): pl.pallas_call(attend_own_kernel, out_shape=kept((rows, depth)), in_specs...]
    ppermute x3, waiting for transfers between devices: 6.88 us -> 7.36 us  [from_outward(): return lax.ppermute(block, AXES, route)]
  transfers between devices with their start and end apart: 8 -> 8, of which waited for: 6 -> 6; matrix products, arithmetic and copies ran while one was open for 0% -> 0% of each run, Pallas kernels for 14% -> 13%
where the time goes in v5:
time: 44.2 us; the launch traced here: 44.1 us
  Pallas kernels  19.5 us (44%)
  starting transfers between devices  13.5 us (31%)
  waiting for transfers between devices  10.2 us (23%)
  between operations  0.81 us (2%)
    ppermute x3, starting transfers between devices, from_outward(): return lax.ppermute(block, AXES, route)  12.2 us
    ppermute x3, waiting for transfers between devices, from_outward(): return lax.ppermute(block, AXES, route)  7.36 us
    pallas_call x1, Pallas kernels, encode(): pl.pallas_call(encode_kernel, out_shape=(kept((cells, depth)), kept((rows...  7.01 us
    pallas_call x1, Pallas kernels, decode(): pl.pallas_call(decode_kernel, out_shape=(jax.ShapeDtypeStruct((cells, dep...  4.59 us
    ppermute x5, waiting for transfers between devices, swapped(): return lax.ppermute(block, AXES, [(i, i ^ 1) for i in range(count)])  2.87 us
    pallas_call x1, Pallas kernels, grid_hidden(): pl.pallas_call(grid_hidden_kernel, out_shape=kept((cells, hidden)), in_sp...  2.35 us
    pallas_call x1, Pallas kernels, attend_near(): pl.pallas_call(attend_near_kernel, out_shape=kept((2 * rows, depth)), in_...  1.98 us
    pallas_call x1, Pallas kernels, attend_own(): pl.pallas_call(attend_own_kernel, out_shape=kept((rows, depth)), in_specs...  1.37 us
  transfers between devices with their start and end apart: 8, of which 6 were waited for; matrix products, arithmetic and copies ran while one was open for 0% of the time, Pallas kernels for 13%

profile of v5, /device:TPU:0, one launch (start us, length us, event | category | flops | bytes accessed | tf_op | source)
XLA Modules:
  0.0 44.1 jit_solution(6205920403432952146)
XLA Ops:
  0.6 7.0 %encode.1 = (bf16[1024,512]{1,0:T(8,128)(2,1)S(1)}, bf16[144,512]{1,0:T(8,128)(2,1)S(1)}, bf16[272,512]{1,0:T(8,128)(2,1)S(1)}, f32[256,512]{1,0:T(8,128)S(1)}) custom-call(s32[8]{0:T(128)} %owner_hbm.1, s32[1,3]{1,0:T(1,128)} %listed_hbm.1, f32[8,128]{1,0:T(8,128)} %bitcast.10, bf16[128,512]{1,0:T(8,128)(2,1)} %feat_hbm.1, bf16[1024,512]{1,0:T(8,128)(2,1)} %x_hbm.1, ...), custom_call_target="tpu_custom_call" | custom-call | flops 4294967296 | bytes 6291456 | tf_op jit(solution)/shard_map/encode/pallas_call | solution.py:132
  7.7 0.5 %collective-permute-start = (bf16[144,512]{1,0:T(8,128)(2,1)S(1)}, bf16[144,512]{1,0:T(8,128)(2,1)S(1)}, u32[]{:S(2)}, u32[]{:S(2)}) collective-permute-start(bf16[144,512]{1,0:T(8,128)(2,1)S(1)} %get-tuple-element.17), channel_id=1, source_target_pairs={{0,1},{1,0},{2,3},{3,2},{4,5},{5,4},{6,7},{7,6},{8,9},{9,8},{10,11... | collective-permute-start | bytes 442376 | tf_op jit(solution)/shard_map/ppermute | solution.py:23
  8.2 1.0 %collective-permute-done.arrived_ref = bf16[144,512]{1,0:T(8,128)(2,1)S(1)} collective-permute-done((bf16[144,512]{1,0:T(8,128)(2,1)S(1)}, bf16[144,512]{1,0:T(8,128)(2,1)S(1)}, u32[]{:S(2)}, u32[]{:S(2)}) %collective-permute-start) | collective-permute-done | bytes 147488 | tf_op jit(solution)/shard_map/ppermute | solution.py:23
  9.2 6.7 %collective-permute-start.1 = (bf16[272,512]{1,0:T(8,128)(2,1)S(1)}, bf16[272,512]{1,0:T(8,128)(2,1)S(1)}, u32[]{:S(2)}, u32[]{:S(2)}) collective-permute-start(bf16[272,512]{1,0:T(8,128)(2,1)S(1)} %outgoing_sums.1.after), channel_id=1, source_target_pairs={{0,31},{1,2},{2,1},{3,4},{4,3},{5,6},{6,5},{7,8},{8,7},{9,10},{10,... | collective-permute-start | bytes 835592 | tf_op jit(solution)/shard_map/ppermute | solution.py:32
  15.9 2.3 %grid_hidden.1.after.grid_ref = bf16[1024,2048]{1,0:T(8,128)(2,1)S(1)} custom-call(bf16[1024,512]{1,0:T(8,128)(2,1)S(1)} %get-tuple-element.18.enc_ref, bf16[512,2048]{1,0:T(8,128)(2,1)S(1)} %copy-done, bf16[272,512]{1,0:T(8,128)(2,1)S(1)} %outgoing_sums.1.after), custom_call_target="tpu_custom_call" | custom-call | flops 2147483648 | bytes 3145728 | tf_op jit(solution)/shard_map/grid_hidden/pallas_call | solution.py:354
  18.2 2.0 %collective-permute-done.1.arrived_ref.sums_ref = bf16[272,512]{1,0:T(8,128)(2,1)S(1)} collective-permute-done((bf16[272,512]{1,0:T(8,128)(2,1)S(1)}, bf16[272,512]{1,0:T(8,128)(2,1)S(1)}, u32[]{:S(2)}, u32[]{:S(2)}) %collective-permute-start.1) | collective-permute-done | bytes 278560 | tf_op jit(solution)/shard_map/ppermute | solution.py:32
  20.2 0.1 chip_share.1
  20.3 0.0 copy-start.3
  20.3 0.1 collective-permute-start.2
  20.4 1.5 %collective-permute-done.2.other_ref = bf16[256,512]{1,0:T(8,128)(2,1)S(1)} collective-permute-done((bf16[256,512]{1,0:T(8,128)(2,1)S(1)}, bf16[256,512]{1,0:T(8,128)(2,1)S(1)}, u32[]{:S(2)}, u32[]{:S(2)}) %collective-permute-start.2) | collective-permute-done | bytes 262176 | tf_op jit(solution)/shard_map/ppermute | solution.py:23
  21.9 0.1 chip_states.1
  22.0 5.3 %collective-permute-start.3 = (bf16[256,512]{1,0:T(8,128)(2,1)S(1)}, bf16[256,512]{1,0:T(8,128)(2,1)S(1)}, u32[]{:S(2)}, u32[]{:S(2)}) collective-permute-start(bf16[256,512]{1,0:T(8,128)(2,1)S(1)} %get-tuple-element.23), channel_id=1, source_target_pairs={{0,31},{1,2},{2,1},{3,4},{4,3},{5,6},{6,5},{7,8},{8,7},{9,10},{10,... | collective-permute-start | bytes 786440 | tf_op jit(solution)/shard_map/ppermute | solution.py:32
  27.3 0.3 collective-permute-start.5
  27.6 4.0 %collective-permute-done.3.near_ref = bf16[256,512]{1,0:T(8,128)(2,1)S(1)} collective-permute-done((bf16[256,512]{1,0:T(8,128)(2,1)S(1)}, bf16[256,512]{1,0:T(8,128)(2,1)S(1)}, u32[]{:S(2)}, u32[]{:S(2)}) %collective-permute-start.3) | collective-permute-done | bytes 262176 | tf_op jit(solution)/shard_map/ppermute | solution.py:32
  31.6 0.1 collective-permute-start.4
  31.7 0.0 copy-done.2
  31.7 0.0 copy-done.5
  31.7 1.0 %project.1 = (bf16[384,512]{1,0:T(8,128)(2,1)S(1)}, bf16[512,1024]{1,0:T(8,128)(2,1)S(1)}) custom-call(bf16[256,512]{1,0:T(8,128)(2,1)S(1)} %get-tuple-element.22.pair_ref, bf16[256,512]{1,0:T(8,128)(2,1)S(1)} %collective-permute-done.3.near_ref, f32[1,512]{1,0:T(1,128)S(1)} %copy-done.5, bf16[512,1536]{1,0:T(8,128)(2,1)S(1)} %bitcast.4), custom_call_target="tpu_custom_call" | custom-call | flops 738197504 | bytes 131072 | tf_op jit(solution)/shard_map/project/pallas_call | solution.py:232
  32.7 0.3 collective-permute-done.4.behind_ref
  33.0 0.0 copy-done.3
  33.0 1.4 %attend_own.1.after.ring_own = bf16[128,512]{1,0:T(8,128)(2,1)S(1)} custom-call(bf16[272,512]{1,0:T(8,128)(2,1)S(1)} %get-tuple-element.15.base_ref, f32[128,512]{1,0:T(8,128)S(1)} %get-tuple-element.21.own_ref, bf16[384,512]{1,0:T(8,128)(2,1)S(1)} %get-tuple-element.24.query_ref, bf16[512,1024]{1,0:T(8,128)(2,1)S(1)} %get-tuple-element.25.kv_ref, ...), custom_call_target="tpu_custom_call" | custom-call | flops 671088640 | bytes 131072 | tf_op jit(solution)/shard_map/attend_own/pallas_call | solution.py:307
  34.4 1.4 %collective-permute-done.5.far_ref = bf16[256,512]{1,0:T(8,128)(2,1)S(1)} collective-permute-done((bf16[256,512]{1,0:T(8,128)(2,1)S(1)}, bf16[256,512]{1,0:T(8,128)(2,1)S(1)}, u32[]{:S(2)}, u32[]{:S(2)}) %collective-permute-start.5) | collective-permute-done | bytes 262176 | tf_op jit(solution)/shard_map/ppermute | solution.py:32
  35.8 2.0 %attend_near.1.ring_near = bf16[256,512]{1,0:T(8,128)(2,1)S(1)} custom-call(bf16[272,512]{1,0:T(8,128)(2,1)S(1)} %collective-permute-done.1.arrived_ref.sums_ref, bf16[256,512]{1,0:T(8,128)(2,1)S(1)} %collective-permute-done.3.near_ref, bf16[384,512]{1,0:T(8,128)(2,1)S(1)} %get-tuple-element.24.query_ref, bf16[512,1024]{1,0:T(8,128)(2,1)S(1)} %get-tuple-element.25.kv_ref, ...), custom_call_target="tpu_custom_call" | custom-call | flops 1342177280 | bytes 131072 | tf_op jit(solution)/shard_map/attend_near/pallas_call | solution.py:323
  37.8 0.0 copy-start.1
  37.8 0.0 copy-start.4
  37.9 0.0 copy-start.6
  37.9 0.1 collective-permute-start.7
  37.9 0.5 %collective-permute-start.6 = (bf16[128,512]{1,0:T(8,128)(2,1)S(1)}, bf16[128,512]{1,0:T(8,128)(2,1)S(1)}, u32[]{:S(2)}, u32[]{:S(2)}) collective-permute-start(bf16[128,512]{1,0:T(8,128)(2,1)S(1)} %attend_own.1.after.ring_own), channel_id=1, source_target_pairs={{0,1},{1,0},{2,3},{3,2},{4,5},{5,4},{6,7},{7,6},{8,9},{9,8},{10,11... | collective-permute-start | bytes 393224 | tf_op jit(solution)/shard_map/ppermute | solution.py:23
  38.4 1.0 %mesh_hidden.1.mesh_in = bf16[640,2048]{1,0:T(8,128)(2,1)S(1)} custom-call(bf16[128,512]{1,0:T(8,128)(2,1)S(1)} %attend_own.1.after.ring_own, bf16[256,512]{1,0:T(8,128)(2,1)S(1)} %attend_near.1.ring_near, bf16[512,2048]{1,0:T(8,128)(2,1)S(1)} %copy-done), custom_call_target="tpu_custom_call" | custom-call | flops 805306368 | bytes 131072 | tf_op jit(solution)/shard_map/mesh_hidden/pallas_call | solution.py:375
  39.4 0.0 collective-permute-done.7.back_near
  39.5 0.0 collective-permute-done.6.back_own
  39.5 4.6 %decode.1 = (bf16[1024,512]{1,0:T(8,128)(2,1)}, bf16[128,512]{1,0:T(8,128)(2,1)}, bf16[640,2048]{1,0:T(8,128)(2,1)S(1)}) custom-call(s32[8]{0:T(128)S(1)} %copy-done.6, f32[8,128]{1,0:T(8,128)S(1)} %bitcast.9, bf16[128,512]{1,0:T(8,128)(2,1)S(1)} %attend_own.1.after.ring_own, ...), custom_call_target="tpu_custom_call", output_to_operand_aliasing={{2}: (7, {})} | custom-call | flops 2147483648 | bytes 6291456 | tf_op jit(solution)/shard_map/decode/pallas_call | solution.py:435
  (10 shorter events, 0.1 us)
Async XLA Ops:
  0.6 15.3 %copy-start = (bf16[512,2048]{1,0:T(8,128)(2,1)S(1)}, bf16[512,2048]{1,0:T(8,128)(2,1)}, u32[]{:S(2)}) copy-start(bf16[512,2048]{1,0:T(8,128)(2,1)} %first.5) | copy-start | bytes 6291460
  7.7 1.5 %collective-permute-start = (bf16[144,512]{1,0:T(8,128)(2,1)S(1)}, bf16[144,512]{1,0:T(8,128)(2,1)S(1)}, u32[]{:S(2)}, u32[]{:S(2)}) collective-permute-start(bf16[144,512]{1,0:T(8,128)(2,1)S(1)} %get-tuple-element.17), channel_id=1, source_target_pairs={{0,1},{1,0},{2,3},{3,2},{4,5},{5,4},{6,7},{7,6},{8,9},{9,8},{10,11... | collective-permute-start | bytes 442376 | tf_op jit(solution)/shard_map/ppermute | solution.py:23
  9.2 11.0 %collective-permute-start.1 = (bf16[272,512]{1,0:T(8,128)(2,1)S(1)}, bf16[272,512]{1,0:T(8,128)(2,1)S(1)}, u32[]{:S(2)}, u32[]{:S(2)}) collective-permute-start(bf16[272,512]{1,0:T(8,128)(2,1)S(1)} %outgoing_sums.1.after), channel_id=1, source_target_pairs={{0,31},{1,2},{2,1},{3,4},{4,3},{5,6},{6,5},{7,8},{8,7},{9,10},{10,... | collective-permute-start | bytes 835592 | tf_op jit(solution)/shard_map/ppermute | solution.py:32
  20.2 11.5 %copy-start.2 = (bf16[1,512,1536]{2,1,0:T(8,128)(2,1)S(1)}, bf16[1,512,1536]{2,1,0:T(8,128)(2,1)}, u32[]{:S(2)}) copy-start(bf16[1,512,1536]{2,1,0:T(8,128)(2,1)} %param.24) | copy-start | bytes 4718596
  20.2 11.5 %copy-start.5 = (f32[1,512]{1,0:T(1,128)S(1)}, f32[1,512]{1,0:T(1,128)}, u32[]{:S(2)}) copy-start(f32[1,512]{1,0:T(1,128)} %gain_ref.5) | copy-start | bytes 6148
  20.3 12.7 %copy-start.3 = (bf16[1,512,512]{2,1,0:T(8,128)(2,1)S(1)}, bf16[1,512,512]{2,1,0:T(8,128)(2,1)}, u32[]{:S(2)}) copy-start(bf16[1,512,512]{2,1,0:T(8,128)(2,1)} %param.25) | copy-start | bytes 1572868
  20.3 1.6 %collective-permute-start.2 = (bf16[256,512]{1,0:T(8,128)(2,1)S(1)}, bf16[256,512]{1,0:T(8,128)(2,1)S(1)}, u32[]{:S(2)}, u32[]{:S(2)}) collective-permute-start(bf16[256,512]{1,0:T(8,128)(2,1)S(1)} %get-tuple-element.20), channel_id=1, source_target_pairs={{0,1},{1,0},{2,3},{3,2},{4,5},{5,4},{6,7},{7,6},{8,9},{9,8},{10,11... | collective-permute-start | bytes 786440 | tf_op jit(solution)/shard_map/ppermute | solution.py:23
  22.0 9.6 %collective-permute-start.3 = (bf16[256,512]{1,0:T(8,128)(2,1)S(1)}, bf16[256,512]{1,0:T(8,128)(2,1)S(1)}, u32[]{:S(2)}, u32[]{:S(2)}) collective-permute-start(bf16[256,512]{1,0:T(8,128)(2,1)S(1)} %get-tuple-element.23), channel_id=1, source_target_pairs={{0,31},{1,2},{2,1},{3,4},{4,3},{5,6},{6,5},{7,8},{8,7},{9,10},{10,... | collective-permute-start | bytes 786440 | tf_op jit(solution)/shard_map/ppermute | solution.py:32
  27.3 8.5 %collective-permute-start.5 = (bf16[256,512]{1,0:T(8,128)(2,1)S(1)}, bf16[256,512]{1,0:T(8,128)(2,1)S(1)}, u32[]{:S(2)}, u32[]{:S(2)}) collective-permute-start(bf16[256,512]{1,0:T(8,128)(2,1)S(1)} %get-tuple-element.23), channel_id=1, source_target_pairs={{0,29},{1,4},{2,31},{3,6},{4,1},{5,8},{6,3},{7,10},{8,5},{9,12},{1... | collective-permute-start | bytes 786440 | tf_op jit(solution)/shard_map/ppermute | solution.py:32
  31.6 1.4 %collective-permute-start.4 = (bf16[128,512]{1,0:T(8,128)(2,1)S(1)}, bf16[128,512]{1,0:T(8,128)(2,1)S(1)}, u32[]{:S(2)}, u32[]{:S(2)}) collective-permute-start(bf16[128,512]{1,0:T(8,128)(2,1)S(1)} %slice.8), channel_id=1, source_target_pairs={{0,1},{1,0},{2,3},{3,2},{4,5},{5,4},{6,7},{7,6},{8,9},{9,8},{10,11... | collective-permute-start | bytes 393224 | tf_op jit(solution)/shard_map/ppermute | solution.py:23
  37.8 1.6 %copy-start.1 = (bf16[2048,512]{1,0:T(8,128)(2,1)S(1)}, bf16[2048,512]{1,0:T(8,128)(2,1)}, u32[]{:S(2)}) copy-start(bf16[2048,512]{1,0:T(8,128)(2,1)} %second.1) | copy-start | bytes 6291460
  37.8 1.6 %copy-start.4 = (f32[1024]{0:T(1024)S(1)}, f32[1024]{0:T(1024)}, u32[]{:S(2)}) copy-start(f32[1024]{0:T(1024)} %param.18) | copy-start | bytes 12292
  37.9 1.6 %copy-start.6 = (s32[8]{0:T(128)S(1)}, s32[8]{0:T(128)}, u32[]{:S(2)}) copy-start(s32[8]{0:T(128)} %owner.1) | copy-start | bytes 100
  37.9 1.6 %collective-permute-start.7 = (bf16[128,512]{1,0:T(8,128)(2,1)S(1)}, bf16[128,512]{1,0:T(8,128)(2,1)S(1)}, u32[]{:S(2)}, u32[]{:S(2)}) collective-permute-start(bf16[128,512]{1,0:T(8,128)(2,1)S(1)} %slice.9), channel_id=1, source_target_pairs={{0,1},{1,0},{2,3},{3,2},{4,5},{5,4},{6,7},{7,6},{8,9},{9,8},{10,11... | collective-permute-start | bytes 393224 | tf_op jit(solution)/shard_map/ppermute | solution.py:23
  37.9 1.5 %collective-permute-start.6 = (bf16[128,512]{1,0:T(8,128)(2,1)S(1)}, bf16[128,512]{1,0:T(8,128)(2,1)S(1)}, u32[]{:S(2)}, u32[]{:S(2)}) collective-permute-start(bf16[128,512]{1,0:T(8,128)(2,1)S(1)} %attend_own.1.after.ring_own), channel_id=1, source_target_pairs={{0,1},{1,0},{2,3},{3,2},{4,5},{5,4},{6,7},{7,6},{8,9},{9,8},{10,11... | collective-permute-start | bytes 393224 | tf_op jit(solution)/shard_map/ppermute | solution.py:23

commit v6 on v5

--- a/solution.py
+++ b/solution.py
@@ -245,23 +245,26 @@
 
 def attention(query, window, keep):
     depth = query.shape[1]
-    heads = []
-    for h in range(depth // HD):
-        cols = slice(h * HD, (h + 1) * HD)
-        value_cols = slice(depth + h * HD, depth + (h + 1) * HD)
-        scores = jnp.concatenate([
+    every = [slice(h * HD, (h + 1) * HD) for h in range(depth // HD)]
+    scores = [
+        jnp.concatenate([
             lax.dot_general(
                 query[:, cols], ref[first:first + size, cols], (((1,), (1,)), ((), ())), preferred_element_type=F32
             )
             for ref, first, size in window
         ], axis=1)
-        scores = jnp.where(keep, scores, -jnp.inf)
-        below = (scores - jnp.max(scores, axis=-1, keepdims=True)) * (HD ** -0.5)
-        grown = jnp.exp(below.astype(BF16))
+        for cols in every
+    ]
+    scores = [jnp.where(keep, score, -jnp.inf) for score in scores]
+    below = [(score - jnp.max(score, axis=-1, keepdims=True)) * (HD ** -0.5) for score in scores]
+    grown = [jnp.exp(score.astype(BF16)) for score in below]
+    heads = []
+    for h, cols in enumerate(every):
         start, taken = 0, None
         for ref, first, size in window:
-            value = jnp.concatenate([ref[first:first + size, value_cols], jnp.ones((size, HD), BF16)], axis=1)
-            term = jnp.dot(grown[:, start:start + size], value, preferred_element_type=F32)
+            value = ref[first:first + size, depth + cols.start:depth + cols.stop]
+            value = jnp.concatenate([value, jnp.ones((size, HD), BF16)], axis=1)
+            term = jnp.dot(grown[h][:, start:start + size], value, preferred_element_type=F32)
             taken = term if taken is None else taken + term
             start += size
         heads.append((taken[:, :HD] / taken[:, HD:]).astype(BF16))
@@ -364,31 +367,32 @@
     )(encoded, first, after)
 
 
-def mesh_hidden_kernel(ring_own, ring_near, first, out_ref):
+def mesh_hidden_kernel(back_own, ring_own, ring_near, first, out_ref):
     rows = ring_own.shape[0]
+    out_ref[rows:REACH * rows, :] = halved(back_own[...], first[...]).astype(BF16)
     out_ref[REACH * rows:(REACH + 1) * rows, :] = halved(ring_own[...], first[...]).astype(BF16)
     out_ref[(REACH + 1) * rows:, :] = halved(ring_near[...], first[...]).astype(BF16)
 
 
-def mesh_hidden(ring_own, ring_near, first):
+def mesh_hidden(back_own, ring_own, ring_near, first):
     rows, depth = ring_own.shape
     return pl.pallas_call(
         mesh_hidden_kernel,
         out_shape=kept(((2 * REACH + 1) * rows, first.shape[1])),
-        in_specs=[VMEM] * 3,
+        in_specs=[VMEM] * 4,
         out_specs=VMEM,
         compiler_params=pltpu.CompilerParams(vmem_limit_bytes=12 << 20),
         cost_estimate=pl.CostEstimate(
-            flops=6 * rows * depth * first.shape[1], bytes_accessed=2 * rows * depth, transcendentals=0
+            flops=8 * rows * depth * first.shape[1], bytes_accessed=2 * rows * depth, transcendentals=0
         ),
         name="mesh_hidden",
-    )(ring_own, ring_near, first)
+    )(back_own, ring_own, ring_near, first)
 
 
 def decode_kernel(
-    owner, weight_ref, ring_own, ring_near, back_own, back_near, grid_ref, mesh_in, enc_ref, first, second,
+    owner_hbm, weight_ref, ring_own, ring_near, back_own, back_near, grid_ref, mesh_in, enc_ref, first, second,
     out_hbm, mesh_hbm, mesh_ref,
-    x_ref, act, ring, io_sems,
+    owner, x_ref, act, ring, io_sems,
 ):
     del mesh_in
     rows = ring_own.shape[0]
@@ -396,16 +400,18 @@
     tile = min(tile, 256)
     tiles, parts = x_ref.shape[0] // tile, first.shape[1] // part
     stores = [pltpu.make_async_copy(ring_own, mesh_hbm, io_sems.at[tiles])]
+    index = pltpu.make_async_copy(owner_hbm, owner, io_sems.at[tiles + 1])
+    index.start()
     stores[0].start()
     mine, count = lax.axis_index(AXES), lax.axis_size(AXES)
     outward = outward_of()
     mesh_ref[:rows, :] = halved(back_near[...], first[...]).astype(BF16)
-    mesh_ref[rows:2 * rows, :] = halved(back_own[...], first[...]).astype(BF16)
     ring[:rows, :] = back_near[...]
     ring[rows:2 * rows, :] = back_own[...]
     ring[2 * rows:3 * rows, :] = ring_own[...]
     ring[3 * rows:, :] = ring_near[...]
     columns = jnp.transpose(weight_ref[...])
+    index.wait()
     for r in range(tiles):
         cut = slice(r * tile, (r + 1) * tile)
         for b in range(r * tile // rows, (r + 1) * tile // rows):
@@ -439,21 +445,22 @@
             jax.ShapeDtypeStruct((rows, depth), BF16),
             kept(mesh_part.shape),
         ),
-        in_specs=[SMEM] + [VMEM] * 10,
+        in_specs=[ANY] + [VMEM] * 10,
         out_specs=(ANY, ANY, VMEM),
         input_output_aliases={7: 2},
         scratch_shapes=[
+            pltpu.SMEM(owner.shape, jnp.int32),
             pltpu.VMEM((cells, depth), BF16),
             pltpu.VMEM((cells, hidden), BF16),
             pltpu.VMEM(((2 * REACH + 1) * rows, depth), BF16),
-            pltpu.SemaphoreType.DMA((cells // min(cells, 256) + 1,)),
+            pltpu.SemaphoreType.DMA((cells // min(cells, 256) + 2,)),
         ],
         compiler_params=pltpu.CompilerParams(vmem_limit_bytes=16 << 20),
         cost_estimate=pl.CostEstimate(
             flops=2 * cells * depth * hidden, bytes_accessed=4 * (cells + hidden) * depth, transcendentals=cells * hidden
         ),
         name="decode",
-    )(owner, weights, ring_own, ring_near, back_own, back_near, grid_part, mesh_part, encoded, first, second)[:2]
+    )(*in_hbm(owner), weights, ring_own, ring_near, back_own, back_near, grid_part, mesh_part, encoded, first, second)[:2]
 
 
 def on_device(
@@ -478,7 +485,7 @@
     ring_near = attend_near(sums, near, query, kv, far, attn_gain, w_qkv[0], w_out[0], ring_own)
     back_own = swapped(ring_own)
     back_near = swapped(ring_near[:rows])
-    mesh_part = mesh_hidden(ring_own, ring_near, dec_w1)
+    mesh_part = mesh_hidden(back_own, ring_own, ring_near, dec_w1)
     return decode(
         m2g_owner, m2g_weight.reshape(nblocks, rows), ring_own, ring_near, back_own, back_near,
         grid_part, mesh_part, encoded, dec_w1, dec_w2,

time: 44.2 us -> 43.7 us (0.989)
  transfers between devices with their start and end apart: 8 -> 8, of which waited for: 6 -> 6; matrix products, arithmetic and copies ran while one was open for 0% -> 0% of each run, Pallas kernels for 13% -> 18%
where the time goes in v6:
time: 43.7 us; the launch traced here: 43.5 us
  Pallas kernels  19.2 us (44%)
  starting transfers between devices  13.2 us (30%)
  waiting for transfers between devices  10.1 us (23%)
  between operations  0.78 us (2%)
    ppermute x3, starting transfers between devices, from_outward(): return lax.ppermute(block, AXES, route)  12.3 us
    ppermute x3, waiting for transfers between devices, from_outward(): return lax.ppermute(block, AXES, route)  7.25 us
    pallas_call x1, Pallas kernels, encode(): pl.pallas_call(encode_kernel, out_shape=(kept((cells, depth)), kept((rows...  7.01 us
    pallas_call x1, Pallas kernels, decode(): pl.pallas_call(decode_kernel, out_shape=(jax.ShapeDtypeStruct((cells, dep...  4.19 us
    ppermute x5, waiting for transfers between devices, swapped(): return lax.ppermute(block, AXES, [(i, i ^ 1) for i in range(count)])  2.89 us
    pallas_call x1, Pallas kernels, grid_hidden(): pl.pallas_call(grid_hidden_kernel, out_shape=kept((cells, hidden)), in_sp...  2.35 us
    pallas_call x1, Pallas kernels, attend_near(): pl.pallas_call(attend_near_kernel, out_shape=kept((2 * rows, depth)), in_...  1.9 us
    pallas_call x1, Pallas kernels, mesh_hidden(): pl.pallas_call(mesh_hidden_kernel, out_shape=kept(((2 * REACH + 1) * rows...  1.28 us
  transfers between devices with their start and end apart: 8, of which 6 were waited for; matrix products, arithmetic and copies ran while one was open for 0% of the time, Pallas kernels for 18%

profile of v6, /device:TPU:0, one launch (start us, length us, event | category | flops | bytes accessed | tf_op | source)
XLA Modules:
  0.0 43.5 jit_solution(14435420901148454847)
XLA Ops:
  0.6 0.0 copy-start
  0.6 7.0 %encode.1 = (bf16[1024,512]{1,0:T(8,128)(2,1)S(1)}, bf16[144,512]{1,0:T(8,128)(2,1)S(1)}, bf16[272,512]{1,0:T(8,128)(2,1)S(1)}, f32[256,512]{1,0:T(8,128)S(1)}) custom-call(s32[8]{0:T(128)} %owner_hbm.2, s32[1,3]{1,0:T(1,128)} %listed_hbm.1, f32[8,128]{1,0:T(8,128)} %bitcast.10, bf16[128,512]{1,0:T(8,128)(2,1)} %feat_hbm.1, bf16[1024,512]{1,0:T(8,128)(2,1)} %x_hbm.1, ...), custom_call_target="tpu_custom_call" | custom-call | flops 4294967296 | bytes 6291456 | tf_op jit(solution)/shard_map/encode/pallas_call | solution.py:132
  7.7 0.5 %collective-permute-start = (bf16[144,512]{1,0:T(8,128)(2,1)S(1)}, bf16[144,512]{1,0:T(8,128)(2,1)S(1)}, u32[]{:S(2)}, u32[]{:S(2)}) collective-permute-start(bf16[144,512]{1,0:T(8,128)(2,1)S(1)} %get-tuple-element.17), channel_id=1, source_target_pairs={{0,1},{1,0},{2,3},{3,2},{4,5},{5,4},{6,7},{7,6},{8,9},{9,8},{10,11... | collective-permute-start | bytes 442376 | tf_op jit(solution)/shard_map/ppermute | solution.py:23
  8.2 1.0 %collective-permute-done.arrived_ref = bf16[144,512]{1,0:T(8,128)(2,1)S(1)} collective-permute-done((bf16[144,512]{1,0:T(8,128)(2,1)S(1)}, bf16[144,512]{1,0:T(8,128)(2,1)S(1)}, u32[]{:S(2)}, u32[]{:S(2)}) %collective-permute-start) | collective-permute-done | bytes 147488 | tf_op jit(solution)/shard_map/ppermute | solution.py:23
  9.2 6.7 %collective-permute-start.1 = (bf16[272,512]{1,0:T(8,128)(2,1)S(1)}, bf16[272,512]{1,0:T(8,128)(2,1)S(1)}, u32[]{:S(2)}, u32[]{:S(2)}) collective-permute-start(bf16[272,512]{1,0:T(8,128)(2,1)S(1)} %outgoing_sums.1.after), channel_id=1, source_target_pairs={{0,31},{1,2},{2,1},{3,4},{4,3},{5,6},{6,5},{7,8},{8,7},{9,10},{10,... | collective-permute-start | bytes 835592 | tf_op jit(solution)/shard_map/ppermute | solution.py:32
  15.9 0.0 copy-done
  15.9 2.3 %grid_hidden.1.after.grid_ref = bf16[1024,2048]{1,0:T(8,128)(2,1)S(1)} custom-call(bf16[1024,512]{1,0:T(8,128)(2,1)S(1)} %get-tuple-element.18.enc_ref, bf16[512,2048]{1,0:T(8,128)(2,1)S(1)} %copy-done, bf16[272,512]{1,0:T(8,128)(2,1)S(1)} %outgoing_sums.1.after), custom_call_target="tpu_custom_call" | custom-call | flops 2147483648 | bytes 3145728 | tf_op jit(solution)/shard_map/grid_hidden/pallas_call | solution.py:357
  18.3 2.0 %collective-permute-done.1.arrived_ref.sums_ref = bf16[272,512]{1,0:T(8,128)(2,1)S(1)} collective-permute-done((bf16[272,512]{1,0:T(8,128)(2,1)S(1)}, bf16[272,512]{1,0:T(8,128)(2,1)S(1)}, u32[]{:S(2)}, u32[]{:S(2)}) %collective-permute-start.1) | collective-permute-done | bytes 278560 | tf_op jit(solution)/shard_map/ppermute | solution.py:32
  20.2 0.1 chip_share.1
  20.3 0.0 copy-start.3
  20.4 0.1 collective-permute-start.2
  20.4 1.5 %collective-permute-done.2.other_ref = bf16[256,512]{1,0:T(8,128)(2,1)S(1)} collective-permute-done((bf16[256,512]{1,0:T(8,128)(2,1)S(1)}, bf16[256,512]{1,0:T(8,128)(2,1)S(1)}, u32[]{:S(2)}, u32[]{:S(2)}) %collective-permute-start.2) | collective-permute-done | bytes 262176 | tf_op jit(solution)/shard_map/ppermute | solution.py:23
  22.0 0.1 chip_states.1
  22.1 5.3 %collective-permute-start.3 = (bf16[256,512]{1,0:T(8,128)(2,1)S(1)}, bf16[256,512]{1,0:T(8,128)(2,1)S(1)}, u32[]{:S(2)}, u32[]{:S(2)}) collective-permute-start(bf16[256,512]{1,0:T(8,128)(2,1)S(1)} %get-tuple-element.23), channel_id=1, source_target_pairs={{0,31},{1,2},{2,1},{3,4},{4,3},{5,6},{6,5},{7,8},{8,7},{9,10},{10,... | collective-permute-start | bytes 786440 | tf_op jit(solution)/shard_map/ppermute | solution.py:32
  27.3 0.3 collective-permute-start.5
  27.6 4.0 %collective-permute-done.3.near_ref = bf16[256,512]{1,0:T(8,128)(2,1)S(1)} collective-permute-done((bf16[256,512]{1,0:T(8,128)(2,1)S(1)}, bf16[256,512]{1,0:T(8,128)(2,1)S(1)}, u32[]{:S(2)}, u32[]{:S(2)}) %collective-permute-start.3) | collective-permute-done | bytes 262176 | tf_op jit(solution)/shard_map/ppermute | solution.py:32
  31.6 0.1 collective-permute-start.4
  31.7 1.0 %project.1 = (bf16[384,512]{1,0:T(8,128)(2,1)S(1)}, bf16[512,1024]{1,0:T(8,128)(2,1)S(1)}) custom-call(bf16[256,512]{1,0:T(8,128)(2,1)S(1)} %get-tuple-element.22.pair_ref, bf16[256,512]{1,0:T(8,128)(2,1)S(1)} %collective-permute-done.3.near_ref, f32[1,512]{1,0:T(1,128)S(1)} %copy-done.5, bf16[512,1536]{1,0:T(8,128)(2,1)S(1)} %bitcast.4), custom_call_target="tpu_custom_call" | custom-call | flops 738197504 | bytes 131072 | tf_op jit(solution)/shard_map/project/pallas_call | solution.py:232
  32.7 0.3 collective-permute-done.4.behind_ref
  33.0 0.0 copy-done.3
  33.0 1.2 %attend_own.1.after.ring_own = bf16[128,512]{1,0:T(8,128)(2,1)S(1)} custom-call(bf16[272,512]{1,0:T(8,128)(2,1)S(1)} %get-tuple-element.15.base_ref, f32[128,512]{1,0:T(8,128)S(1)} %get-tuple-element.21.own_ref, bf16[384,512]{1,0:T(8,128)(2,1)S(1)} %get-tuple-element.24.query_ref, bf16[512,1024]{1,0:T(8,128)(2,1)S(1)} %get-tuple-element.25.kv_ref, ...), custom_call_target="tpu_custom_call" | custom-call | flops 671088640 | bytes 131072 | tf_op jit(solution)/shard_map/attend_own/pallas_call | solution.py:310
  34.3 0.3 collective-permute-start.6
  34.5 1.3 %collective-permute-done.5.far_ref = bf16[256,512]{1,0:T(8,128)(2,1)S(1)} collective-permute-done((bf16[256,512]{1,0:T(8,128)(2,1)S(1)}, bf16[256,512]{1,0:T(8,128)(2,1)S(1)}, u32[]{:S(2)}, u32[]{:S(2)}) %collective-permute-start.5) | collective-permute-done | bytes 262176 | tf_op jit(solution)/shard_map/ppermute | solution.py:32
  35.8 1.9 %attend_near.1.ring_near = bf16[256,512]{1,0:T(8,128)(2,1)S(1)} custom-call(bf16[272,512]{1,0:T(8,128)(2,1)S(1)} %collective-permute-done.1.arrived_ref.sums_ref, bf16[256,512]{1,0:T(8,128)(2,1)S(1)} %collective-permute-done.3.near_ref, bf16[384,512]{1,0:T(8,128)(2,1)S(1)} %get-tuple-element.24.query_ref, bf16[512,1024]{1,0:T(8,128)(2,1)S(1)} %get-tuple-element.25.kv_ref, ...), custom_call_target="tpu_custom_call" | custom-call | flops 1342177280 | bytes 131072 | tf_op jit(solution)/shard_map/attend_near/pallas_call | solution.py:326
  37.8 0.0 copy-start.1
  37.8 0.0 copy-start.4
  37.8 0.1 collective-permute-start.7
  37.9 0.0 collective-permute-done.6.back_own
  37.9 1.3 %mesh_hidden.1.mesh_in = bf16[640,2048]{1,0:T(8,128)(2,1)S(1)} custom-call(bf16[128,512]{1,0:T(8,128)(2,1)S(1)} %collective-permute-done.6.back_own, bf16[128,512]{1,0:T(8,128)(2,1)S(1)} %attend_own.1.after.ring_own, bf16[256,512]{1,0:T(8,128)(2,1)S(1)} %attend_near.1.ring_near, bf16[512,2048]{1,0:T(8,128)(2,1)S(1)} %copy-done), custom_call_target="tpu_custom_call" | custom-call | flops 1073741824 | bytes 131072 | tf_op jit(solution)/shard_map/mesh_hidden/pallas_call | solution.py:379
  39.2 0.0 collective-permute-done.7.back_near
  39.2 0.2 copy-done.1
  39.4 4.2 %decode.1 = (bf16[1024,512]{1,0:T(8,128)(2,1)}, bf16[128,512]{1,0:T(8,128)(2,1)}, bf16[640,2048]{1,0:T(8,128)(2,1)S(1)}) custom-call(s32[8]{0:T(128)} %owner_hbm.3, f32[8,128]{1,0:T(8,128)S(1)} %bitcast.9, bf16[128,512]{1,0:T(8,128)(2,1)S(1)} %attend_own.1.after.ring_own, ...), custom_call_target="tpu_custom_call", output_to_operand_aliasing={{2}: (7, {})} | custom-call | flops 2147483648 | bytes 6291456 | tf_op jit(solution)/shard_map/decode/pallas_call | solution.py:441
  (8 shorter events, 0.1 us)
Async XLA Ops:
  0.6 15.3 %copy-start = (bf16[512,2048]{1,0:T(8,128)(2,1)S(1)}, bf16[512,2048]{1,0:T(8,128)(2,1)}, u32[]{:S(2)}) copy-start(bf16[512,2048]{1,0:T(8,128)(2,1)} %first.5) | copy-start | bytes 6291460
  7.7 1.5 %collective-permute-start = (bf16[144,512]{1,0:T(8,128)(2,1)S(1)}, bf16[144,512]{1,0:T(8,128)(2,1)S(1)}, u32[]{:S(2)}, u32[]{:S(2)}) collective-permute-start(bf16[144,512]{1,0:T(8,128)(2,1)S(1)} %get-tuple-element.17), channel_id=1, source_target_pairs={{0,1},{1,0},{2,3},{3,2},{4,5},{5,4},{6,7},{7,6},{8,9},{9,8},{10,11... | collective-permute-start | bytes 442376 | tf_op jit(solution)/shard_map/ppermute | solution.py:23
  9.2 11.0 %collective-permute-start.1 = (bf16[272,512]{1,0:T(8,128)(2,1)S(1)}, bf16[272,512]{1,0:T(8,128)(2,1)S(1)}, u32[]{:S(2)}, u32[]{:S(2)}) collective-permute-start(bf16[272,512]{1,0:T(8,128)(2,1)S(1)} %outgoing_sums.1.after), channel_id=1, source_target_pairs={{0,31},{1,2},{2,1},{3,4},{4,3},{5,6},{6,5},{7,8},{8,7},{9,10},{10,... | collective-permute-start | bytes 835592 | tf_op jit(solution)/shard_map/ppermute | solution.py:32
  20.2 11.5 %copy-start.2 = (bf16[1,512,1536]{2,1,0:T(8,128)(2,1)S(1)}, bf16[1,512,1536]{2,1,0:T(8,128)(2,1)}, u32[]{:S(2)}) copy-start(bf16[1,512,1536]{2,1,0:T(8,128)(2,1)} %param.24) | copy-start | bytes 4718596
  20.2 11.5 %copy-start.5 = (f32[1,512]{1,0:T(1,128)S(1)}, f32[1,512]{1,0:T(1,128)}, u32[]{:S(2)}) copy-start(f32[1,512]{1,0:T(1,128)} %gain_ref.5) | copy-start | bytes 6148
  20.3 12.7 %copy-start.3 = (bf16[1,512,512]{2,1,0:T(8,128)(2,1)S(1)}, bf16[1,512,512]{2,1,0:T(8,128)(2,1)}, u32[]{:S(2)}) copy-start(bf16[1,512,512]{2,1,0:T(8,128)(2,1)} %param.25) | copy-start | bytes 1572868
  20.4 1.6 %collective-permute-start.2 = (bf16[256,512]{1,0:T(8,128)(2,1)S(1)}, bf16[256,512]{1,0:T(8,128)(2,1)S(1)}, u32[]{:S(2)}, u32[]{:S(2)}) collective-permute-start(bf16[256,512]{1,0:T(8,128)(2,1)S(1)} %get-tuple-element.20), channel_id=1, source_target_pairs={{0,1},{1,0},{2,3},{3,2},{4,5},{5,4},{6,7},{7,6},{8,9},{9,8},{10,11... | collective-permute-start | bytes 786440 | tf_op jit(solution)/shard_map/ppermute | solution.py:23
  22.1 9.6 %collective-permute-start.3 = (bf16[256,512]{1,0:T(8,128)(2,1)S(1)}, bf16[256,512]{1,0:T(8,128)(2,1)S(1)}, u32[]{:S(2)}, u32[]{:S(2)}) collective-permute-start(bf16[256,512]{1,0:T(8,128)(2,1)S(1)} %get-tuple-element.23), channel_id=1, source_target_pairs={{0,31},{1,2},{2,1},{3,4},{4,3},{5,6},{6,5},{7,8},{8,7},{9,10},{10,... | collective-permute-start | bytes 786440 | tf_op jit(solution)/shard_map/ppermute | solution.py:32
  27.3 8.5 %collective-permute-start.5 = (bf16[256,512]{1,0:T(8,128)(2,1)S(1)}, bf16[256,512]{1,0:T(8,128)(2,1)S(1)}, u32[]{:S(2)}, u32[]{:S(2)}) collective-permute-start(bf16[256,512]{1,0:T(8,128)(2,1)S(1)} %get-tuple-element.23), channel_id=1, source_target_pairs={{0,29},{1,4},{2,31},{3,6},{4,1},{5,8},{6,3},{7,10},{8,5},{9,12},{1... | collective-permute-start | bytes 786440 | tf_op jit(solution)/shard_map/ppermute | solution.py:32
  31.6 1.4 %collective-permute-start.4 = (bf16[128,512]{1,0:T(8,128)(2,1)S(1)}, bf16[128,512]{1,0:T(8,128)(2,1)S(1)}, u32[]{:S(2)}, u32[]{:S(2)}) collective-permute-start(bf16[128,512]{1,0:T(8,128)(2,1)S(1)} %slice.8), channel_id=1, source_target_pairs={{0,1},{1,0},{2,3},{3,2},{4,5},{5,4},{6,7},{7,6},{8,9},{9,8},{10,11... | collective-permute-start | bytes 393224 | tf_op jit(solution)/shard_map/ppermute | solution.py:23
  34.3 3.6 %collective-permute-start.6 = (bf16[128,512]{1,0:T(8,128)(2,1)S(1)}, bf16[128,512]{1,0:T(8,128)(2,1)S(1)}, u32[]{:S(2)}, u32[]{:S(2)}) collective-permute-start(bf16[128,512]{1,0:T(8,128)(2,1)S(1)} %attend_own.1.after.ring_own), channel_id=1, source_target_pairs={{0,1},{1,0},{2,3},{3,2},{4,5},{5,4},{6,7},{7,6},{8,9},{9,8},{10,11... | collective-permute-start | bytes 393224 | tf_op jit(solution)/shard_map/ppermute | solution.py:23
  37.8 1.6 %copy-start.1 = (bf16[2048,512]{1,0:T(8,128)(2,1)S(1)}, bf16[2048,512]{1,0:T(8,128)(2,1)}, u32[]{:S(2)}) copy-start(bf16[2048,512]{1,0:T(8,128)(2,1)} %second.1) | copy-start | bytes 6291460
  37.8 1.6 %copy-start.4 = (f32[1024]{0:T(1024)S(1)}, f32[1024]{0:T(1024)}, u32[]{:S(2)}) copy-start(f32[1024]{0:T(1024)} %param.18) | copy-start | bytes 12292
  37.8 1.4 %collective-permute-start.7 = (bf16[128,512]{1,0:T(8,128)(2,1)S(1)}, bf16[128,512]{1,0:T(8,128)(2,1)S(1)}, u32[]{:S(2)}, u32[]{:S(2)}) collective-permute-start(bf16[128,512]{1,0:T(8,128)(2,1)S(1)} %slice.9), channel_id=1, source_target_pairs={{0,1},{1,0},{2,3},{3,2},{4,5},{5,4},{6,7},{7,6},{8,9},{9,8},{10,11... | collective-permute-start | bytes 393224 | tf_op jit(solution)/shard_map/ppermute | solution.py:23

commit v7 on v6

--- a/solution.py
+++ b/solution.py
@@ -33,7 +33,7 @@
 
 
 def tiles_of(rows, columns):
-    return min(rows, 512), min(columns, 1024)
+    return min(rows, 1024), min(columns, 1024)
 
 
 def outward_of():
@@ -65,8 +65,8 @@
 
 
 def encode_kernel(
-    owner_hbm, listed_hbm, weight_hbm, feat_hbm, x_hbm, first_hbm, second_hbm,
-    enc_ref, msg_ref, base_ref, loc_ref,
+    owner_hbm, listed_hbm, weight_hbm, feat_hbm, x_hbm, first_hbm, second_hbm, next_hbm,
+    enc_ref, msg_ref, base_ref, loc_ref, next_ref,
     owner, listed, weight_ref, feat_ref, first, second, act, total, sems, io_sems,
 ):
     rows, depth = feat_ref.shape
@@ -87,32 +87,36 @@
         pltpu.make_async_copy(owner_hbm, owner, io_sems.at[tiles + 2]),
         pltpu.make_async_copy(listed_hbm, listed, io_sems.at[tiles + 3]),
     ]
-    for copy in loads + ones:
+    later = pltpu.make_async_copy(next_hbm, next_ref, io_sems.at[tiles + 4])
+    for copy in loads + ones + twos + small + [later]:
         copy.start()
 
     def arrive(r):
         if r == 0:
             for copy in loads:
                 copy.wait()
-            for copy in twos + small:
-                copy.start()
 
     mine, count = lax.axis_index(AXES), lax.axis_size(AXES)
     outward = outward_of()
     total[...] = jnp.zeros_like(total)
-    hidden_layer(enc_ref, first, act, tile, part, arrive, lambda j: ones[j].wait())
-    for copy in twos + small:
-        copy.wait()
+
+    def before(j):
+        due = ones[:1] if j == 0 else []
+        if j == min(1, parts - 1):
+            due = due + ones[1:] + twos + small
+        for copy in due:
+            copy.wait()
+
+    hidden_layer(enc_ref, first, act, tile, part, arrive, before)
     columns = jnp.transpose(weight_ref[...])
     tile = min(tile, 256)
     for r in range(enc_ref.shape[0] // tile):
         cut = slice(r * tile, (r + 1) * tile)
-        out = jnp.dot(act[cut, :], second[...], preferred_element_type=F32)
-        enc_ref[cut, :] = (enc_ref[cut, :].astype(F32) + out).astype(BF16)
+        out = enc_ref[cut, :].astype(F32) + jnp.dot(act[cut, :], second[...], preferred_element_type=F32)
+        enc_ref[cut, :] = out.astype(BF16)
         for b in range(r * tile // rows, (r + 1) * tile // rows):
             slot = outward * offset_of(owner[b], mine, count) + REACH
-            block = enc_ref[b * rows:(b + 1) * rows, :].astype(F32)
-            total[slot] += columns[:, b:b + 1] * block
+            total[slot] += columns[:, b:b + 1] * out[b * rows - r * tile:(b + 1) * rows - r * tile, :]
     absent = sum(-offset_of(listed[0, n], mine, count) for n in range(listed.shape[1])).astype(F32)
     spot = lax.broadcasted_iota(jnp.int32, (EXTRA, depth), 1)
     msg_ref[:rows, :] = total[0].astype(BF16)
@@ -122,9 +126,10 @@
     base_ref[2 * rows:, :] = jnp.where(spot == 0, absent, 0.0).astype(BF16)
     loc_ref[:rows, :] = total[1]
     loc_ref[rows:, :] = total[2] + feat_ref[...].astype(F32)
-
-
-def encode(owner, listed, weights, feat, grid, first, second):
+    later.wait()
+
+
+def encode(owner, listed, weights, feat, grid, first, second, following):
     cells, depth = grid.shape
     hidden = first.shape[1]
     rows = feat.shape[0]
@@ -136,9 +141,10 @@
             kept((rows + EXTRA, depth)),
             kept((2 * rows + EXTRA, depth)),
             kept((2 * rows, depth), F32),
-        ),
-        in_specs=[ANY] * 7,
-        out_specs=(VMEM,) * 4,
+            kept(following.shape),
+        ),
+        in_specs=[ANY] * 8,
+        out_specs=(VMEM,) * 5,
         scratch_shapes=[
             pltpu.SMEM(owner.shape, jnp.int32),
             pltpu.SMEM(listed.shape, jnp.int32),
@@ -149,14 +155,14 @@
             pltpu.VMEM((cells, hidden), BF16),
             pltpu.VMEM((2 * REACH + 1, rows, depth), F32),
             pltpu.SemaphoreType.DMA((2, hidden // part)),
-            pltpu.SemaphoreType.DMA((cells // tile + 4,)),
+            pltpu.SemaphoreType.DMA((cells // tile + 5,)),
         ],
         compiler_params=pltpu.CompilerParams(vmem_limit_bytes=24 << 20),
         cost_estimate=pl.CostEstimate(
             flops=4 * cells * depth * hidden, bytes_accessed=4 * (cells + hidden) * depth, transcendentals=cells * hidden
         ),
         name="encode",
-    )(*in_hbm(owner, listed, weights, feat, grid, first, second))
+    )(*in_hbm(owner, listed, weights, feat, grid, first, second, following))
 
 
 def outgoing_kernel(base_ref, arrived_ref, out_ref):
@@ -273,7 +279,7 @@
 
 def kept_lanes(rows, absent):
     block = (lax.broadcasted_iota(jnp.int32, (rows, (2 * REACH + 1) * rows), 1) // rows).astype(F32)
-    return block != outward_of().astype(F32) * absent.astype(F32) + REACH
+    return block != outward_of().astype(F32) * absent + REACH
 
 
 def attend_own_kernel(base_ref, own_ref, query_ref, kv_ref, behind_ref, gain_ref, w_qkv, w_out, ring_ref, kv_behind):
@@ -281,7 +287,7 @@
     kv_behind[...] = jnp.dot(
         normal(behind_ref[...], gain_ref[...]), w_qkv[:, depth:], preferred_element_type=F32
     ).astype(BF16)
-    keep = kept_lanes(rows, base_ref[2 * rows:2 * rows + 1, 0:1])
+    keep = kept_lanes(rows, base_ref[2 * rows:, 0:HD].astype(F32)[0:1, 0:1])
     mixed = attention(query_ref[:rows, :], [(kv_behind, 0, rows), (kv_ref, 0, 4 * rows)], keep)
     ring_ref[...] = (own_ref[...] + jnp.dot(mixed, w_out[...], preferred_element_type=F32)).astype(BF16)
 
@@ -299,7 +305,7 @@
         [(kv_ref, rows, 3 * rows), (kv_far, 0, 2 * rows)],
     ]
     for n, window in enumerate(windows):
-        keep = kept_lanes(rows, sums_ref[2 * rows:2 * rows + 1, n:n + 1])
+        keep = kept_lanes(rows, sums_ref[2 * rows:, 0:HD].astype(F32)[0:1, n:n + 1])
         mixed[n * rows:(n + 1) * rows, :] = attention(query_ref[(n + 1) * rows:(n + 2) * rows, :], window, keep)
     added = jnp.dot(mixed[...], w_out[...], preferred_element_type=F32)
     ring_ref[...] = (near_ref[...].astype(F32) + added).astype(BF16)
@@ -341,30 +347,34 @@
     return jnp.dot(rows * BF16(0.5), first, preferred_element_type=F32)
 
 
-def grid_hidden_kernel(enc_ref, first, after, out_ref):
+def grid_hidden_kernel(enc_ref, first, second_hbm, after, out_ref, second, sem):
     del after
+    copy = pltpu.make_async_copy(second_hbm, second, sem)
+    copy.start()
     tile, part = tiles_of(*out_ref.shape)
     for j in range(out_ref.shape[1] // part):
         cols = slice(j * part, (j + 1) * part)
         for r in range(out_ref.shape[0] // tile):
             cut = slice(r * tile, (r + 1) * tile)
             out_ref[cut, cols] = halved(enc_ref[cut, :], first[:, cols]).astype(BF16)
-
-
-def grid_hidden(encoded, first, after):
+    copy.wait()
+
+
+def grid_hidden(encoded, first, second, after):
     cells, depth = encoded.shape
     hidden = first.shape[1]
     return pl.pallas_call(
         grid_hidden_kernel,
-        out_shape=kept((cells, hidden)),
-        in_specs=[VMEM] * 2 + [ANY],
-        out_specs=VMEM,
+        out_shape=(kept((cells, hidden)), kept(second.shape)),
+        in_specs=[VMEM] * 2 + [ANY] * 2,
+        out_specs=(VMEM, VMEM),
+        scratch_shapes=[pltpu.SemaphoreType.DMA],
         compiler_params=pltpu.CompilerParams(vmem_limit_bytes=12 << 20),
         cost_estimate=pl.CostEstimate(
             flops=2 * cells * depth * hidden, bytes_accessed=2 * (cells + hidden) * depth, transcendentals=0
         ),
         name="grid_hidden",
-    )(encoded, first, after)
+    )(encoded, first, *in_hbm(second), after)
 
 
 def mesh_hidden_kernel(back_own, ring_own, ring_near, first, out_ref):
@@ -469,12 +479,12 @@
 ):
     rows = mesh_feat.shape[0]
     nblocks = g2m_owner.shape[0]
-    encoded, message, base, local = encode(
-        g2m_owner, neighbours, g2m_weight.reshape(nblocks, rows), mesh_feat, grid, enc_w1, enc_w2
+    encoded, message, base, local, first = encode(
+        g2m_owner, neighbours, g2m_weight.reshape(nblocks, rows), mesh_feat, grid, enc_w1, enc_w2, dec_w1
     )
     outgoing = outgoing_sums(base, swapped(message))
     sums = from_outward(outgoing, 1)
-    grid_part = grid_hidden(encoded, dec_w1, outgoing)
+    grid_part, second = grid_hidden(encoded, first, dec_w2, outgoing)
     share, message = chip_share(local, sums, grid_part)
     own, pair, message = chip_states(share, swapped(message))
     near = from_outward(message, 1)
@@ -485,10 +495,10 @@
     ring_near = attend_near(sums, near, query, kv, far, attn_gain, w_qkv[0], w_out[0], ring_own)
     back_own = swapped(ring_own)
     back_near = swapped(ring_near[:rows])
-    mesh_part = mesh_hidden(back_own, ring_own, ring_near, dec_w1)
+    mesh_part = mesh_hidden(back_own, ring_own, ring_near, first)
     return decode(
         m2g_owner, m2g_weight.reshape(nblocks, rows), ring_own, ring_near, back_own, back_near,
-        grid_part, mesh_part, encoded, dec_w1, dec_w2,
+        grid_part, mesh_part, encoded, first, second,
     )
 
 

time: 43.7 us -> 43 us (0.984)
  Pallas kernels: 19.2 us -> 18.7 us
where the time goes in v7:
time: 43 us; the launch traced here: 42.9 us
  Pallas kernels  18.7 us (43%)
  starting transfers between devices  13.2 us (31%)
  waiting for transfers between devices  10.1 us (23%)
  between operations  0.77 us (2%)
    ppermute x3, starting transfers between devices, from_outward(): return lax.ppermute(block, AXES, route)  12.3 us
    ppermute x3, waiting for transfers between devices, from_outward(): return lax.ppermute(block, AXES, route)  7.24 us
    pallas_call x1, Pallas kernels, encode(): pl.pallas_call(encode_kernel, out_shape=(kept((cells, depth)), kept((rows...  6.59 us
    pallas_call x1, Pallas kernels, decode(): pl.pallas_call(decode_kernel, out_shape=(jax.ShapeDtypeStruct((cells, dep...  4.1 us
    ppermute x5, waiting for transfers between devices, swapped(): return lax.ppermute(block, AXES, [(i, i ^ 1) for i in range(count)])  2.9 us
    pallas_call x1, Pallas kernels, grid_hidden(): pl.pallas_call(grid_hidden_kernel, out_shape=(kept((cells, hidden)), kept...  2.36 us
    pallas_call x1, Pallas kernels, attend_near(): pl.pallas_call(attend_near_kernel, out_shape=kept((2 * rows, depth)), in_...  1.9 us
    pallas_call x1, Pallas kernels, mesh_hidden(): pl.pallas_call(mesh_hidden_kernel, out_shape=kept(((2 * REACH + 1) * rows...  1.28 us
  transfers between devices with their start and end apart: 8, of which 6 were waited for; matrix products, arithmetic and copies ran while one was open for 0% of the time, Pallas kernels for 18%

profile of v7, /device:TPU:0, one launch (start us, length us, event | category | flops | bytes accessed | tf_op | source)
XLA Modules:
  0.0 42.9 jit_solution(5642118821245965306)
XLA Ops:
  0.6 6.6 %encode.1 = (bf16[1024,512]{1,0:T(8,128)(2,1)S(1)}, bf16[144,512]{1,0:T(8,128)(2,1)S(1)}, bf16[272,512]{1,0:T(8,128)(2,1)S(1)}, f32[256,512]{1,0:T(8,128)S(1)}, bf16[512,2048]{1,0:T(8,128)(2,1)S(1)}) custom-call(s32[8]{0:T(128)} %owner_hbm.2, s32[1,3]{1,0:T(1,128)} %listed_hbm.1, f32[8,128]{1,0:T(8,128)} %bitcast.10, bf16[128,512]{1,0:T(8,128)(2,1)} %feat_hbm.1, ...), custom_call_target="tpu_custom_call" | custom-call | flops 4294967296 | bytes 6291456 | tf_op jit(solution)/shard_map/encode/pallas_call | solution.py:137
  7.2 0.5 %collective-permute-start = (bf16[144,512]{1,0:T(8,128)(2,1)S(1)}, bf16[144,512]{1,0:T(8,128)(2,1)S(1)}, u32[]{:S(2)}, u32[]{:S(2)}) collective-permute-start(bf16[144,512]{1,0:T(8,128)(2,1)S(1)} %get-tuple-element.20), channel_id=1, source_target_pairs={{0,1},{1,0},{2,3},{3,2},{4,5},{5,4},{6,7},{7,6},{8,9},{9,8},{10,11... | collective-permute-start | bytes 442376 | tf_op jit(solution)/shard_map/ppermute | solution.py:23
  7.7 1.0 %collective-permute-done.arrived_ref = bf16[144,512]{1,0:T(8,128)(2,1)S(1)} collective-permute-done((bf16[144,512]{1,0:T(8,128)(2,1)S(1)}, bf16[144,512]{1,0:T(8,128)(2,1)S(1)}, u32[]{:S(2)}, u32[]{:S(2)}) %collective-permute-start) | collective-permute-done | bytes 147488 | tf_op jit(solution)/shard_map/ppermute | solution.py:23
  8.8 6.7 %collective-permute-start.1 = (bf16[272,512]{1,0:T(8,128)(2,1)S(1)}, bf16[272,512]{1,0:T(8,128)(2,1)S(1)}, u32[]{:S(2)}, u32[]{:S(2)}) collective-permute-start(bf16[272,512]{1,0:T(8,128)(2,1)S(1)} %outgoing_sums.1.after), channel_id=1, source_target_pairs={{0,31},{1,2},{2,1},{3,4},{4,3},{5,6},{6,5},{7,8},{8,7},{9,10},{10,... | collective-permute-start | bytes 835592 | tf_op jit(solution)/shard_map/ppermute | solution.py:32
  15.5 2.4 %grid_hidden.1 = (bf16[1024,2048]{1,0:T(8,128)(2,1)S(1)}, bf16[2048,512]{1,0:T(8,128)(2,1)S(1)}) custom-call(bf16[1024,512]{1,0:T(8,128)(2,1)S(1)} %get-tuple-element.21.enc_ref, bf16[512,2048]{1,0:T(8,128)(2,1)S(1)} %get-tuple-element.22.first, bf16[2048,512]{1,0:T(8,128)(2,1)} %second_hbm.3, bf16[272,512]{1,0:T(8,128)(2,1)S(1)} %outgoing_sums.1.after), custom_call_target="tpu_custom_call" | custom-call | flops 2147483648 | bytes 3145728 | tf_op jit(solution)/shard_map/grid_hidden/pallas_call | solution.py:366
  17.8 2.0 %collective-permute-done.1.arrived_ref.sums_ref = bf16[272,512]{1,0:T(8,128)(2,1)S(1)} collective-permute-done((bf16[272,512]{1,0:T(8,128)(2,1)S(1)}, bf16[272,512]{1,0:T(8,128)(2,1)S(1)}, u32[]{:S(2)}, u32[]{:S(2)}) %collective-permute-start.1) | collective-permute-done | bytes 278560 | tf_op jit(solution)/shard_map/ppermute | solution.py:32
  19.8 0.0 copy-start
  19.8 0.1 chip_share.1
  19.9 0.0 copy-start.1
  19.9 0.1 collective-permute-start.2
  20.0 1.5 %collective-permute-done.2.other_ref = bf16[256,512]{1,0:T(8,128)(2,1)S(1)} collective-permute-done((bf16[256,512]{1,0:T(8,128)(2,1)S(1)}, bf16[256,512]{1,0:T(8,128)(2,1)S(1)}, u32[]{:S(2)}, u32[]{:S(2)}) %collective-permute-start.2) | collective-permute-done | bytes 262176 | tf_op jit(solution)/shard_map/ppermute | solution.py:23
  21.5 0.1 chip_states.1
  21.6 5.3 %collective-permute-start.3 = (bf16[256,512]{1,0:T(8,128)(2,1)S(1)}, bf16[256,512]{1,0:T(8,128)(2,1)S(1)}, u32[]{:S(2)}, u32[]{:S(2)}) collective-permute-start(bf16[256,512]{1,0:T(8,128)(2,1)S(1)} %get-tuple-element.28), channel_id=1, source_target_pairs={{0,31},{1,2},{2,1},{3,4},{4,3},{5,6},{6,5},{7,8},{8,7},{9,10},{10,... | collective-permute-start | bytes 786440 | tf_op jit(solution)/shard_map/ppermute | solution.py:32
  26.9 0.3 collective-permute-start.5
  27.2 4.0 %collective-permute-done.3.near_ref = bf16[256,512]{1,0:T(8,128)(2,1)S(1)} collective-permute-done((bf16[256,512]{1,0:T(8,128)(2,1)S(1)}, bf16[256,512]{1,0:T(8,128)(2,1)S(1)}, u32[]{:S(2)}, u32[]{:S(2)}) %collective-permute-start.3) | collective-permute-done | bytes 262176 | tf_op jit(solution)/shard_map/ppermute | solution.py:32
  31.2 0.1 collective-permute-start.4
  31.3 0.0 copy-done
  31.3 0.0 copy-done.3
  31.3 1.0 %project.1 = (bf16[384,512]{1,0:T(8,128)(2,1)S(1)}, bf16[512,1024]{1,0:T(8,128)(2,1)S(1)}) custom-call(bf16[256,512]{1,0:T(8,128)(2,1)S(1)} %get-tuple-element.27.pair_ref, bf16[256,512]{1,0:T(8,128)(2,1)S(1)} %collective-permute-done.3.near_ref, f32[1,512]{1,0:T(1,128)S(1)} %copy-done.3, bf16[512,1536]{1,0:T(8,128)(2,1)S(1)} %bitcast.4), custom_call_target="tpu_custom_call" | custom-call | flops 738197504 | bytes 131072 | tf_op jit(solution)/shard_map/project/pallas_call | solution.py:238
  32.3 0.3 collective-permute-done.4.behind_ref
  32.6 0.0 copy-done.1
  32.6 1.2 %attend_own.1.after.ring_own = bf16[128,512]{1,0:T(8,128)(2,1)S(1)} custom-call(bf16[272,512]{1,0:T(8,128)(2,1)S(1)} %get-tuple-element.18.base_ref, f32[128,512]{1,0:T(8,128)S(1)} %get-tuple-element.26.own_ref, bf16[384,512]{1,0:T(8,128)(2,1)S(1)} %get-tuple-element.29.query_ref, bf16[512,1024]{1,0:T(8,128)(2,1)S(1)} %get-tuple-element.30.kv_ref, ...), custom_call_target="tpu_custom_call" | custom-call | flops 671088640 | bytes 131072 | tf_op jit(solution)/shard_map/attend_own/pallas_call | solution.py:316
  33.9 0.2 collective-permute-start.6
  34.1 1.3 %collective-permute-done.5.far_ref = bf16[256,512]{1,0:T(8,128)(2,1)S(1)} collective-permute-done((bf16[256,512]{1,0:T(8,128)(2,1)S(1)}, bf16[256,512]{1,0:T(8,128)(2,1)S(1)}, u32[]{:S(2)}, u32[]{:S(2)}) %collective-permute-start.5) | collective-permute-done | bytes 262176 | tf_op jit(solution)/shard_map/ppermute | solution.py:32
  35.4 1.9 %attend_near.1.ring_near = bf16[256,512]{1,0:T(8,128)(2,1)S(1)} custom-call(bf16[272,512]{1,0:T(8,128)(2,1)S(1)} %collective-permute-done.1.arrived_ref.sums_ref, bf16[256,512]{1,0:T(8,128)(2,1)S(1)} %collective-permute-done.3.near_ref, bf16[384,512]{1,0:T(8,128)(2,1)S(1)} %get-tuple-element.29.query_ref, bf16[512,1024]{1,0:T(8,128)(2,1)S(1)} %get-tuple-element.30.kv_ref, ...), custom_call_target="tpu_custom_call" | custom-call | flops 1342177280 | bytes 131072 | tf_op jit(solution)/shard_map/attend_near/pallas_call | solution.py:332
  37.3 0.0 copy-start.2
  37.3 0.1 collective-permute-start.7
  37.4 0.0 collective-permute-done.6.back_own
  37.4 1.3 %mesh_hidden.1.mesh_in = bf16[640,2048]{1,0:T(8,128)(2,1)S(1)} custom-call(bf16[128,512]{1,0:T(8,128)(2,1)S(1)} %collective-permute-done.6.back_own, bf16[128,512]{1,0:T(8,128)(2,1)S(1)} %attend_own.1.after.ring_own, bf16[256,512]{1,0:T(8,128)(2,1)S(1)} %attend_near.1.ring_near, bf16[512,2048]{1,0:T(8,128)(2,1)S(1)} %get-tuple-element.22.first), custom_call_target="tpu_custom_call" | custom-call | flops 1073741824 | bytes 131072 | tf_op jit(solution)/shard_map/mesh_hidden/pallas_call | solution.py:389
  38.7 0.0 collective-permute-done.7.back_near
  38.8 0.0 copy-done.2
  38.8 4.1 %decode.1 = (bf16[1024,512]{1,0:T(8,128)(2,1)}, bf16[128,512]{1,0:T(8,128)(2,1)}, bf16[640,2048]{1,0:T(8,128)(2,1)S(1)}) custom-call(s32[8]{0:T(128)} %owner_hbm.3, f32[8,128]{1,0:T(8,128)S(1)} %bitcast.9, bf16[128,512]{1,0:T(8,128)(2,1)S(1)} %attend_own.1.after.ring_own, ...), custom_call_target="tpu_custom_call", output_to_operand_aliasing={{2}: (7, {})} | custom-call | flops 2147483648 | bytes 6291456 | tf_op jit(solution)/shard_map/decode/pallas_call | solution.py:451
  (4 shorter events, 0.1 us)
Async XLA Ops:
  7.2 1.5 %collective-permute-start = (bf16[144,512]{1,0:T(8,128)(2,1)S(1)}, bf16[144,512]{1,0:T(8,128)(2,1)S(1)}, u32[]{:S(2)}, u32[]{:S(2)}) collective-permute-start(bf16[144,512]{1,0:T(8,128)(2,1)S(1)} %get-tuple-element.20), channel_id=1, source_target_pairs={{0,1},{1,0},{2,3},{3,2},{4,5},{5,4},{6,7},{7,6},{8,9},{9,8},{10,11... | collective-permute-start | bytes 442376 | tf_op jit(solution)/shard_map/ppermute | solution.py:23
  8.8 11.0 %collective-permute-start.1 = (bf16[272,512]{1,0:T(8,128)(2,1)S(1)}, bf16[272,512]{1,0:T(8,128)(2,1)S(1)}, u32[]{:S(2)}, u32[]{:S(2)}) collective-permute-start(bf16[272,512]{1,0:T(8,128)(2,1)S(1)} %outgoing_sums.1.after), channel_id=1, source_target_pairs={{0,31},{1,2},{2,1},{3,4},{4,3},{5,6},{6,5},{7,8},{8,7},{9,10},{10,... | collective-permute-start | bytes 835592 | tf_op jit(solution)/shard_map/ppermute | solution.py:32
  19.8 11.5 %copy-start = (bf16[1,512,1536]{2,1,0:T(8,128)(2,1)S(1)}, bf16[1,512,1536]{2,1,0:T(8,128)(2,1)}, u32[]{:S(2)}) copy-start(bf16[1,512,1536]{2,1,0:T(8,128)(2,1)} %param.24) | copy-start | bytes 4718596
  19.8 11.5 %copy-start.3 = (f32[1,512]{1,0:T(1,128)S(1)}, f32[1,512]{1,0:T(1,128)}, u32[]{:S(2)}) copy-start(f32[1,512]{1,0:T(1,128)} %gain_ref.5) | copy-start | bytes 6148
  19.9 12.7 %copy-start.1 = (bf16[1,512,512]{2,1,0:T(8,128)(2,1)S(1)}, bf16[1,512,512]{2,1,0:T(8,128)(2,1)}, u32[]{:S(2)}) copy-start(bf16[1,512,512]{2,1,0:T(8,128)(2,1)} %param.25) | copy-start | bytes 1572868
  19.9 1.6 %collective-permute-start.2 = (bf16[256,512]{1,0:T(8,128)(2,1)S(1)}, bf16[256,512]{1,0:T(8,128)(2,1)S(1)}, u32[]{:S(2)}, u32[]{:S(2)}) collective-permute-start(bf16[256,512]{1,0:T(8,128)(2,1)S(1)} %get-tuple-element.25), channel_id=1, source_target_pairs={{0,1},{1,0},{2,3},{3,2},{4,5},{5,4},{6,7},{7,6},{8,9},{9,8},{10,11... | collective-permute-start | bytes 786440 | tf_op jit(solution)/shard_map/ppermute | solution.py:23
  21.6 9.6 %collective-permute-start.3 = (bf16[256,512]{1,0:T(8,128)(2,1)S(1)}, bf16[256,512]{1,0:T(8,128)(2,1)S(1)}, u32[]{:S(2)}, u32[]{:S(2)}) collective-permute-start(bf16[256,512]{1,0:T(8,128)(2,1)S(1)} %get-tuple-element.28), channel_id=1, source_target_pairs={{0,31},{1,2},{2,1},{3,4},{4,3},{5,6},{6,5},{7,8},{8,7},{9,10},{10,... | collective-permute-start | bytes 786440 | tf_op jit(solution)/shard_map/ppermute | solution.py:32
  26.9 8.5 %collective-permute-start.5 = (bf16[256,512]{1,0:T(8,128)(2,1)S(1)}, bf16[256,512]{1,0:T(8,128)(2,1)S(1)}, u32[]{:S(2)}, u32[]{:S(2)}) collective-permute-start(bf16[256,512]{1,0:T(8,128)(2,1)S(1)} %get-tuple-element.28), channel_id=1, source_target_pairs={{0,29},{1,4},{2,31},{3,6},{4,1},{5,8},{6,3},{7,10},{8,5},{9,12},{1... | collective-permute-start | bytes 786440 | tf_op jit(solution)/shard_map/ppermute | solution.py:32
  31.2 1.4 %collective-permute-start.4 = (bf16[128,512]{1,0:T(8,128)(2,1)S(1)}, bf16[128,512]{1,0:T(8,128)(2,1)S(1)}, u32[]{:S(2)}, u32[]{:S(2)}) collective-permute-start(bf16[128,512]{1,0:T(8,128)(2,1)S(1)} %slice.8), channel_id=1, source_target_pairs={{0,1},{1,0},{2,3},{3,2},{4,5},{5,4},{6,7},{7,6},{8,9},{9,8},{10,11... | collective-permute-start | bytes 393224 | tf_op jit(solution)/shard_map/ppermute | solution.py:23
  33.9 3.6 %collective-permute-start.6 = (bf16[128,512]{1,0:T(8,128)(2,1)S(1)}, bf16[128,512]{1,0:T(8,128)(2,1)S(1)}, u32[]{:S(2)}, u32[]{:S(2)}) collective-permute-start(bf16[128,512]{1,0:T(8,128)(2,1)S(1)} %attend_own.1.after.ring_own), channel_id=1, source_target_pairs={{0,1},{1,0},{2,3},{3,2},{4,5},{5,4},{6,7},{7,6},{8,9},{9,8},{10,11... | collective-permute-start | bytes 393224 | tf_op jit(solution)/shard_map/ppermute | solution.py:23
  37.3 1.4 %copy-start.2 = (f32[1024]{0:T(1024)S(1)}, f32[1024]{0:T(1024)}, u32[]{:S(2)}) copy-start(f32[1024]{0:T(1024)} %param.18) | copy-start | bytes 12292
  37.3 1.4 %collective-permute-start.7 = (bf16[128,512]{1,0:T(8,128)(2,1)S(1)}, bf16[128,512]{1,0:T(8,128)(2,1)S(1)}, u32[]{:S(2)}, u32[]{:S(2)}) collective-permute-start(bf16[128,512]{1,0:T(8,128)(2,1)S(1)} %slice.9), channel_id=1, source_target_pairs={{0,1},{1,0},{2,3},{3,2},{4,5},{5,4},{6,7},{7,6},{8,9},{9,8},{10,11... | collective-permute-start | bytes 393224 | tf_op jit(solution)/shard_map/ppermute | solution.py:23

commit v8 on v7

--- a/solution.py
+++ b/solution.py
@@ -9,6 +9,7 @@
 
 HD = 128
 REACH = 2
+LOG2E = 1.4426950408889634
 EXTRA = 16
 AXES = ("tile", "sub")
 BF16 = jnp.bfloat16
@@ -262,8 +263,8 @@
         for cols in every
     ]
     scores = [jnp.where(keep, score, -jnp.inf) for score in scores]
-    below = [(score - jnp.max(score, axis=-1, keepdims=True)) * (HD ** -0.5) for score in scores]
-    grown = [jnp.exp(score.astype(BF16)) for score in below]
+    below = [(score - jnp.max(score, axis=-1, keepdims=True)) * (HD ** -0.5 * LOG2E) for score in scores]
+    grown = [jnp.exp2(score.astype(BF16)) for score in below]
     heads = []
     for h, cols in enumerate(every):
         start, taken = 0, None
@@ -409,8 +410,8 @@
     tile, part = tiles_of(x_ref.shape[0], first.shape[1])
     tile = min(tile, 256)
     tiles, parts = x_ref.shape[0] // tile, first.shape[1] // part
-    stores = [pltpu.make_async_copy(ring_own, mesh_hbm, io_sems.at[tiles])]
-    index = pltpu.make_async_copy(owner_hbm, owner, io_sems.at[tiles + 1])
+    stores = [pltpu.make_async_copy(ring_own, mesh_hbm, io_sems.at[x_ref.shape[0] // rows])]
+    index = pltpu.make_async_copy(owner_hbm, owner, io_sems.at[x_ref.shape[0] // rows + 1])
     index.start()
     stores[0].start()
     mine, count = lax.axis_index(AXES), lax.axis_size(AXES)
@@ -424,6 +425,7 @@
     index.wait()
     for r in range(tiles):
         cut = slice(r * tile, (r + 1) * tile)
+        reads = []
         for b in range(r * tile // rows, (r + 1) * tile // rows):
             slot = outward * offset_of(owner[b], mine, count) + REACH
             lines = pl.ds(pl.multiple_of(slot * rows, rows), rows)
@@ -434,12 +436,14 @@
                 cols = slice(j * part, (j + 1) * part)
                 half = grid_ref[block, cols] + narrow * mesh_ref[lines, cols]
                 act[block, cols] = half * jnp.tanh(half) + half
-            x_ref[block, :] = (enc_ref[block, :].astype(F32) + weight * ring[lines, :].astype(F32)).astype(BF16)
+            reads.append((block, weight, lines))
         out = jnp.dot(act[cut, :], second[...], preferred_element_type=F32)
-        x_ref[cut, :] = (x_ref[cut, :].astype(F32) + out).astype(BF16)
-        copy = pltpu.make_async_copy(x_ref.at[pl.ds(r * tile, tile)], out_hbm.at[pl.ds(r * tile, tile)], io_sems.at[r])
-        copy.start()
-        stores.append(copy)
+        for n, (block, weight, lines) in enumerate(reads):
+            rest = enc_ref[block, :].astype(F32) + weight * ring[lines, :].astype(F32)
+            x_ref[block, :] = (rest + out[n * rows:(n + 1) * rows, :]).astype(BF16)
+            copy = pltpu.make_async_copy(x_ref.at[block], out_hbm.at[block], io_sems.at[r * tile // rows + n])
+            copy.start()
+            stores.append(copy)
     for copy in stores:
         copy.wait()
 
@@ -463,7 +467,7 @@
             pltpu.VMEM((cells, depth), BF16),
             pltpu.VMEM((cells, hidden), BF16),
             pltpu.VMEM(((2 * REACH + 1) * rows, depth), BF16),
-            pltpu.SemaphoreType.DMA((cells // min(cells, 256) + 2,)),
+            pltpu.SemaphoreType.DMA((cells // rows + 2,)),
         ],
         compiler_params=pltpu.CompilerParams(vmem_limit_bytes=16 << 20),
         cost_estimate=pl.CostEstimate(

time: 43 us -> 42.9 us (level)
  no operation moved by 1% of the time
where the time goes in v8:
time: 42.9 us; the launch traced here: 42.7 us
  Pallas kernels  18.5 us (43%)
  starting transfers between devices  13.2 us (31%)
  waiting for transfers between devices  10.2 us (24%)
  between operations  0.77 us (2%)
    ppermute x3, starting transfers between devices, from_outward(): return lax.ppermute(block, AXES, route)  12.3 us
    ppermute x3, waiting for transfers between devices, from_outward(): return lax.ppermute(block, AXES, route)  7.26 us
    pallas_call x1, Pallas kernels, encode(): pl.pallas_call(encode_kernel, out_shape=(kept((cells, depth)), kept((rows...  6.59 us
    pallas_call x1, Pallas kernels, decode(): pl.pallas_call(decode_kernel, out_shape=(jax.ShapeDtypeStruct((cells, dep...  4.02 us
    ppermute x5, waiting for transfers between devices, swapped(): return lax.ppermute(block, AXES, [(i, i ^ 1) for i in range(count)])  2.9 us
    pallas_call x1, Pallas kernels, grid_hidden(): pl.pallas_call(grid_hidden_kernel, out_shape=(kept((cells, hidden)), kept...  2.36 us
    pallas_call x1, Pallas kernels, attend_near(): pl.pallas_call(attend_near_kernel, out_shape=kept((2 * rows, depth)), in_...  1.86 us
    pallas_call x1, Pallas kernels, mesh_hidden(): pl.pallas_call(mesh_hidden_kernel, out_shape=kept(((2 * REACH + 1) * rows...  1.27 us
  transfers between devices with their start and end apart: 8, of which 6 were waited for; matrix products, arithmetic and copies ran while one was open for 0% of the time, Pallas kernels for 18%

profile of v8, /device:TPU:0, one launch (start us, length us, event | category | flops | bytes accessed | tf_op | source)
XLA Modules:
  0.0 42.7 jit_solution(13075496142142079220)
XLA Ops:
  0.6 6.6 %encode.1 = (bf16[1024,512]{1,0:T(8,128)(2,1)S(1)}, bf16[144,512]{1,0:T(8,128)(2,1)S(1)}, bf16[272,512]{1,0:T(8,128)(2,1)S(1)}, f32[256,512]{1,0:T(8,128)S(1)}, bf16[512,2048]{1,0:T(8,128)(2,1)S(1)}) custom-call(s32[8]{0:T(128)} %owner_hbm.2, s32[1,3]{1,0:T(1,128)} %listed_hbm.1, f32[8,128]{1,0:T(8,128)} %bitcast.10, bf16[128,512]{1,0:T(8,128)(2,1)} %feat_hbm.1, ...), custom_call_target="tpu_custom_call" | custom-call | flops 4294967296 | bytes 6291456 | tf_op jit(solution)/shard_map/encode/pallas_call | solution.py:138
  7.2 0.5 %collective-permute-start = (bf16[144,512]{1,0:T(8,128)(2,1)S(1)}, bf16[144,512]{1,0:T(8,128)(2,1)S(1)}, u32[]{:S(2)}, u32[]{:S(2)}) collective-permute-start(bf16[144,512]{1,0:T(8,128)(2,1)S(1)} %get-tuple-element.20), channel_id=1, source_target_pairs={{0,1},{1,0},{2,3},{3,2},{4,5},{5,4},{6,7},{7,6},{8,9},{9,8},{10,11... | collective-permute-start | bytes 442376 | tf_op jit(solution)/shard_map/ppermute | solution.py:24
  7.7 1.0 %collective-permute-done.arrived_ref = bf16[144,512]{1,0:T(8,128)(2,1)S(1)} collective-permute-done((bf16[144,512]{1,0:T(8,128)(2,1)S(1)}, bf16[144,512]{1,0:T(8,128)(2,1)S(1)}, u32[]{:S(2)}, u32[]{:S(2)}) %collective-permute-start) | collective-permute-done | bytes 147488 | tf_op jit(solution)/shard_map/ppermute | solution.py:24
  8.8 6.7 %collective-permute-start.1 = (bf16[272,512]{1,0:T(8,128)(2,1)S(1)}, bf16[272,512]{1,0:T(8,128)(2,1)S(1)}, u32[]{:S(2)}, u32[]{:S(2)}) collective-permute-start(bf16[272,512]{1,0:T(8,128)(2,1)S(1)} %outgoing_sums.1.after), channel_id=1, source_target_pairs={{0,31},{1,2},{2,1},{3,4},{4,3},{5,6},{6,5},{7,8},{8,7},{9,10},{10,... | collective-permute-start | bytes 835592 | tf_op jit(solution)/shard_map/ppermute | solution.py:33
  15.5 2.4 %grid_hidden.1 = (bf16[1024,2048]{1,0:T(8,128)(2,1)S(1)}, bf16[2048,512]{1,0:T(8,128)(2,1)S(1)}) custom-call(bf16[1024,512]{1,0:T(8,128)(2,1)S(1)} %get-tuple-element.21.enc_ref, bf16[512,2048]{1,0:T(8,128)(2,1)S(1)} %get-tuple-element.22.first, bf16[2048,512]{1,0:T(8,128)(2,1)} %second_hbm.3, bf16[272,512]{1,0:T(8,128)(2,1)S(1)} %outgoing_sums.1.after), custom_call_target="tpu_custom_call" | custom-call | flops 2147483648 | bytes 3145728 | tf_op jit(solution)/shard_map/grid_hidden/pallas_call | solution.py:367
  17.8 2.0 %collective-permute-done.1.arrived_ref.sums_ref = bf16[272,512]{1,0:T(8,128)(2,1)S(1)} collective-permute-done((bf16[272,512]{1,0:T(8,128)(2,1)S(1)}, bf16[272,512]{1,0:T(8,128)(2,1)S(1)}, u32[]{:S(2)}, u32[]{:S(2)}) %collective-permute-start.1) | collective-permute-done | bytes 278560 | tf_op jit(solution)/shard_map/ppermute | solution.py:33
  19.8 0.0 copy-start
  19.8 0.1 chip_share.1
  19.9 0.0 copy-start.1
  19.9 0.1 collective-permute-start.2
  20.0 1.5 %collective-permute-done.2.other_ref = bf16[256,512]{1,0:T(8,128)(2,1)S(1)} collective-permute-done((bf16[256,512]{1,0:T(8,128)(2,1)S(1)}, bf16[256,512]{1,0:T(8,128)(2,1)S(1)}, u32[]{:S(2)}, u32[]{:S(2)}) %collective-permute-start.2) | collective-permute-done | bytes 262176 | tf_op jit(solution)/shard_map/ppermute | solution.py:24
  21.5 0.1 chip_states.1
  21.6 5.3 %collective-permute-start.3 = (bf16[256,512]{1,0:T(8,128)(2,1)S(1)}, bf16[256,512]{1,0:T(8,128)(2,1)S(1)}, u32[]{:S(2)}, u32[]{:S(2)}) collective-permute-start(bf16[256,512]{1,0:T(8,128)(2,1)S(1)} %get-tuple-element.28), channel_id=1, source_target_pairs={{0,31},{1,2},{2,1},{3,4},{4,3},{5,6},{6,5},{7,8},{8,7},{9,10},{10,... | collective-permute-start | bytes 786440 | tf_op jit(solution)/shard_map/ppermute | solution.py:33
  26.9 0.3 collective-permute-start.5
  27.2 4.0 %collective-permute-done.3.near_ref = bf16[256,512]{1,0:T(8,128)(2,1)S(1)} collective-permute-done((bf16[256,512]{1,0:T(8,128)(2,1)S(1)}, bf16[256,512]{1,0:T(8,128)(2,1)S(1)}, u32[]{:S(2)}, u32[]{:S(2)}) %collective-permute-start.3) | collective-permute-done | bytes 262176 | tf_op jit(solution)/shard_map/ppermute | solution.py:33
  31.2 0.1 collective-permute-start.4
  31.3 0.0 copy-done
  31.3 0.0 copy-done.3
  31.3 1.0 %project.1 = (bf16[384,512]{1,0:T(8,128)(2,1)S(1)}, bf16[512,1024]{1,0:T(8,128)(2,1)S(1)}) custom-call(bf16[256,512]{1,0:T(8,128)(2,1)S(1)} %get-tuple-element.27.pair_ref, bf16[256,512]{1,0:T(8,128)(2,1)S(1)} %collective-permute-done.3.near_ref, f32[1,512]{1,0:T(1,128)S(1)} %copy-done.3, bf16[512,1536]{1,0:T(8,128)(2,1)S(1)} %bitcast.4), custom_call_target="tpu_custom_call" | custom-call | flops 738197504 | bytes 131072 | tf_op jit(solution)/shard_map/project/pallas_call | solution.py:239
  32.3 0.3 collective-permute-done.4.behind_ref
  32.6 0.0 copy-done.1
  32.6 1.2 %attend_own.1.after.ring_own = bf16[128,512]{1,0:T(8,128)(2,1)S(1)} custom-call(bf16[272,512]{1,0:T(8,128)(2,1)S(1)} %get-tuple-element.18.base_ref, f32[128,512]{1,0:T(8,128)S(1)} %get-tuple-element.26.own_ref, bf16[384,512]{1,0:T(8,128)(2,1)S(1)} %get-tuple-element.29.query_ref, bf16[512,1024]{1,0:T(8,128)(2,1)S(1)} %get-tuple-element.30.kv_ref, ...), custom_call_target="tpu_custom_call" | custom-call | flops 671088640 | bytes 131072 | tf_op jit(solution)/shard_map/attend_own/pallas_call | solution.py:317
  33.8 0.2 collective-permute-start.6
  34.1 1.3 %collective-permute-done.5.far_ref = bf16[256,512]{1,0:T(8,128)(2,1)S(1)} collective-permute-done((bf16[256,512]{1,0:T(8,128)(2,1)S(1)}, bf16[256,512]{1,0:T(8,128)(2,1)S(1)}, u32[]{:S(2)}, u32[]{:S(2)}) %collective-permute-start.5) | collective-permute-done | bytes 262176 | tf_op jit(solution)/shard_map/ppermute | solution.py:33
  35.4 1.9 %attend_near.1.ring_near = bf16[256,512]{1,0:T(8,128)(2,1)S(1)} custom-call(bf16[272,512]{1,0:T(8,128)(2,1)S(1)} %collective-permute-done.1.arrived_ref.sums_ref, bf16[256,512]{1,0:T(8,128)(2,1)S(1)} %collective-permute-done.3.near_ref, bf16[384,512]{1,0:T(8,128)(2,1)S(1)} %get-tuple-element.29.query_ref, bf16[512,1024]{1,0:T(8,128)(2,1)S(1)} %get-tuple-element.30.kv_ref, ...), custom_call_target="tpu_custom_call" | custom-call | flops 1342177280 | bytes 131072 | tf_op jit(solution)/shard_map/attend_near/pallas_call | solution.py:333
  37.3 0.0 copy-start.2
  37.3 0.1 collective-permute-start.7
  37.4 0.0 collective-permute-done.6.back_own
  37.4 1.3 %mesh_hidden.1.mesh_in = bf16[640,2048]{1,0:T(8,128)(2,1)S(1)} custom-call(bf16[128,512]{1,0:T(8,128)(2,1)S(1)} %collective-permute-done.6.back_own, bf16[128,512]{1,0:T(8,128)(2,1)S(1)} %attend_own.1.after.ring_own, bf16[256,512]{1,0:T(8,128)(2,1)S(1)} %attend_near.1.ring_near, bf16[512,2048]{1,0:T(8,128)(2,1)S(1)} %get-tuple-element.22.first), custom_call_target="tpu_custom_call" | custom-call | flops 1073741824 | bytes 131072 | tf_op jit(solution)/shard_map/mesh_hidden/pallas_call | solution.py:390
  38.7 0.0 collective-permute-done.7.back_near
  38.7 0.0 copy-done.2
  38.7 4.0 %decode.1 = (bf16[1024,512]{1,0:T(8,128)(2,1)}, bf16[128,512]{1,0:T(8,128)(2,1)}, bf16[640,2048]{1,0:T(8,128)(2,1)S(1)}) custom-call(s32[8]{0:T(128)} %owner_hbm.3, f32[8,128]{1,0:T(8,128)S(1)} %bitcast.9, bf16[128,512]{1,0:T(8,128)(2,1)S(1)} %attend_own.1.after.ring_own, ...), custom_call_target="tpu_custom_call", output_to_operand_aliasing={{2}: (7, {})} | custom-call | flops 2147483648 | bytes 6291456 | tf_op jit(solution)/shard_map/decode/pallas_call | solution.py:455
  (4 shorter events, 0.1 us)
Async XLA Ops:
  7.2 1.5 %collective-permute-start = (bf16[144,512]{1,0:T(8,128)(2,1)S(1)}, bf16[144,512]{1,0:T(8,128)(2,1)S(1)}, u32[]{:S(2)}, u32[]{:S(2)}) collective-permute-start(bf16[144,512]{1,0:T(8,128)(2,1)S(1)} %get-tuple-element.20), channel_id=1, source_target_pairs={{0,1},{1,0},{2,3},{3,2},{4,5},{5,4},{6,7},{7,6},{8,9},{9,8},{10,11... | collective-permute-start | bytes 442376 | tf_op jit(solution)/shard_map/ppermute | solution.py:24
  8.8 11.0 %collective-permute-start.1 = (bf16[272,512]{1,0:T(8,128)(2,1)S(1)}, bf16[272,512]{1,0:T(8,128)(2,1)S(1)}, u32[]{:S(2)}, u32[]{:S(2)}) collective-permute-start(bf16[272,512]{1,0:T(8,128)(2,1)S(1)} %outgoing_sums.1.after), channel_id=1, source_target_pairs={{0,31},{1,2},{2,1},{3,4},{4,3},{5,6},{6,5},{7,8},{8,7},{9,10},{10,... | collective-permute-start | bytes 835592 | tf_op jit(solution)/shard_map/ppermute | solution.py:33
  19.8 11.5 %copy-start = (bf16[1,512,1536]{2,1,0:T(8,128)(2,1)S(1)}, bf16[1,512,1536]{2,1,0:T(8,128)(2,1)}, u32[]{:S(2)}) copy-start(bf16[1,512,1536]{2,1,0:T(8,128)(2,1)} %param.24) | copy-start | bytes 4718596
  19.8 11.5 %copy-start.3 = (f32[1,512]{1,0:T(1,128)S(1)}, f32[1,512]{1,0:T(1,128)}, u32[]{:S(2)}) copy-start(f32[1,512]{1,0:T(1,128)} %gain_ref.5) | copy-start | bytes 6148
  19.9 12.7 %copy-start.1 = (bf16[1,512,512]{2,1,0:T(8,128)(2,1)S(1)}, bf16[1,512,512]{2,1,0:T(8,128)(2,1)}, u32[]{:S(2)}) copy-start(bf16[1,512,512]{2,1,0:T(8,128)(2,1)} %param.25) | copy-start | bytes 1572868
  19.9 1.6 %collective-permute-start.2 = (bf16[256,512]{1,0:T(8,128)(2,1)S(1)}, bf16[256,512]{1,0:T(8,128)(2,1)S(1)}, u32[]{:S(2)}, u32[]{:S(2)}) collective-permute-start(bf16[256,512]{1,0:T(8,128)(2,1)S(1)} %get-tuple-element.25), channel_id=1, source_target_pairs={{0,1},{1,0},{2,3},{3,2},{4,5},{5,4},{6,7},{7,6},{8,9},{9,8},{10,11... | collective-permute-start | bytes 786440 | tf_op jit(solution)/shard_map/ppermute | solution.py:24
  21.6 9.6 %collective-permute-start.3 = (bf16[256,512]{1,0:T(8,128)(2,1)S(1)}, bf16[256,512]{1,0:T(8,128)(2,1)S(1)}, u32[]{:S(2)}, u32[]{:S(2)}) collective-permute-start(bf16[256,512]{1,0:T(8,128)(2,1)S(1)} %get-tuple-element.28), channel_id=1, source_target_pairs={{0,31},{1,2},{2,1},{3,4},{4,3},{5,6},{6,5},{7,8},{8,7},{9,10},{10,... | collective-permute-start | bytes 786440 | tf_op jit(solution)/shard_map/ppermute | solution.py:33
  26.9 8.5 %collective-permute-start.5 = (bf16[256,512]{1,0:T(8,128)(2,1)S(1)}, bf16[256,512]{1,0:T(8,128)(2,1)S(1)}, u32[]{:S(2)}, u32[]{:S(2)}) collective-permute-start(bf16[256,512]{1,0:T(8,128)(2,1)S(1)} %get-tuple-element.28), channel_id=1, source_target_pairs={{0,29},{1,4},{2,31},{3,6},{4,1},{5,8},{6,3},{7,10},{8,5},{9,12},{1... | collective-permute-start | bytes 786440 | tf_op jit(solution)/shard_map/ppermute | solution.py:33
  31.2 1.4 %collective-permute-start.4 = (bf16[128,512]{1,0:T(8,128)(2,1)S(1)}, bf16[128,512]{1,0:T(8,128)(2,1)S(1)}, u32[]{:S(2)}, u32[]{:S(2)}) collective-permute-start(bf16[128,512]{1,0:T(8,128)(2,1)S(1)} %slice.8), channel_id=1, source_target_pairs={{0,1},{1,0},{2,3},{3,2},{4,5},{5,4},{6,7},{7,6},{8,9},{9,8},{10,11... | collective-permute-start | bytes 393224 | tf_op jit(solution)/shard_map/ppermute | solution.py:24
  33.8 3.5 %collective-permute-start.6 = (bf16[128,512]{1,0:T(8,128)(2,1)S(1)}, bf16[128,512]{1,0:T(8,128)(2,1)S(1)}, u32[]{:S(2)}, u32[]{:S(2)}) collective-permute-start(bf16[128,512]{1,0:T(8,128)(2,1)S(1)} %attend_own.1.after.ring_own), channel_id=1, source_target_pairs={{0,1},{1,0},{2,3},{3,2},{4,5},{5,4},{6,7},{7,6},{8,9},{9,8},{10,11... | collective-permute-start | bytes 393224 | tf_op jit(solution)/shard_map/ppermute | solution.py:24
  37.3 1.4 %copy-start.2 = (f32[1024]{0:T(1024)S(1)}, f32[1024]{0:T(1024)}, u32[]{:S(2)}) copy-start(f32[1024]{0:T(1024)} %param.18) | copy-start | bytes 12292
  37.3 1.4 %collective-permute-start.7 = (bf16[128,512]{1,0:T(8,128)(2,1)S(1)}, bf16[128,512]{1,0:T(8,128)(2,1)S(1)}, u32[]{:S(2)}, u32[]{:S(2)}) collective-permute-start(bf16[128,512]{1,0:T(8,128)(2,1)S(1)} %slice.9), channel_id=1, source_target_pairs={{0,1},{1,0},{2,3},{3,2},{4,5},{5,4},{6,7},{7,6},{8,9},{9,8},{10,11... | collective-permute-start | bytes 393224 | tf_op jit(solution)/shard_map/ppermute | solution.py:24

commit v9 on v8

--- a/solution.py
+++ b/solution.py
@@ -11,6 +11,7 @@
 REACH = 2
 LOG2E = 1.4426950408889634
 EXTRA = 16
+LANES = 128
 AXES = ("tile", "sub")
 BF16 = jnp.bfloat16
 F32 = jnp.float32
@@ -51,6 +52,16 @@
 
 def in_hbm(*arrays):
     return [pltpu.with_memory_space_constraint(a, pltpu.HBM) for a in arrays]
+
+
+def strips(depth):
+    return [slice(k, k + LANES) for k in range(0, depth, LANES)]
+
+
+def spread(ref, first, block):
+    rows = block.shape[0]
+    for k, cols in enumerate(strips(block.shape[1])):
+        ref[first + k * rows:first + (k + 1) * rows, :] = block[:, cols].astype(BF16)
 
 
 def hidden_layer(x_ref, first, act, tile, part, arrive, before):
@@ -119,12 +130,13 @@
             slot = outward * offset_of(owner[b], mine, count) + REACH
             total[slot] += columns[:, b:b + 1] * out[b * rows - r * tile:(b + 1) * rows - r * tile, :]
     absent = sum(-offset_of(listed[0, n], mine, count) for n in range(listed.shape[1])).astype(F32)
-    spot = lax.broadcasted_iota(jnp.int32, (EXTRA, depth), 1)
-    msg_ref[:rows, :] = total[0].astype(BF16)
-    msg_ref[rows:, :] = jnp.where(spot == 1, absent, 0.0).astype(BF16)
-    base_ref[:rows, :] = total[4].astype(BF16)
-    base_ref[rows:2 * rows, :] = total[3].astype(BF16)
-    base_ref[2 * rows:, :] = jnp.where(spot == 0, absent, 0.0).astype(BF16)
+    spot = lax.broadcasted_iota(jnp.int32, (EXTRA, LANES), 1)
+    lines = rows * depth // LANES
+    spread(msg_ref, 0, total[0])
+    msg_ref[lines:, :] = jnp.where(spot == 1, absent, 0.0).astype(BF16)
+    spread(base_ref, 0, total[4])
+    spread(base_ref, lines, total[3])
+    base_ref[2 * lines:, :] = jnp.where(spot == 0, absent, 0.0).astype(BF16)
     loc_ref[:rows, :] = total[1]
     loc_ref[rows:, :] = total[2] + feat_ref[...].astype(F32)
     later.wait()
@@ -139,8 +151,8 @@
         encode_kernel,
         out_shape=(
             kept((cells, depth)),
-            kept((rows + EXTRA, depth)),
-            kept((2 * rows + EXTRA, depth)),
+            kept((rows * depth // LANES + EXTRA, LANES)),
+            kept((2 * rows * depth // LANES + EXTRA, LANES)),
             kept((2 * rows, depth), F32),
             kept(following.shape),
         ),
@@ -181,8 +193,12 @@
 
 def share_kernel(loc_ref, arrived_ref, after, share_ref, msg_ref):
     del after
-    rows = loc_ref.shape[0] // 2
-    share_ref[...] = loc_ref[...] + arrived_ref[:2 * rows, :].astype(F32)
+    rows, depth = loc_ref.shape[0] // 2, loc_ref.shape[1]
+    for half in range(2):
+        cut = slice(half * rows, (half + 1) * rows)
+        for k, cols in enumerate(strips(depth)):
+            line = (half * depth // LANES + k) * rows
+            share_ref[cut, cols] = loc_ref[cut, cols] + arrived_ref[line:line + rows, :].astype(F32)
     msg_ref[:rows, :] = share_ref[rows:, :].astype(BF16)
     msg_ref[rows:, :] = share_ref[:rows, :].astype(BF16)
 
@@ -288,7 +304,7 @@
     kv_behind[...] = jnp.dot(
         normal(behind_ref[...], gain_ref[...]), w_qkv[:, depth:], preferred_element_type=F32
     ).astype(BF16)
-    keep = kept_lanes(rows, base_ref[2 * rows:, 0:HD].astype(F32)[0:1, 0:1])
+    keep = kept_lanes(rows, base_ref[2 * rows * depth // LANES:, :].astype(F32)[0:1, 0:1])
     mixed = attention(query_ref[:rows, :], [(kv_behind, 0, rows), (kv_ref, 0, 4 * rows)], keep)
     ring_ref[...] = (own_ref[...] + jnp.dot(mixed, w_out[...], preferred_element_type=F32)).astype(BF16)
 
@@ -306,7 +322,7 @@
         [(kv_ref, rows, 3 * rows), (kv_far, 0, 2 * rows)],
     ]
     for n, window in enumerate(windows):
-        keep = kept_lanes(rows, sums_ref[2 * rows:, 0:HD].astype(F32)[0:1, n:n + 1])
+        keep = kept_lanes(rows, sums_ref[2 * rows * depth // LANES:, :].astype(F32)[0:1, n:n + 1])
         mixed[n * rows:(n + 1) * rows, :] = attention(query_ref[(n + 1) * rows:(n + 2) * rows, :], window, keep)
     added = jnp.dot(mixed[...], w_out[...], preferred_element_type=F32)
     ring_ref[...] = (near_ref[...].astype(F32) + added).astype(BF16)

time: 42.9 us -> 42.8 us (level)
  no operation moved by 1% of the time
where the time goes in v9:
time: 42.8 us; the launch traced here: 42.6 us
  Pallas kernels  18.5 us (43%)
  starting transfers between devices  13.3 us (31%)
  waiting for transfers between devices  9.97 us (23%)
  between operations  0.77 us (2%)
    ppermute x3, starting transfers between devices, from_outward(): return lax.ppermute(block, AXES, route)  12.3 us
    ppermute x3, waiting for transfers between devices, from_outward(): return lax.ppermute(block, AXES, route)  7.1 us
    pallas_call x1, Pallas kernels, encode(): pl.pallas_call(encode_kernel, out_shape=(kept((cells, depth)), kept((rows...  6.59 us
    pallas_call x1, Pallas kernels, decode(): pl.pallas_call(decode_kernel, out_shape=(jax.ShapeDtypeStruct((cells, dep...  4.02 us
    ppermute x5, waiting for transfers between devices, swapped(): return lax.ppermute(block, AXES, [(i, i ^ 1) for i in range(count)])  2.87 us
    pallas_call x1, Pallas kernels, grid_hidden(): pl.pallas_call(grid_hidden_kernel, out_shape=(kept((cells, hidden)), kept...  2.36 us
    pallas_call x1, Pallas kernels, attend_near(): pl.pallas_call(attend_near_kernel, out_shape=kept((2 * rows, depth)), in_...  1.84 us
    pallas_call x1, Pallas kernels, mesh_hidden(): pl.pallas_call(mesh_hidden_kernel, out_shape=kept(((2 * REACH + 1) * rows...  1.28 us
  transfers between devices with their start and end apart: 8, of which 6 were waited for; matrix products, arithmetic and copies ran while one was open for 0% of the time, Pallas kernels for 18%

profile of v9, /device:TPU:0, one launch (start us, length us, event | category | flops | bytes accessed | tf_op | source)
XLA Modules:
  0.0 42.6 jit_solution(10911822049066635548)
XLA Ops:
  0.6 6.6 %encode.1 = (bf16[1024,512]{1,0:T(8,128)(2,1)S(1)}, bf16[528,128]{1,0:T(8,128)(2,1)S(1)}, bf16[1040,128]{1,0:T(8,128)(2,1)S(1)}, f32[256,512]{1,0:T(8,128)S(1)}, bf16[512,2048]{1,0:T(8,128)(2,1)S(1)}) custom-call(s32[8]{0:T(128)} %owner_hbm.2, s32[1,3]{1,0:T(1,128)} %listed_hbm.1, f32[8,128]{1,0:T(8,128)} %bitcast.10, bf16[128,512]{1,0:T(8,128)(2,1)} %feat_hbm.1, ...), custom_call_target="tpu_custom_call" | custom-call | flops 4294967296 | bytes 6291456 | tf_op jit(solution)/shard_map/encode/pallas_call | solution.py:150
  7.2 0.5 %collective-permute-start = (bf16[528,128]{1,0:T(8,128)(2,1)S(1)}, bf16[528,128]{1,0:T(8,128)(2,1)S(1)}, u32[]{:S(2)}, u32[]{:S(2)}) collective-permute-start(bf16[528,128]{1,0:T(8,128)(2,1)S(1)} %get-tuple-element.20), channel_id=1, source_target_pairs={{0,1},{1,0},{2,3},{3,2},{4,5},{5,4},{6,7},{7,6},{8,9},{9,8},{10,11... | collective-permute-start | bytes 405512 | tf_op jit(solution)/shard_map/ppermute | solution.py:25
  7.7 1.0 %collective-permute-done.arrived_ref = bf16[528,128]{1,0:T(8,128)(2,1)S(1)} collective-permute-done((bf16[528,128]{1,0:T(8,128)(2,1)S(1)}, bf16[528,128]{1,0:T(8,128)(2,1)S(1)}, u32[]{:S(2)}, u32[]{:S(2)}) %collective-permute-start) | collective-permute-done | bytes 135200 | tf_op jit(solution)/shard_map/ppermute | solution.py:25
  8.8 6.7 %collective-permute-start.1 = (bf16[1040,128]{1,0:T(8,128)(2,1)S(1)}, bf16[1040,128]{1,0:T(8,128)(2,1)S(1)}, u32[]{:S(2)}, u32[]{:S(2)}) collective-permute-start(bf16[1040,128]{1,0:T(8,128)(2,1)S(1)} %outgoing_sums.1.after), channel_id=1, source_target_pairs={{0,31},{1,2},{2,1},{3,4},{4,3},{5,6},{6,5},{7,8},{8,7},{9,10},{10,... | collective-permute-start | bytes 798728 | tf_op jit(solution)/shard_map/ppermute | solution.py:34
  15.4 2.4 %grid_hidden.1 = (bf16[1024,2048]{1,0:T(8,128)(2,1)S(1)}, bf16[2048,512]{1,0:T(8,128)(2,1)S(1)}) custom-call(bf16[1024,512]{1,0:T(8,128)(2,1)S(1)} %get-tuple-element.21.enc_ref, bf16[512,2048]{1,0:T(8,128)(2,1)S(1)} %get-tuple-element.22.first, bf16[2048,512]{1,0:T(8,128)(2,1)} %second_hbm.3, bf16[1040,128]{1,0:T(8,128)(2,1)S(1)} %outgoing_sums.1.after), custom_call_target="tpu_custom_call" | custom-call | flops 2147483648 | bytes 3145728 | tf_op jit(solution)/shard_map/grid_hidden/pallas_call | solution.py:383
  17.8 1.8 %collective-permute-done.1.arrived_ref.sums_ref = bf16[1040,128]{1,0:T(8,128)(2,1)S(1)} collective-permute-done((bf16[1040,128]{1,0:T(8,128)(2,1)S(1)}, bf16[1040,128]{1,0:T(8,128)(2,1)S(1)}, u32[]{:S(2)}, u32[]{:S(2)}) %collective-permute-start.1) | collective-permute-done | bytes 266272 | tf_op jit(solution)/shard_map/ppermute | solution.py:34
  19.7 0.0 copy-start.3
  19.7 0.1 chip_share.1
  19.8 0.0 copy-start.1
  19.8 0.1 collective-permute-start.2
  19.9 1.5 %collective-permute-done.2.other_ref = bf16[256,512]{1,0:T(8,128)(2,1)S(1)} collective-permute-done((bf16[256,512]{1,0:T(8,128)(2,1)S(1)}, bf16[256,512]{1,0:T(8,128)(2,1)S(1)}, u32[]{:S(2)}, u32[]{:S(2)}) %collective-permute-start.2) | collective-permute-done | bytes 262176 | tf_op jit(solution)/shard_map/ppermute | solution.py:25
  21.4 0.1 chip_states.1
  21.5 5.3 %collective-permute-start.3 = (bf16[256,512]{1,0:T(8,128)(2,1)S(1)}, bf16[256,512]{1,0:T(8,128)(2,1)S(1)}, u32[]{:S(2)}, u32[]{:S(2)}) collective-permute-start(bf16[256,512]{1,0:T(8,128)(2,1)S(1)} %get-tuple-element.28), channel_id=1, source_target_pairs={{0,31},{1,2},{2,1},{3,4},{4,3},{5,6},{6,5},{7,8},{8,7},{9,10},{10,... | collective-permute-start | bytes 786440 | tf_op jit(solution)/shard_map/ppermute | solution.py:34
  26.8 0.3 collective-permute-start.5
  27.1 4.0 %collective-permute-done.3.near_ref = bf16[256,512]{1,0:T(8,128)(2,1)S(1)} collective-permute-done((bf16[256,512]{1,0:T(8,128)(2,1)S(1)}, bf16[256,512]{1,0:T(8,128)(2,1)S(1)}, u32[]{:S(2)}, u32[]{:S(2)}) %collective-permute-start.3) | collective-permute-done | bytes 262176 | tf_op jit(solution)/shard_map/ppermute | solution.py:34
  31.1 0.1 collective-permute-start.4
  31.1 0.0 copy-done
  31.1 0.0 copy-done.3
  31.2 1.0 %project.1 = (bf16[384,512]{1,0:T(8,128)(2,1)S(1)}, bf16[512,1024]{1,0:T(8,128)(2,1)S(1)}) custom-call(bf16[256,512]{1,0:T(8,128)(2,1)S(1)} %get-tuple-element.27.pair_ref, bf16[256,512]{1,0:T(8,128)(2,1)S(1)} %collective-permute-done.3.near_ref, f32[1,512]{1,0:T(1,128)S(1)} %copy-done.3, bf16[512,1536]{1,0:T(8,128)(2,1)S(1)} %bitcast.4), custom_call_target="tpu_custom_call" | custom-call | flops 738197504 | bytes 131072 | tf_op jit(solution)/shard_map/project/pallas_call | solution.py:255
  32.1 0.3 collective-permute-done.4.behind_ref
  32.5 0.0 copy-done.1
  32.5 1.2 %attend_own.1.after.ring_own = bf16[128,512]{1,0:T(8,128)(2,1)S(1)} custom-call(bf16[1040,128]{1,0:T(8,128)(2,1)S(1)} %get-tuple-element.18.base_ref, f32[128,512]{1,0:T(8,128)S(1)} %get-tuple-element.26.own_ref, bf16[384,512]{1,0:T(8,128)(2,1)S(1)} %get-tuple-element.29.query_ref, bf16[512,1024]{1,0:T(8,128)(2,1)S(1)} %get-tuple-element.30.kv_ref, ...), custom_call_target="tpu_custom_call" | custom-call | flops 671088640 | bytes 131072 | tf_op jit(solution)/shard_map/attend_own/pallas_call | solution.py:333
  33.7 0.3 collective-permute-start.6
  34.0 1.3 %collective-permute-done.5.far_ref = bf16[256,512]{1,0:T(8,128)(2,1)S(1)} collective-permute-done((bf16[256,512]{1,0:T(8,128)(2,1)S(1)}, bf16[256,512]{1,0:T(8,128)(2,1)S(1)}, u32[]{:S(2)}, u32[]{:S(2)}) %collective-permute-start.5) | collective-permute-done | bytes 262176 | tf_op jit(solution)/shard_map/ppermute | solution.py:34
  35.3 1.8 %attend_near.1.ring_near = bf16[256,512]{1,0:T(8,128)(2,1)S(1)} custom-call(bf16[1040,128]{1,0:T(8,128)(2,1)S(1)} %collective-permute-done.1.arrived_ref.sums_ref, bf16[256,512]{1,0:T(8,128)(2,1)S(1)} %collective-permute-done.3.near_ref, bf16[384,512]{1,0:T(8,128)(2,1)S(1)} %get-tuple-element.29.query_ref, bf16[512,1024]{1,0:T(8,128)(2,1)S(1)} %get-tuple-element.30.kv_ref, ...), custom_call_target="tpu_custom_call" | custom-call | flops 1342177280 | bytes 131072 | tf_op jit(solution)/shard_map/attend_near/pallas_call | solution.py:349
  37.1 0.0 copy-start.2
  37.1 0.1 collective-permute-start.7
  37.2 0.0 collective-permute-done.6.back_own
  37.2 1.3 %mesh_hidden.1.mesh_in = bf16[640,2048]{1,0:T(8,128)(2,1)S(1)} custom-call(bf16[128,512]{1,0:T(8,128)(2,1)S(1)} %collective-permute-done.6.back_own, bf16[128,512]{1,0:T(8,128)(2,1)S(1)} %attend_own.1.after.ring_own, bf16[256,512]{1,0:T(8,128)(2,1)S(1)} %attend_near.1.ring_near, bf16[512,2048]{1,0:T(8,128)(2,1)S(1)} %get-tuple-element.22.first), custom_call_target="tpu_custom_call" | custom-call | flops 1073741824 | bytes 131072 | tf_op jit(solution)/shard_map/mesh_hidden/pallas_call | solution.py:406
  38.5 0.0 collective-permute-done.7.back_near
  38.6 0.0 copy-done.2
  38.6 4.0 %decode.1 = (bf16[1024,512]{1,0:T(8,128)(2,1)}, bf16[128,512]{1,0:T(8,128)(2,1)}, bf16[640,2048]{1,0:T(8,128)(2,1)S(1)}) custom-call(s32[8]{0:T(128)} %owner_hbm.3, f32[8,128]{1,0:T(8,128)S(1)} %bitcast.9, bf16[128,512]{1,0:T(8,128)(2,1)S(1)} %attend_own.1.after.ring_own, ...), custom_call_target="tpu_custom_call", output_to_operand_aliasing={{2}: (7, {})} | custom-call | flops 2147483648 | bytes 6291456 | tf_op jit(solution)/shard_map/decode/pallas_call | solution.py:471
  (4 shorter events, 0.1 us)
Async XLA Ops:
  7.2 1.5 %collective-permute-start = (bf16[528,128]{1,0:T(8,128)(2,1)S(1)}, bf16[528,128]{1,0:T(8,128)(2,1)S(1)}, u32[]{:S(2)}, u32[]{:S(2)}) collective-permute-start(bf16[528,128]{1,0:T(8,128)(2,1)S(1)} %get-tuple-element.20), channel_id=1, source_target_pairs={{0,1},{1,0},{2,3},{3,2},{4,5},{5,4},{6,7},{7,6},{8,9},{9,8},{10,11... | collective-permute-start | bytes 405512 | tf_op jit(solution)/shard_map/ppermute | solution.py:25
  8.8 10.9 %collective-permute-start.1 = (bf16[1040,128]{1,0:T(8,128)(2,1)S(1)}, bf16[1040,128]{1,0:T(8,128)(2,1)S(1)}, u32[]{:S(2)}, u32[]{:S(2)}) collective-permute-start(bf16[1040,128]{1,0:T(8,128)(2,1)S(1)} %outgoing_sums.1.after), channel_id=1, source_target_pairs={{0,31},{1,2},{2,1},{3,4},{4,3},{5,6},{6,5},{7,8},{8,7},{9,10},{10,... | collective-permute-start | bytes 798728 | tf_op jit(solution)/shard_map/ppermute | solution.py:34
  19.7 11.5 %copy-start = (bf16[1,512,1536]{2,1,0:T(8,128)(2,1)S(1)}, bf16[1,512,1536]{2,1,0:T(8,128)(2,1)}, u32[]{:S(2)}) copy-start(bf16[1,512,1536]{2,1,0:T(8,128)(2,1)} %param.24) | copy-start | bytes 4718596
  19.7 11.5 %copy-start.3 = (f32[1,512]{1,0:T(1,128)S(1)}, f32[1,512]{1,0:T(1,128)}, u32[]{:S(2)}) copy-start(f32[1,512]{1,0:T(1,128)} %gain_ref.5) | copy-start | bytes 6148
  19.8 12.7 %copy-start.1 = (bf16[1,512,512]{2,1,0:T(8,128)(2,1)S(1)}, bf16[1,512,512]{2,1,0:T(8,128)(2,1)}, u32[]{:S(2)}) copy-start(bf16[1,512,512]{2,1,0:T(8,128)(2,1)} %param.25) | copy-start | bytes 1572868
  19.8 1.6 %collective-permute-start.2 = (bf16[256,512]{1,0:T(8,128)(2,1)S(1)}, bf16[256,512]{1,0:T(8,128)(2,1)S(1)}, u32[]{:S(2)}, u32[]{:S(2)}) collective-permute-start(bf16[256,512]{1,0:T(8,128)(2,1)S(1)} %get-tuple-element.25), channel_id=1, source_target_pairs={{0,1},{1,0},{2,3},{3,2},{4,5},{5,4},{6,7},{7,6},{8,9},{9,8},{10,11... | collective-permute-start | bytes 786440 | tf_op jit(solution)/shard_map/ppermute | solution.py:25
  21.5 9.6 %collective-permute-start.3 = (bf16[256,512]{1,0:T(8,128)(2,1)S(1)}, bf16[256,512]{1,0:T(8,128)(2,1)S(1)}, u32[]{:S(2)}, u32[]{:S(2)}) collective-permute-start(bf16[256,512]{1,0:T(8,128)(2,1)S(1)} %get-tuple-element.28), channel_id=1, source_target_pairs={{0,31},{1,2},{2,1},{3,4},{4,3},{5,6},{6,5},{7,8},{8,7},{9,10},{10,... | collective-permute-start | bytes 786440 | tf_op jit(solution)/shard_map/ppermute | solution.py:34
  26.8 8.5 %collective-permute-start.5 = (bf16[256,512]{1,0:T(8,128)(2,1)S(1)}, bf16[256,512]{1,0:T(8,128)(2,1)S(1)}, u32[]{:S(2)}, u32[]{:S(2)}) collective-permute-start(bf16[256,512]{1,0:T(8,128)(2,1)S(1)} %get-tuple-element.28), channel_id=1, source_target_pairs={{0,29},{1,4},{2,31},{3,6},{4,1},{5,8},{6,3},{7,10},{8,5},{9,12},{1... | collective-permute-start | bytes 786440 | tf_op jit(solution)/shard_map/ppermute | solution.py:34
  31.1 1.4 %collective-permute-start.4 = (bf16[128,512]{1,0:T(8,128)(2,1)S(1)}, bf16[128,512]{1,0:T(8,128)(2,1)S(1)}, u32[]{:S(2)}, u32[]{:S(2)}) collective-permute-start(bf16[128,512]{1,0:T(8,128)(2,1)S(1)} %slice.8), channel_id=1, source_target_pairs={{0,1},{1,0},{2,3},{3,2},{4,5},{5,4},{6,7},{7,6},{8,9},{9,8},{10,11... | collective-permute-start | bytes 393224 | tf_op jit(solution)/shard_map/ppermute | solution.py:25
  33.7 3.5 %collective-permute-start.6 = (bf16[128,512]{1,0:T(8,128)(2,1)S(1)}, bf16[128,512]{1,0:T(8,128)(2,1)S(1)}, u32[]{:S(2)}, u32[]{:S(2)}) collective-permute-start(bf16[128,512]{1,0:T(8,128)(2,1)S(1)} %attend_own.1.after.ring_own), channel_id=1, source_target_pairs={{0,1},{1,0},{2,3},{3,2},{4,5},{5,4},{6,7},{7,6},{8,9},{9,8},{10,11... | collective-permute-start | bytes 393224 | tf_op jit(solution)/shard_map/ppermute | solution.py:25
  37.1 1.4 %copy-start.2 = (f32[1024]{0:T(1024)S(1)}, f32[1024]{0:T(1024)}, u32[]{:S(2)}) copy-start(f32[1024]{0:T(1024)} %param.18) | copy-start | bytes 12292
  37.1 1.4 %collective-permute-start.7 = (bf16[128,512]{1,0:T(8,128)(2,1)S(1)}, bf16[128,512]{1,0:T(8,128)(2,1)S(1)}, u32[]{:S(2)}, u32[]{:S(2)}) collective-permute-start(bf16[128,512]{1,0:T(8,128)(2,1)S(1)} %slice.9), channel_id=1, source_target_pairs={{0,1},{1,0},{2,3},{3,2},{4,5},{5,4},{6,7},{7,6},{8,9},{9,8},{10,11... | collective-permute-start | bytes 393224 | tf_op jit(solution)/shard_map/ppermute | solution.py:25

commit v10 on v9

--- a/solution.py
+++ b/solution.py
@@ -266,32 +266,35 @@
     )(pair, near, gain, w_qkv)
 
 
-def attention(query, window, keep):
-    depth = query.shape[1]
-    every = [slice(h * HD, (h + 1) * HD) for h in range(depth // HD)]
+def attention(items):
+    units = [
+        (n, slice(h * HD, (h + 1) * HD)) for n, (query, _, _) in enumerate(items) for h in range(query.shape[1] // HD)
+    ]
     scores = [
         jnp.concatenate([
             lax.dot_general(
-                query[:, cols], ref[first:first + size, cols], (((1,), (1,)), ((), ())), preferred_element_type=F32
+                items[n][0][:, cols], ref[first:first + size, cols], (((1,), (1,)), ((), ())), preferred_element_type=F32
             )
-            for ref, first, size in window
+            for ref, first, size in items[n][1]
         ], axis=1)
-        for cols in every
+        for n, cols in units
     ]
-    scores = [jnp.where(keep, score, -jnp.inf) for score in scores]
+    scores = [jnp.where(items[n][2], score, -jnp.inf) for (n, _), score in zip(units, scores)]
     below = [(score - jnp.max(score, axis=-1, keepdims=True)) * (HD ** -0.5 * LOG2E) for score in scores]
     grown = [jnp.exp2(score.astype(BF16)) for score in below]
-    heads = []
-    for h, cols in enumerate(every):
+    heads = [[] for _ in items]
+    for (n, cols), weights in zip(units, grown):
+        query, window, _ = items[n]
+        depth = query.shape[1]
         start, taken = 0, None
         for ref, first, size in window:
             value = ref[first:first + size, depth + cols.start:depth + cols.stop]
             value = jnp.concatenate([value, jnp.ones((size, HD), BF16)], axis=1)
-            term = jnp.dot(grown[h][:, start:start + size], value, preferred_element_type=F32)
+            term = jnp.dot(weights[:, start:start + size], value, preferred_element_type=F32)
             taken = term if taken is None else taken + term
             start += size
-        heads.append((taken[:, :HD] / taken[:, HD:]).astype(BF16))
-    return jnp.concatenate(heads, axis=1)
+        heads[n].append((taken[:, :HD] / taken[:, HD:]).astype(BF16))
+    return [jnp.concatenate(parts, axis=1) for parts in heads]
 
 
 def kept_lanes(rows, absent):
@@ -305,7 +308,7 @@
         normal(behind_ref[...], gain_ref[...]), w_qkv[:, depth:], preferred_element_type=F32
     ).astype(BF16)
     keep = kept_lanes(rows, base_ref[2 * rows * depth // LANES:, :].astype(F32)[0:1, 0:1])
-    mixed = attention(query_ref[:rows, :], [(kv_behind, 0, rows), (kv_ref, 0, 4 * rows)], keep)
+    mixed = attention([(query_ref[:rows, :], [(kv_behind, 0, rows), (kv_ref, 0, 4 * rows)], keep)])[0]
     ring_ref[...] = (own_ref[...] + jnp.dot(mixed, w_out[...], preferred_element_type=F32)).astype(BF16)
 
 
@@ -321,9 +324,12 @@
         [(kv_ref, 0, 4 * rows), (kv_far, 0, rows)],
         [(kv_ref, rows, 3 * rows), (kv_far, 0, 2 * rows)],
     ]
+    items = []
     for n, window in enumerate(windows):
         keep = kept_lanes(rows, sums_ref[2 * rows * depth // LANES:, :].astype(F32)[0:1, n:n + 1])
-        mixed[n * rows:(n + 1) * rows, :] = attention(query_ref[(n + 1) * rows:(n + 2) * rows, :], window, keep)
+        items.append((query_ref[(n + 1) * rows:(n + 2) * rows, :], window, keep))
+    for n, block in enumerate(attention(items)):
+        mixed[n * rows:(n + 1) * rows, :] = block
     added = jnp.dot(mixed[...], w_out[...], preferred_element_type=F32)
     ring_ref[...] = (near_ref[...].astype(F32) + added).astype(BF16)
 

time: 42.8 us -> 42.6 us (level)
  no operation moved by 1% of the time
where the time goes in v10:
time: 42.6 us; the launch traced here: 42.5 us
  Pallas kernels  18.4 us (43%)
  starting transfers between devices  13.3 us (31%)
  waiting for transfers between devices  9.98 us (23%)
  between operations  0.77 us (2%)
    ppermute x3, starting transfers between devices, from_outward(): return lax.ppermute(block, AXES, route)  12.3 us
    ppermute x3, waiting for transfers between devices, from_outward(): return lax.ppermute(block, AXES, route)  7.1 us
    pallas_call x1, Pallas kernels, encode(): pl.pallas_call(encode_kernel, out_shape=(kept((cells, depth)), kept((rows...  6.59 us
    pallas_call x1, Pallas kernels, decode(): pl.pallas_call(decode_kernel, out_shape=(jax.ShapeDtypeStruct((cells, dep...  4.04 us
    ppermute x5, waiting for transfers between devices, swapped(): return lax.ppermute(block, AXES, [(i, i ^ 1) for i in range(count)])  2.87 us
    pallas_call x1, Pallas kernels, grid_hidden(): pl.pallas_call(grid_hidden_kernel, out_shape=(kept((cells, hidden)), kept...  2.36 us
    pallas_call x1, Pallas kernels, attend_near(): pl.pallas_call(attend_near_kernel, out_shape=kept((2 * rows, depth)), in_...  1.71 us
    pallas_call x1, Pallas kernels, mesh_hidden(): pl.pallas_call(mesh_hidden_kernel, out_shape=kept(((2 * REACH + 1) * rows...  1.27 us
  transfers between devices with their start and end apart: 8, of which 6 were waited for; matrix products, arithmetic and copies ran while one was open for 0% of the time, Pallas kernels for 18%

profile of v10, /device:TPU:0, one launch (start us, length us, event | category | flops | bytes accessed | tf_op | source)
XLA Modules:
  0.0 42.5 jit_solution(1196852535593223520)
XLA Ops:
  0.6 6.6 %encode.1 = (bf16[1024,512]{1,0:T(8,128)(2,1)S(1)}, bf16[528,128]{1,0:T(8,128)(2,1)S(1)}, bf16[1040,128]{1,0:T(8,128)(2,1)S(1)}, f32[256,512]{1,0:T(8,128)S(1)}, bf16[512,2048]{1,0:T(8,128)(2,1)S(1)}) custom-call(s32[8]{0:T(128)} %owner_hbm.2, s32[1,3]{1,0:T(1,128)} %listed_hbm.1, f32[8,128]{1,0:T(8,128)} %bitcast.10, bf16[128,512]{1,0:T(8,128)(2,1)} %feat_hbm.1, ...), custom_call_target="tpu_custom_call" | custom-call | flops 4294967296 | bytes 6291456 | tf_op jit(solution)/shard_map/encode/pallas_call | solution.py:150
  7.2 0.5 %collective-permute-start = (bf16[528,128]{1,0:T(8,128)(2,1)S(1)}, bf16[528,128]{1,0:T(8,128)(2,1)S(1)}, u32[]{:S(2)}, u32[]{:S(2)}) collective-permute-start(bf16[528,128]{1,0:T(8,128)(2,1)S(1)} %get-tuple-element.20), channel_id=1, source_target_pairs={{0,1},{1,0},{2,3},{3,2},{4,5},{5,4},{6,7},{7,6},{8,9},{9,8},{10,11... | collective-permute-start | bytes 405512 | tf_op jit(solution)/shard_map/ppermute | solution.py:25
  7.7 1.0 %collective-permute-done.arrived_ref = bf16[528,128]{1,0:T(8,128)(2,1)S(1)} collective-permute-done((bf16[528,128]{1,0:T(8,128)(2,1)S(1)}, bf16[528,128]{1,0:T(8,128)(2,1)S(1)}, u32[]{:S(2)}, u32[]{:S(2)}) %collective-permute-start) | collective-permute-done | bytes 135200 | tf_op jit(solution)/shard_map/ppermute | solution.py:25
  8.8 6.7 %collective-permute-start.1 = (bf16[1040,128]{1,0:T(8,128)(2,1)S(1)}, bf16[1040,128]{1,0:T(8,128)(2,1)S(1)}, u32[]{:S(2)}, u32[]{:S(2)}) collective-permute-start(bf16[1040,128]{1,0:T(8,128)(2,1)S(1)} %outgoing_sums.1.after), channel_id=1, source_target_pairs={{0,31},{1,2},{2,1},{3,4},{4,3},{5,6},{6,5},{7,8},{8,7},{9,10},{10,... | collective-permute-start | bytes 798728 | tf_op jit(solution)/shard_map/ppermute | solution.py:34
  15.4 2.4 %grid_hidden.1 = (bf16[1024,2048]{1,0:T(8,128)(2,1)S(1)}, bf16[2048,512]{1,0:T(8,128)(2,1)S(1)}) custom-call(bf16[1024,512]{1,0:T(8,128)(2,1)S(1)} %get-tuple-element.21.enc_ref, bf16[512,2048]{1,0:T(8,128)(2,1)S(1)} %get-tuple-element.22.first, bf16[2048,512]{1,0:T(8,128)(2,1)} %second_hbm.3, bf16[1040,128]{1,0:T(8,128)(2,1)S(1)} %outgoing_sums.1.after), custom_call_target="tpu_custom_call" | custom-call | flops 2147483648 | bytes 3145728 | tf_op jit(solution)/shard_map/grid_hidden/pallas_call | solution.py:389
  17.8 1.8 %collective-permute-done.1.arrived_ref.sums_ref = bf16[1040,128]{1,0:T(8,128)(2,1)S(1)} collective-permute-done((bf16[1040,128]{1,0:T(8,128)(2,1)S(1)}, bf16[1040,128]{1,0:T(8,128)(2,1)S(1)}, u32[]{:S(2)}, u32[]{:S(2)}) %collective-permute-start.1) | collective-permute-done | bytes 266272 | tf_op jit(solution)/shard_map/ppermute | solution.py:34
  19.7 0.0 copy-start
  19.7 0.1 chip_share.1
  19.8 0.0 copy-start.1
  19.8 0.1 collective-permute-start.2
  19.9 1.5 %collective-permute-done.2.other_ref = bf16[256,512]{1,0:T(8,128)(2,1)S(1)} collective-permute-done((bf16[256,512]{1,0:T(8,128)(2,1)S(1)}, bf16[256,512]{1,0:T(8,128)(2,1)S(1)}, u32[]{:S(2)}, u32[]{:S(2)}) %collective-permute-start.2) | collective-permute-done | bytes 262176 | tf_op jit(solution)/shard_map/ppermute | solution.py:25
  21.4 0.1 chip_states.1
  21.5 5.3 %collective-permute-start.3 = (bf16[256,512]{1,0:T(8,128)(2,1)S(1)}, bf16[256,512]{1,0:T(8,128)(2,1)S(1)}, u32[]{:S(2)}, u32[]{:S(2)}) collective-permute-start(bf16[256,512]{1,0:T(8,128)(2,1)S(1)} %get-tuple-element.28), channel_id=1, source_target_pairs={{0,31},{1,2},{2,1},{3,4},{4,3},{5,6},{6,5},{7,8},{8,7},{9,10},{10,... | collective-permute-start | bytes 786440 | tf_op jit(solution)/shard_map/ppermute | solution.py:34
  26.8 0.3 collective-permute-start.5
  27.1 4.0 %collective-permute-done.3.near_ref = bf16[256,512]{1,0:T(8,128)(2,1)S(1)} collective-permute-done((bf16[256,512]{1,0:T(8,128)(2,1)S(1)}, bf16[256,512]{1,0:T(8,128)(2,1)S(1)}, u32[]{:S(2)}, u32[]{:S(2)}) %collective-permute-start.3) | collective-permute-done | bytes 262176 | tf_op jit(solution)/shard_map/ppermute | solution.py:34
  31.1 0.1 collective-permute-start.4
  31.1 0.0 copy-done
  31.1 0.0 copy-done.3
  31.2 1.0 %project.1 = (bf16[384,512]{1,0:T(8,128)(2,1)S(1)}, bf16[512,1024]{1,0:T(8,128)(2,1)S(1)}) custom-call(bf16[256,512]{1,0:T(8,128)(2,1)S(1)} %get-tuple-element.27.pair_ref, bf16[256,512]{1,0:T(8,128)(2,1)S(1)} %collective-permute-done.3.near_ref, f32[1,512]{1,0:T(1,128)S(1)} %copy-done.3, bf16[512,1536]{1,0:T(8,128)(2,1)S(1)} %bitcast.4), custom_call_target="tpu_custom_call" | custom-call | flops 738197504 | bytes 131072 | tf_op jit(solution)/shard_map/project/pallas_call | solution.py:255
  32.1 0.3 collective-permute-done.4.behind_ref
  32.5 0.0 copy-done.1
  32.5 1.2 %attend_own.1.after.ring_own = bf16[128,512]{1,0:T(8,128)(2,1)S(1)} custom-call(bf16[1040,128]{1,0:T(8,128)(2,1)S(1)} %get-tuple-element.18.base_ref, f32[128,512]{1,0:T(8,128)S(1)} %get-tuple-element.26.own_ref, bf16[384,512]{1,0:T(8,128)(2,1)S(1)} %get-tuple-element.29.query_ref, bf16[512,1024]{1,0:T(8,128)(2,1)S(1)} %get-tuple-element.30.kv_ref, ...), custom_call_target="tpu_custom_call" | custom-call | flops 671088640 | bytes 131072 | tf_op jit(solution)/shard_map/attend_own/pallas_call | solution.py:339
  33.7 0.3 collective-permute-start.6
  34.0 1.3 %collective-permute-done.5.far_ref = bf16[256,512]{1,0:T(8,128)(2,1)S(1)} collective-permute-done((bf16[256,512]{1,0:T(8,128)(2,1)S(1)}, bf16[256,512]{1,0:T(8,128)(2,1)S(1)}, u32[]{:S(2)}, u32[]{:S(2)}) %collective-permute-start.5) | collective-permute-done | bytes 262176 | tf_op jit(solution)/shard_map/ppermute | solution.py:34
  35.3 1.7 %attend_near.1.ring_near = bf16[256,512]{1,0:T(8,128)(2,1)S(1)} custom-call(bf16[1040,128]{1,0:T(8,128)(2,1)S(1)} %collective-permute-done.1.arrived_ref.sums_ref, bf16[256,512]{1,0:T(8,128)(2,1)S(1)} %collective-permute-done.3.near_ref, bf16[384,512]{1,0:T(8,128)(2,1)S(1)} %get-tuple-element.29.query_ref, bf16[512,1024]{1,0:T(8,128)(2,1)S(1)} %get-tuple-element.30.kv_ref, ...), custom_call_target="tpu_custom_call" | custom-call | flops 1342177280 | bytes 131072 | tf_op jit(solution)/shard_map/attend_near/pallas_call | solution.py:355
  37.0 0.0 copy-start.2
  37.0 0.1 collective-permute-start.7
  37.1 0.0 collective-permute-done.6.back_own
  37.1 1.3 %mesh_hidden.1.mesh_in = bf16[640,2048]{1,0:T(8,128)(2,1)S(1)} custom-call(bf16[128,512]{1,0:T(8,128)(2,1)S(1)} %collective-permute-done.6.back_own, bf16[128,512]{1,0:T(8,128)(2,1)S(1)} %attend_own.1.after.ring_own, bf16[256,512]{1,0:T(8,128)(2,1)S(1)} %attend_near.1.ring_near, bf16[512,2048]{1,0:T(8,128)(2,1)S(1)} %get-tuple-element.22.first), custom_call_target="tpu_custom_call" | custom-call | flops 1073741824 | bytes 131072 | tf_op jit(solution)/shard_map/mesh_hidden/pallas_call | solution.py:412
  38.4 0.0 collective-permute-done.7.back_near
  38.4 0.0 copy-done.2
  38.4 4.0 %decode.1 = (bf16[1024,512]{1,0:T(8,128)(2,1)}, bf16[128,512]{1,0:T(8,128)(2,1)}, bf16[640,2048]{1,0:T(8,128)(2,1)S(1)}) custom-call(s32[8]{0:T(128)} %owner_hbm.3, f32[8,128]{1,0:T(8,128)S(1)} %bitcast.9, bf16[128,512]{1,0:T(8,128)(2,1)S(1)} %attend_own.1.after.ring_own, ...), custom_call_target="tpu_custom_call", output_to_operand_aliasing={{2}: (7, {})} | custom-call | flops 2147483648 | bytes 6291456 | tf_op jit(solution)/shard_map/decode/pallas_call | solution.py:477
  (4 shorter events, 0.1 us)
Async XLA Ops:
  7.2 1.5 %collective-permute-start = (bf16[528,128]{1,0:T(8,128)(2,1)S(1)}, bf16[528,128]{1,0:T(8,128)(2,1)S(1)}, u32[]{:S(2)}, u32[]{:S(2)}) collective-permute-start(bf16[528,128]{1,0:T(8,128)(2,1)S(1)} %get-tuple-element.20), channel_id=1, source_target_pairs={{0,1},{1,0},{2,3},{3,2},{4,5},{5,4},{6,7},{7,6},{8,9},{9,8},{10,11... | collective-permute-start | bytes 405512 | tf_op jit(solution)/shard_map/ppermute | solution.py:25
  8.8 10.9 %collective-permute-start.1 = (bf16[1040,128]{1,0:T(8,128)(2,1)S(1)}, bf16[1040,128]{1,0:T(8,128)(2,1)S(1)}, u32[]{:S(2)}, u32[]{:S(2)}) collective-permute-start(bf16[1040,128]{1,0:T(8,128)(2,1)S(1)} %outgoing_sums.1.after), channel_id=1, source_target_pairs={{0,31},{1,2},{2,1},{3,4},{4,3},{5,6},{6,5},{7,8},{8,7},{9,10},{10,... | collective-permute-start | bytes 798728 | tf_op jit(solution)/shard_map/ppermute | solution.py:34
  19.7 11.5 %copy-start = (bf16[1,512,1536]{2,1,0:T(8,128)(2,1)S(1)}, bf16[1,512,1536]{2,1,0:T(8,128)(2,1)}, u32[]{:S(2)}) copy-start(bf16[1,512,1536]{2,1,0:T(8,128)(2,1)} %param.24) | copy-start | bytes 4718596
  19.7 11.5 %copy-start.3 = (f32[1,512]{1,0:T(1,128)S(1)}, f32[1,512]{1,0:T(1,128)}, u32[]{:S(2)}) copy-start(f32[1,512]{1,0:T(1,128)} %gain_ref.5) | copy-start | bytes 6148
  19.8 12.7 %copy-start.1 = (bf16[1,512,512]{2,1,0:T(8,128)(2,1)S(1)}, bf16[1,512,512]{2,1,0:T(8,128)(2,1)}, u32[]{:S(2)}) copy-start(bf16[1,512,512]{2,1,0:T(8,128)(2,1)} %param.25) | copy-start | bytes 1572868
  19.8 1.6 %collective-permute-start.2 = (bf16[256,512]{1,0:T(8,128)(2,1)S(1)}, bf16[256,512]{1,0:T(8,128)(2,1)S(1)}, u32[]{:S(2)}, u32[]{:S(2)}) collective-permute-start(bf16[256,512]{1,0:T(8,128)(2,1)S(1)} %get-tuple-element.25), channel_id=1, source_target_pairs={{0,1},{1,0},{2,3},{3,2},{4,5},{5,4},{6,7},{7,6},{8,9},{9,8},{10,11... | collective-permute-start | bytes 786440 | tf_op jit(solution)/shard_map/ppermute | solution.py:25
  21.5 9.6 %collective-permute-start.3 = (bf16[256,512]{1,0:T(8,128)(2,1)S(1)}, bf16[256,512]{1,0:T(8,128)(2,1)S(1)}, u32[]{:S(2)}, u32[]{:S(2)}) collective-permute-start(bf16[256,512]{1,0:T(8,128)(2,1)S(1)} %get-tuple-element.28), channel_id=1, source_target_pairs={{0,31},{1,2},{2,1},{3,4},{4,3},{5,6},{6,5},{7,8},{8,7},{9,10},{10,... | collective-permute-start | bytes 786440 | tf_op jit(solution)/shard_map/ppermute | solution.py:34
  26.8 8.5 %collective-permute-start.5 = (bf16[256,512]{1,0:T(8,128)(2,1)S(1)}, bf16[256,512]{1,0:T(8,128)(2,1)S(1)}, u32[]{:S(2)}, u32[]{:S(2)}) collective-permute-start(bf16[256,512]{1,0:T(8,128)(2,1)S(1)} %get-tuple-element.28), channel_id=1, source_target_pairs={{0,29},{1,4},{2,31},{3,6},{4,1},{5,8},{6,3},{7,10},{8,5},{9,12},{1... | collective-permute-start | bytes 786440 | tf_op jit(solution)/shard_map/ppermute | solution.py:34
  31.1 1.4 %collective-permute-start.4 = (bf16[128,512]{1,0:T(8,128)(2,1)S(1)}, bf16[128,512]{1,0:T(8,128)(2,1)S(1)}, u32[]{:S(2)}, u32[]{:S(2)}) collective-permute-start(bf16[128,512]{1,0:T(8,128)(2,1)S(1)} %slice.8), channel_id=1, source_target_pairs={{0,1},{1,0},{2,3},{3,2},{4,5},{5,4},{6,7},{7,6},{8,9},{9,8},{10,11... | collective-permute-start | bytes 393224 | tf_op jit(solution)/shard_map/ppermute | solution.py:25
  33.7 3.4 %collective-permute-start.6 = (bf16[128,512]{1,0:T(8,128)(2,1)S(1)}, bf16[128,512]{1,0:T(8,128)(2,1)S(1)}, u32[]{:S(2)}, u32[]{:S(2)}) collective-permute-start(bf16[128,512]{1,0:T(8,128)(2,1)S(1)} %attend_own.1.after.ring_own), channel_id=1, source_target_pairs={{0,1},{1,0},{2,3},{3,2},{4,5},{5,4},{6,7},{7,6},{8,9},{9,8},{10,11... | collective-permute-start | bytes 393224 | tf_op jit(solution)/shard_map/ppermute | solution.py:25
  37.0 1.4 %copy-start.2 = (f32[1024]{0:T(1024)S(1)}, f32[1024]{0:T(1024)}, u32[]{:S(2)}) copy-start(f32[1024]{0:T(1024)} %param.18) | copy-start | bytes 12292
  37.0 1.4 %collective-permute-start.7 = (bf16[128,512]{1,0:T(8,128)(2,1)S(1)}, bf16[128,512]{1,0:T(8,128)(2,1)S(1)}, u32[]{:S(2)}, u32[]{:S(2)}) collective-permute-start(bf16[128,512]{1,0:T(8,128)(2,1)S(1)} %slice.9), channel_id=1, source_target_pairs={{0,1},{1,0},{2,3},{3,2},{4,5},{5,4},{6,7},{7,6},{8,9},{9,8},{10,11... | collective-permute-start | bytes 393224 | tf_op jit(solution)/shard_map/ppermute | solution.py:25

commit v11 on v10

--- a/solution.py
+++ b/solution.py
@@ -121,7 +121,7 @@
 
     hidden_layer(enc_ref, first, act, tile, part, arrive, before)
     columns = jnp.transpose(weight_ref[...])
-    tile = min(tile, 256)
+    tile = min(tile, 512)
     for r in range(enc_ref.shape[0] // tile):
         cut = slice(r * tile, (r + 1) * tile)
         out = enc_ref[cut, :].astype(F32) + jnp.dot(act[cut, :], second[...], preferred_element_type=F32)

time: 42.6 us -> 42.6 us (level)
  no operation moved by 1% of the time
where the time goes in v11:
time: 42.6 us; the launch traced here: 42.4 us
  Pallas kernels  18.4 us (43%)
  starting transfers between devices  13.2 us (31%)
  waiting for transfers between devices  9.98 us (23%)
  between operations  0.77 us (2%)
    ppermute x3, starting transfers between devices, from_outward(): return lax.ppermute(block, AXES, route)  12.3 us
    ppermute x3, waiting for transfers between devices, from_outward(): return lax.ppermute(block, AXES, route)  7.11 us
    pallas_call x1, Pallas kernels, encode(): pl.pallas_call(encode_kernel, out_shape=(kept((cells, depth)), kept((rows...  6.56 us
    pallas_call x1, Pallas kernels, decode(): pl.pallas_call(decode_kernel, out_shape=(jax.ShapeDtypeStruct((cells, dep...  4.02 us
    ppermute x5, waiting for transfers between devices, swapped(): return lax.ppermute(block, AXES, [(i, i ^ 1) for i in range(count)])  2.87 us
    pallas_call x1, Pallas kernels, grid_hidden(): pl.pallas_call(grid_hidden_kernel, out_shape=(kept((cells, hidden)), kept...  2.36 us
    pallas_call x1, Pallas kernels, attend_near(): pl.pallas_call(attend_near_kernel, out_shape=kept((2 * rows, depth)), in_...  1.72 us
    pallas_call x1, Pallas kernels, mesh_hidden(): pl.pallas_call(mesh_hidden_kernel, out_shape=kept(((2 * REACH + 1) * rows...  1.28 us
  transfers between devices with their start and end apart: 8, of which 6 were waited for; matrix products, arithmetic and copies ran while one was open for 0% of the time, Pallas kernels for 18%

profile of v11, /device:TPU:0, one launch (start us, length us, event | category | flops | bytes accessed | tf_op | source)
XLA Modules:
  0.0 42.4 jit_solution(8893491318012670172)
XLA Ops:
  0.6 6.6 %encode.1 = (bf16[1024,512]{1,0:T(8,128)(2,1)S(1)}, bf16[528,128]{1,0:T(8,128)(2,1)S(1)}, bf16[1040,128]{1,0:T(8,128)(2,1)S(1)}, f32[256,512]{1,0:T(8,128)S(1)}, bf16[512,2048]{1,0:T(8,128)(2,1)S(1)}) custom-call(s32[8]{0:T(128)} %owner_hbm.2, s32[1,3]{1,0:T(1,128)} %listed_hbm.1, f32[8,128]{1,0:T(8,128)} %bitcast.10, bf16[128,512]{1,0:T(8,128)(2,1)} %feat_hbm.1, ...), custom_call_target="tpu_custom_call" | custom-call | flops 4294967296 | bytes 6291456 | tf_op jit(solution)/shard_map/encode/pallas_call | solution.py:150
  7.2 0.5 %collective-permute-start = (bf16[528,128]{1,0:T(8,128)(2,1)S(1)}, bf16[528,128]{1,0:T(8,128)(2,1)S(1)}, u32[]{:S(2)}, u32[]{:S(2)}) collective-permute-start(bf16[528,128]{1,0:T(8,128)(2,1)S(1)} %get-tuple-element.20), channel_id=1, source_target_pairs={{0,1},{1,0},{2,3},{3,2},{4,5},{5,4},{6,7},{7,6},{8,9},{9,8},{10,11... | collective-permute-start | bytes 405512 | tf_op jit(solution)/shard_map/ppermute | solution.py:25
  7.7 1.0 %collective-permute-done.arrived_ref = bf16[528,128]{1,0:T(8,128)(2,1)S(1)} collective-permute-done((bf16[528,128]{1,0:T(8,128)(2,1)S(1)}, bf16[528,128]{1,0:T(8,128)(2,1)S(1)}, u32[]{:S(2)}, u32[]{:S(2)}) %collective-permute-start) | collective-permute-done | bytes 135200 | tf_op jit(solution)/shard_map/ppermute | solution.py:25
  8.8 6.7 %collective-permute-start.1 = (bf16[1040,128]{1,0:T(8,128)(2,1)S(1)}, bf16[1040,128]{1,0:T(8,128)(2,1)S(1)}, u32[]{:S(2)}, u32[]{:S(2)}) collective-permute-start(bf16[1040,128]{1,0:T(8,128)(2,1)S(1)} %outgoing_sums.1.after), channel_id=1, source_target_pairs={{0,31},{1,2},{2,1},{3,4},{4,3},{5,6},{6,5},{7,8},{8,7},{9,10},{10,... | collective-permute-start | bytes 798728 | tf_op jit(solution)/shard_map/ppermute | solution.py:34
  15.4 2.4 %grid_hidden.1 = (bf16[1024,2048]{1,0:T(8,128)(2,1)S(1)}, bf16[2048,512]{1,0:T(8,128)(2,1)S(1)}) custom-call(bf16[1024,512]{1,0:T(8,128)(2,1)S(1)} %get-tuple-element.21.enc_ref, bf16[512,2048]{1,0:T(8,128)(2,1)S(1)} %get-tuple-element.22.first, bf16[2048,512]{1,0:T(8,128)(2,1)} %second_hbm.3, bf16[1040,128]{1,0:T(8,128)(2,1)S(1)} %outgoing_sums.1.after), custom_call_target="tpu_custom_call" | custom-call | flops 2147483648 | bytes 3145728 | tf_op jit(solution)/shard_map/grid_hidden/pallas_call | solution.py:389
  17.8 1.8 %collective-permute-done.1.arrived_ref.sums_ref = bf16[1040,128]{1,0:T(8,128)(2,1)S(1)} collective-permute-done((bf16[1040,128]{1,0:T(8,128)(2,1)S(1)}, bf16[1040,128]{1,0:T(8,128)(2,1)S(1)}, u32[]{:S(2)}, u32[]{:S(2)}) %collective-permute-start.1) | collective-permute-done | bytes 266272 | tf_op jit(solution)/shard_map/ppermute | solution.py:34
  19.6 0.0 copy-start
  19.6 0.1 chip_share.1
  19.7 0.0 copy-start.1
  19.7 0.1 collective-permute-start.2
  19.8 1.5 %collective-permute-done.2.other_ref = bf16[256,512]{1,0:T(8,128)(2,1)S(1)} collective-permute-done((bf16[256,512]{1,0:T(8,128)(2,1)S(1)}, bf16[256,512]{1,0:T(8,128)(2,1)S(1)}, u32[]{:S(2)}, u32[]{:S(2)}) %collective-permute-start.2) | collective-permute-done | bytes 262176 | tf_op jit(solution)/shard_map/ppermute | solution.py:25
  21.3 0.1 chip_states.1
  21.4 5.3 %collective-permute-start.3 = (bf16[256,512]{1,0:T(8,128)(2,1)S(1)}, bf16[256,512]{1,0:T(8,128)(2,1)S(1)}, u32[]{:S(2)}, u32[]{:S(2)}) collective-permute-start(bf16[256,512]{1,0:T(8,128)(2,1)S(1)} %get-tuple-element.28), channel_id=1, source_target_pairs={{0,31},{1,2},{2,1},{3,4},{4,3},{5,6},{6,5},{7,8},{8,7},{9,10},{10,... | collective-permute-start | bytes 786440 | tf_op jit(solution)/shard_map/ppermute | solution.py:34
  26.7 0.3 collective-permute-start.5
  27.0 4.0 %collective-permute-done.3.near_ref = bf16[256,512]{1,0:T(8,128)(2,1)S(1)} collective-permute-done((bf16[256,512]{1,0:T(8,128)(2,1)S(1)}, bf16[256,512]{1,0:T(8,128)(2,1)S(1)}, u32[]{:S(2)}, u32[]{:S(2)}) %collective-permute-start.3) | collective-permute-done | bytes 262176 | tf_op jit(solution)/shard_map/ppermute | solution.py:34
  31.0 0.1 collective-permute-start.4
  31.1 0.0 copy-done
  31.1 0.0 copy-done.3
  31.1 1.0 %project.1 = (bf16[384,512]{1,0:T(8,128)(2,1)S(1)}, bf16[512,1024]{1,0:T(8,128)(2,1)S(1)}) custom-call(bf16[256,512]{1,0:T(8,128)(2,1)S(1)} %get-tuple-element.27.pair_ref, bf16[256,512]{1,0:T(8,128)(2,1)S(1)} %collective-permute-done.3.near_ref, f32[1,512]{1,0:T(1,128)S(1)} %copy-done.3, bf16[512,1536]{1,0:T(8,128)(2,1)S(1)} %bitcast.4), custom_call_target="tpu_custom_call" | custom-call | flops 738197504 | bytes 131072 | tf_op jit(solution)/shard_map/project/pallas_call | solution.py:255
  32.1 0.3 collective-permute-done.4.behind_ref
  32.4 0.0 copy-done.1
  32.4 1.2 %attend_own.1.after.ring_own = bf16[128,512]{1,0:T(8,128)(2,1)S(1)} custom-call(bf16[1040,128]{1,0:T(8,128)(2,1)S(1)} %get-tuple-element.18.base_ref, f32[128,512]{1,0:T(8,128)S(1)} %get-tuple-element.26.own_ref, bf16[384,512]{1,0:T(8,128)(2,1)S(1)} %get-tuple-element.29.query_ref, bf16[512,1024]{1,0:T(8,128)(2,1)S(1)} %get-tuple-element.30.kv_ref, ...), custom_call_target="tpu_custom_call" | custom-call | flops 671088640 | bytes 131072 | tf_op jit(solution)/shard_map/attend_own/pallas_call | solution.py:339
  33.7 0.2 collective-permute-start.6
  33.9 1.3 %collective-permute-done.5.far_ref = bf16[256,512]{1,0:T(8,128)(2,1)S(1)} collective-permute-done((bf16[256,512]{1,0:T(8,128)(2,1)S(1)}, bf16[256,512]{1,0:T(8,128)(2,1)S(1)}, u32[]{:S(2)}, u32[]{:S(2)}) %collective-permute-start.5) | collective-permute-done | bytes 262176 | tf_op jit(solution)/shard_map/ppermute | solution.py:34
  35.2 1.7 %attend_near.1.ring_near = bf16[256,512]{1,0:T(8,128)(2,1)S(1)} custom-call(bf16[1040,128]{1,0:T(8,128)(2,1)S(1)} %collective-permute-done.1.arrived_ref.sums_ref, bf16[256,512]{1,0:T(8,128)(2,1)S(1)} %collective-permute-done.3.near_ref, bf16[384,512]{1,0:T(8,128)(2,1)S(1)} %get-tuple-element.29.query_ref, bf16[512,1024]{1,0:T(8,128)(2,1)S(1)} %get-tuple-element.30.kv_ref, ...), custom_call_target="tpu_custom_call" | custom-call | flops 1342177280 | bytes 131072 | tf_op jit(solution)/shard_map/attend_near/pallas_call | solution.py:355
  37.0 0.0 copy-start.2
  37.0 0.1 collective-permute-start.7
  37.1 0.0 collective-permute-done.6.back_own
  37.1 1.3 %mesh_hidden.1.mesh_in = bf16[640,2048]{1,0:T(8,128)(2,1)S(1)} custom-call(bf16[128,512]{1,0:T(8,128)(2,1)S(1)} %collective-permute-done.6.back_own, bf16[128,512]{1,0:T(8,128)(2,1)S(1)} %attend_own.1.after.ring_own, bf16[256,512]{1,0:T(8,128)(2,1)S(1)} %attend_near.1.ring_near, bf16[512,2048]{1,0:T(8,128)(2,1)S(1)} %get-tuple-element.22.first), custom_call_target="tpu_custom_call" | custom-call | flops 1073741824 | bytes 131072 | tf_op jit(solution)/shard_map/mesh_hidden/pallas_call | solution.py:412
  38.4 0.0 collective-permute-done.7.back_near
  38.4 0.0 copy-done.2
  38.4 4.0 %decode.1 = (bf16[1024,512]{1,0:T(8,128)(2,1)}, bf16[128,512]{1,0:T(8,128)(2,1)}, bf16[640,2048]{1,0:T(8,128)(2,1)S(1)}) custom-call(s32[8]{0:T(128)} %owner_hbm.3, f32[8,128]{1,0:T(8,128)S(1)} %bitcast.9, bf16[128,512]{1,0:T(8,128)(2,1)S(1)} %attend_own.1.after.ring_own, ...), custom_call_target="tpu_custom_call", output_to_operand_aliasing={{2}: (7, {})} | custom-call | flops 2147483648 | bytes 6291456 | tf_op jit(solution)/shard_map/decode/pallas_call | solution.py:477
  (4 shorter events, 0.1 us)
Async XLA Ops:
  7.2 1.5 %collective-permute-start = (bf16[528,128]{1,0:T(8,128)(2,1)S(1)}, bf16[528,128]{1,0:T(8,128)(2,1)S(1)}, u32[]{:S(2)}, u32[]{:S(2)}) collective-permute-start(bf16[528,128]{1,0:T(8,128)(2,1)S(1)} %get-tuple-element.20), channel_id=1, source_target_pairs={{0,1},{1,0},{2,3},{3,2},{4,5},{5,4},{6,7},{7,6},{8,9},{9,8},{10,11... | collective-permute-start | bytes 405512 | tf_op jit(solution)/shard_map/ppermute | solution.py:25
  8.8 10.9 %collective-permute-start.1 = (bf16[1040,128]{1,0:T(8,128)(2,1)S(1)}, bf16[1040,128]{1,0:T(8,128)(2,1)S(1)}, u32[]{:S(2)}, u32[]{:S(2)}) collective-permute-start(bf16[1040,128]{1,0:T(8,128)(2,1)S(1)} %outgoing_sums.1.after), channel_id=1, source_target_pairs={{0,31},{1,2},{2,1},{3,4},{4,3},{5,6},{6,5},{7,8},{8,7},{9,10},{10,... | collective-permute-start | bytes 798728 | tf_op jit(solution)/shard_map/ppermute | solution.py:34
  19.6 11.5 %copy-start = (bf16[1,512,1536]{2,1,0:T(8,128)(2,1)S(1)}, bf16[1,512,1536]{2,1,0:T(8,128)(2,1)}, u32[]{:S(2)}) copy-start(bf16[1,512,1536]{2,1,0:T(8,128)(2,1)} %param.24) | copy-start | bytes 4718596
  19.6 11.5 %copy-start.3 = (f32[1,512]{1,0:T(1,128)S(1)}, f32[1,512]{1,0:T(1,128)}, u32[]{:S(2)}) copy-start(f32[1,512]{1,0:T(1,128)} %gain_ref.5) | copy-start | bytes 6148
  19.7 12.7 %copy-start.1 = (bf16[1,512,512]{2,1,0:T(8,128)(2,1)S(1)}, bf16[1,512,512]{2,1,0:T(8,128)(2,1)}, u32[]{:S(2)}) copy-start(bf16[1,512,512]{2,1,0:T(8,128)(2,1)} %param.25) | copy-start | bytes 1572868
  19.7 1.6 %collective-permute-start.2 = (bf16[256,512]{1,0:T(8,128)(2,1)S(1)}, bf16[256,512]{1,0:T(8,128)(2,1)S(1)}, u32[]{:S(2)}, u32[]{:S(2)}) collective-permute-start(bf16[256,512]{1,0:T(8,128)(2,1)S(1)} %get-tuple-element.25), channel_id=1, source_target_pairs={{0,1},{1,0},{2,3},{3,2},{4,5},{5,4},{6,7},{7,6},{8,9},{9,8},{10,11... | collective-permute-start | bytes 786440 | tf_op jit(solution)/shard_map/ppermute | solution.py:25
  21.4 9.6 %collective-permute-start.3 = (bf16[256,512]{1,0:T(8,128)(2,1)S(1)}, bf16[256,512]{1,0:T(8,128)(2,1)S(1)}, u32[]{:S(2)}, u32[]{:S(2)}) collective-permute-start(bf16[256,512]{1,0:T(8,128)(2,1)S(1)} %get-tuple-element.28), channel_id=1, source_target_pairs={{0,31},{1,2},{2,1},{3,4},{4,3},{5,6},{6,5},{7,8},{8,7},{9,10},{10,... | collective-permute-start | bytes 786440 | tf_op jit(solution)/shard_map/ppermute | solution.py:34
  26.7 8.5 %collective-permute-start.5 = (bf16[256,512]{1,0:T(8,128)(2,1)S(1)}, bf16[256,512]{1,0:T(8,128)(2,1)S(1)}, u32[]{:S(2)}, u32[]{:S(2)}) collective-permute-start(bf16[256,512]{1,0:T(8,128)(2,1)S(1)} %get-tuple-element.28), channel_id=1, source_target_pairs={{0,29},{1,4},{2,31},{3,6},{4,1},{5,8},{6,3},{7,10},{8,5},{9,12},{1... | collective-permute-start | bytes 786440 | tf_op jit(solution)/shard_map/ppermute | solution.py:34
  31.0 1.4 %collective-permute-start.4 = (bf16[128,512]{1,0:T(8,128)(2,1)S(1)}, bf16[128,512]{1,0:T(8,128)(2,1)S(1)}, u32[]{:S(2)}, u32[]{:S(2)}) collective-permute-start(bf16[128,512]{1,0:T(8,128)(2,1)S(1)} %slice.8), channel_id=1, source_target_pairs={{0,1},{1,0},{2,3},{3,2},{4,5},{5,4},{6,7},{7,6},{8,9},{9,8},{10,11... | collective-permute-start | bytes 393224 | tf_op jit(solution)/shard_map/ppermute | solution.py:25
  33.7 3.4 %collective-permute-start.6 = (bf16[128,512]{1,0:T(8,128)(2,1)S(1)}, bf16[128,512]{1,0:T(8,128)(2,1)S(1)}, u32[]{:S(2)}, u32[]{:S(2)}) collective-permute-start(bf16[128,512]{1,0:T(8,128)(2,1)S(1)} %attend_own.1.after.ring_own), channel_id=1, source_target_pairs={{0,1},{1,0},{2,3},{3,2},{4,5},{5,4},{6,7},{7,6},{8,9},{9,8},{10,11... | collective-permute-start | bytes 393224 | tf_op jit(solution)/shard_map/ppermute | solution.py:25
  37.0 1.4 %copy-start.2 = (f32[1024]{0:T(1024)S(1)}, f32[1024]{0:T(1024)}, u32[]{:S(2)}) copy-start(f32[1024]{0:T(1024)} %param.18) | copy-start | bytes 12292
  37.0 1.4 %collective-permute-start.7 = (bf16[128,512]{1,0:T(8,128)(2,1)S(1)}, bf16[128,512]{1,0:T(8,128)(2,1)S(1)}, u32[]{:S(2)}, u32[]{:S(2)}) collective-permute-start(bf16[128,512]{1,0:T(8,128)(2,1)S(1)} %slice.9), channel_id=1, source_target_pairs={{0,1},{1,0},{2,3},{3,2},{4,5},{5,4},{6,7},{7,6},{8,9},{9,8},{10,11... | collective-permute-start | bytes 393224 | tf_op jit(solution)/shard_map/ppermute | solution.py:25

commit v12 on v11

--- a/solution.py
+++ b/solution.py
@@ -439,10 +439,6 @@
     mine, count = lax.axis_index(AXES), lax.axis_size(AXES)
     outward = outward_of()
     mesh_ref[:rows, :] = halved(back_near[...], first[...]).astype(BF16)
-    ring[:rows, :] = back_near[...]
-    ring[rows:2 * rows, :] = back_own[...]
-    ring[2 * rows:3 * rows, :] = ring_own[...]
-    ring[3 * rows:, :] = ring_near[...]
     columns = jnp.transpose(weight_ref[...])
     index.wait()
     for r in range(tiles):
@@ -460,6 +456,11 @@
                 act[block, cols] = half * jnp.tanh(half) + half
             reads.append((block, weight, lines))
         out = jnp.dot(act[cut, :], second[...], preferred_element_type=F32)
+        if r == 0:
+            ring[:rows, :] = back_near[...]
+            ring[rows:2 * rows, :] = back_own[...]
+            ring[2 * rows:3 * rows, :] = ring_own[...]
+            ring[3 * rows:, :] = ring_near[...]
         for n, (block, weight, lines) in enumerate(reads):
             rest = enc_ref[block, :].astype(F32) + weight * ring[lines, :].astype(F32)
             x_ref[block, :] = (rest + out[n * rows:(n + 1) * rows, :]).astype(BF16)

time: 42.6 us -> 42.6 us (level)
  no operation moved by 1% of the time
where the time goes in v12:
time: 42.6 us; the launch traced here: 42.5 us
  Pallas kernels  18.4 us (43%)
  starting transfers between devices  13.2 us (31%)
  waiting for transfers between devices  9.98 us (23%)
  between operations  0.77 us (2%)
    ppermute x3, starting transfers between devices, from_outward(): return lax.ppermute(block, AXES, route)  12.3 us
    ppermute x3, waiting for transfers between devices, from_outward(): return lax.ppermute(block, AXES, route)  7.11 us
    pallas_call x1, Pallas kernels, encode(): pl.pallas_call(encode_kernel, out_shape=(kept((cells, depth)), kept((rows...  6.56 us
    pallas_call x1, Pallas kernels, decode(): pl.pallas_call(decode_kernel, out_shape=(jax.ShapeDtypeStruct((cells, dep...  4.05 us
    ppermute x5, waiting for transfers between devices, swapped(): return lax.ppermute(block, AXES, [(i, i ^ 1) for i in range(count)])  2.87 us
    pallas_call x1, Pallas kernels, grid_hidden(): pl.pallas_call(grid_hidden_kernel, out_shape=(kept((cells, hidden)), kept...  2.36 us
    pallas_call x1, Pallas kernels, attend_near(): pl.pallas_call(attend_near_kernel, out_shape=kept((2 * rows, depth)), in_...  1.72 us
    pallas_call x1, Pallas kernels, mesh_hidden(): pl.pallas_call(mesh_hidden_kernel, out_shape=kept(((2 * REACH + 1) * rows...  1.28 us
  transfers between devices with their start and end apart: 8, of which 6 were waited for; matrix products, arithmetic and copies ran while one was open for 0% of the time, Pallas kernels for 18%

profile of v12, /device:TPU:0, one launch (start us, length us, event | category | flops | bytes accessed | tf_op | source)
XLA Modules:
  0.0 42.5 jit_solution(11485871440168304307)
XLA Ops:
  0.6 6.6 %encode.1 = (bf16[1024,512]{1,0:T(8,128)(2,1)S(1)}, bf16[528,128]{1,0:T(8,128)(2,1)S(1)}, bf16[1040,128]{1,0:T(8,128)(2,1)S(1)}, f32[256,512]{1,0:T(8,128)S(1)}, bf16[512,2048]{1,0:T(8,128)(2,1)S(1)}) custom-call(s32[8]{0:T(128)} %owner_hbm.2, s32[1,3]{1,0:T(1,128)} %listed_hbm.1, f32[8,128]{1,0:T(8,128)} %bitcast.10, bf16[128,512]{1,0:T(8,128)(2,1)} %feat_hbm.1, ...), custom_call_target="tpu_custom_call" | custom-call | flops 4294967296 | bytes 6291456 | tf_op jit(solution)/shard_map/encode/pallas_call | solution.py:150
  7.2 0.5 %collective-permute-start = (bf16[528,128]{1,0:T(8,128)(2,1)S(1)}, bf16[528,128]{1,0:T(8,128)(2,1)S(1)}, u32[]{:S(2)}, u32[]{:S(2)}) collective-permute-start(bf16[528,128]{1,0:T(8,128)(2,1)S(1)} %get-tuple-element.20), channel_id=1, source_target_pairs={{0,1},{1,0},{2,3},{3,2},{4,5},{5,4},{6,7},{7,6},{8,9},{9,8},{10,11... | collective-permute-start | bytes 405512 | tf_op jit(solution)/shard_map/ppermute | solution.py:25
  7.7 1.0 %collective-permute-done.arrived_ref = bf16[528,128]{1,0:T(8,128)(2,1)S(1)} collective-permute-done((bf16[528,128]{1,0:T(8,128)(2,1)S(1)}, bf16[528,128]{1,0:T(8,128)(2,1)S(1)}, u32[]{:S(2)}, u32[]{:S(2)}) %collective-permute-start) | collective-permute-done | bytes 135200 | tf_op jit(solution)/shard_map/ppermute | solution.py:25
  8.8 6.7 %collective-permute-start.1 = (bf16[1040,128]{1,0:T(8,128)(2,1)S(1)}, bf16[1040,128]{1,0:T(8,128)(2,1)S(1)}, u32[]{:S(2)}, u32[]{:S(2)}) collective-permute-start(bf16[1040,128]{1,0:T(8,128)(2,1)S(1)} %outgoing_sums.1.after), channel_id=1, source_target_pairs={{0,31},{1,2},{2,1},{3,4},{4,3},{5,6},{6,5},{7,8},{8,7},{9,10},{10,... | collective-permute-start | bytes 798728 | tf_op jit(solution)/shard_map/ppermute | solution.py:34
  15.4 2.4 %grid_hidden.1 = (bf16[1024,2048]{1,0:T(8,128)(2,1)S(1)}, bf16[2048,512]{1,0:T(8,128)(2,1)S(1)}) custom-call(bf16[1024,512]{1,0:T(8,128)(2,1)S(1)} %get-tuple-element.21.enc_ref, bf16[512,2048]{1,0:T(8,128)(2,1)S(1)} %get-tuple-element.22.first, bf16[2048,512]{1,0:T(8,128)(2,1)} %second_hbm.3, bf16[1040,128]{1,0:T(8,128)(2,1)S(1)} %outgoing_sums.1.after), custom_call_target="tpu_custom_call" | custom-call | flops 2147483648 | bytes 3145728 | tf_op jit(solution)/shard_map/grid_hidden/pallas_call | solution.py:389
  17.8 1.8 %collective-permute-done.1.arrived_ref.sums_ref = bf16[1040,128]{1,0:T(8,128)(2,1)S(1)} collective-permute-done((bf16[1040,128]{1,0:T(8,128)(2,1)S(1)}, bf16[1040,128]{1,0:T(8,128)(2,1)S(1)}, u32[]{:S(2)}, u32[]{:S(2)}) %collective-permute-start.1) | collective-permute-done | bytes 266272 | tf_op jit(solution)/shard_map/ppermute | solution.py:34
  19.6 0.0 copy-start
  19.6 0.1 chip_share.1
  19.7 0.0 copy-start.1
  19.7 0.1 collective-permute-start.2
  19.8 1.5 %collective-permute-done.2.other_ref = bf16[256,512]{1,0:T(8,128)(2,1)S(1)} collective-permute-done((bf16[256,512]{1,0:T(8,128)(2,1)S(1)}, bf16[256,512]{1,0:T(8,128)(2,1)S(1)}, u32[]{:S(2)}, u32[]{:S(2)}) %collective-permute-start.2) | collective-permute-done | bytes 262176 | tf_op jit(solution)/shard_map/ppermute | solution.py:25
  21.3 0.1 chip_states.1
  21.4 5.3 %collective-permute-start.3 = (bf16[256,512]{1,0:T(8,128)(2,1)S(1)}, bf16[256,512]{1,0:T(8,128)(2,1)S(1)}, u32[]{:S(2)}, u32[]{:S(2)}) collective-permute-start(bf16[256,512]{1,0:T(8,128)(2,1)S(1)} %get-tuple-element.28), channel_id=1, source_target_pairs={{0,31},{1,2},{2,1},{3,4},{4,3},{5,6},{6,5},{7,8},{8,7},{9,10},{10,... | collective-permute-start | bytes 786440 | tf_op jit(solution)/shard_map/ppermute | solution.py:34
  26.7 0.3 collective-permute-start.5
  27.0 4.0 %collective-permute-done.3.near_ref = bf16[256,512]{1,0:T(8,128)(2,1)S(1)} collective-permute-done((bf16[256,512]{1,0:T(8,128)(2,1)S(1)}, bf16[256,512]{1,0:T(8,128)(2,1)S(1)}, u32[]{:S(2)}, u32[]{:S(2)}) %collective-permute-start.3) | collective-permute-done | bytes 262176 | tf_op jit(solution)/shard_map/ppermute | solution.py:34
  31.0 0.1 collective-permute-start.4
  31.1 0.0 copy-done
  31.1 0.0 copy-done.3
  31.1 1.0 %project.1 = (bf16[384,512]{1,0:T(8,128)(2,1)S(1)}, bf16[512,1024]{1,0:T(8,128)(2,1)S(1)}) custom-call(bf16[256,512]{1,0:T(8,128)(2,1)S(1)} %get-tuple-element.27.pair_ref, bf16[256,512]{1,0:T(8,128)(2,1)S(1)} %collective-permute-done.3.near_ref, f32[1,512]{1,0:T(1,128)S(1)} %copy-done.3, bf16[512,1536]{1,0:T(8,128)(2,1)S(1)} %bitcast.4), custom_call_target="tpu_custom_call" | custom-call | flops 738197504 | bytes 131072 | tf_op jit(solution)/shard_map/project/pallas_call | solution.py:255
  32.1 0.3 collective-permute-done.4.behind_ref
  32.4 0.0 copy-done.1
  32.4 1.2 %attend_own.1.after.ring_own = bf16[128,512]{1,0:T(8,128)(2,1)S(1)} custom-call(bf16[1040,128]{1,0:T(8,128)(2,1)S(1)} %get-tuple-element.18.base_ref, f32[128,512]{1,0:T(8,128)S(1)} %get-tuple-element.26.own_ref, bf16[384,512]{1,0:T(8,128)(2,1)S(1)} %get-tuple-element.29.query_ref, bf16[512,1024]{1,0:T(8,128)(2,1)S(1)} %get-tuple-element.30.kv_ref, ...), custom_call_target="tpu_custom_call" | custom-call | flops 671088640 | bytes 131072 | tf_op jit(solution)/shard_map/attend_own/pallas_call | solution.py:339
  33.7 0.2 collective-permute-start.6
  33.9 1.3 %collective-permute-done.5.far_ref = bf16[256,512]{1,0:T(8,128)(2,1)S(1)} collective-permute-done((bf16[256,512]{1,0:T(8,128)(2,1)S(1)}, bf16[256,512]{1,0:T(8,128)(2,1)S(1)}, u32[]{:S(2)}, u32[]{:S(2)}) %collective-permute-start.5) | collective-permute-done | bytes 262176 | tf_op jit(solution)/shard_map/ppermute | solution.py:34
  35.2 1.7 %attend_near.1.ring_near = bf16[256,512]{1,0:T(8,128)(2,1)S(1)} custom-call(bf16[1040,128]{1,0:T(8,128)(2,1)S(1)} %collective-permute-done.1.arrived_ref.sums_ref, bf16[256,512]{1,0:T(8,128)(2,1)S(1)} %collective-permute-done.3.near_ref, bf16[384,512]{1,0:T(8,128)(2,1)S(1)} %get-tuple-element.29.query_ref, bf16[512,1024]{1,0:T(8,128)(2,1)S(1)} %get-tuple-element.30.kv_ref, ...), custom_call_target="tpu_custom_call" | custom-call | flops 1342177280 | bytes 131072 | tf_op jit(solution)/shard_map/attend_near/pallas_call | solution.py:355
  37.0 0.0 copy-start.2
  37.0 0.1 collective-permute-start.7
  37.1 0.0 collective-permute-done.6.back_own
  37.1 1.3 %mesh_hidden.1.mesh_in = bf16[640,2048]{1,0:T(8,128)(2,1)S(1)} custom-call(bf16[128,512]{1,0:T(8,128)(2,1)S(1)} %collective-permute-done.6.back_own, bf16[128,512]{1,0:T(8,128)(2,1)S(1)} %attend_own.1.after.ring_own, bf16[256,512]{1,0:T(8,128)(2,1)S(1)} %attend_near.1.ring_near, bf16[512,2048]{1,0:T(8,128)(2,1)S(1)} %get-tuple-element.22.first), custom_call_target="tpu_custom_call" | custom-call | flops 1073741824 | bytes 131072 | tf_op jit(solution)/shard_map/mesh_hidden/pallas_call | solution.py:412
  38.4 0.0 collective-permute-done.7.back_near
  38.4 0.0 copy-done.2
  38.4 4.1 %decode.1 = (bf16[1024,512]{1,0:T(8,128)(2,1)}, bf16[128,512]{1,0:T(8,128)(2,1)}, bf16[640,2048]{1,0:T(8,128)(2,1)S(1)}) custom-call(s32[8]{0:T(128)} %owner_hbm.3, f32[8,128]{1,0:T(8,128)S(1)} %bitcast.9, bf16[128,512]{1,0:T(8,128)(2,1)S(1)} %attend_own.1.after.ring_own, ...), custom_call_target="tpu_custom_call", output_to_operand_aliasing={{2}: (7, {})} | custom-call | flops 2147483648 | bytes 6291456 | tf_op jit(solution)/shard_map/decode/pallas_call | solution.py:478
  (4 shorter events, 0.1 us)
Async XLA Ops:
  7.2 1.5 %collective-permute-start = (bf16[528,128]{1,0:T(8,128)(2,1)S(1)}, bf16[528,128]{1,0:T(8,128)(2,1)S(1)}, u32[]{:S(2)}, u32[]{:S(2)}) collective-permute-start(bf16[528,128]{1,0:T(8,128)(2,1)S(1)} %get-tuple-element.20), channel_id=1, source_target_pairs={{0,1},{1,0},{2,3},{3,2},{4,5},{5,4},{6,7},{7,6},{8,9},{9,8},{10,11... | collective-permute-start | bytes 405512 | tf_op jit(solution)/shard_map/ppermute | solution.py:25
  8.8 10.9 %collective-permute-start.1 = (bf16[1040,128]{1,0:T(8,128)(2,1)S(1)}, bf16[1040,128]{1,0:T(8,128)(2,1)S(1)}, u32[]{:S(2)}, u32[]{:S(2)}) collective-permute-start(bf16[1040,128]{1,0:T(8,128)(2,1)S(1)} %outgoing_sums.1.after), channel_id=1, source_target_pairs={{0,31},{1,2},{2,1},{3,4},{4,3},{5,6},{6,5},{7,8},{8,7},{9,10},{10,... | collective-permute-start | bytes 798728 | tf_op jit(solution)/shard_map/ppermute | solution.py:34
  19.6 11.5 %copy-start = (bf16[1,512,1536]{2,1,0:T(8,128)(2,1)S(1)}, bf16[1,512,1536]{2,1,0:T(8,128)(2,1)}, u32[]{:S(2)}) copy-start(bf16[1,512,1536]{2,1,0:T(8,128)(2,1)} %param.24) | copy-start | bytes 4718596
  19.6 11.5 %copy-start.3 = (f32[1,512]{1,0:T(1,128)S(1)}, f32[1,512]{1,0:T(1,128)}, u32[]{:S(2)}) copy-start(f32[1,512]{1,0:T(1,128)} %gain_ref.5) | copy-start | bytes 6148
  19.7 12.7 %copy-start.1 = (bf16[1,512,512]{2,1,0:T(8,128)(2,1)S(1)}, bf16[1,512,512]{2,1,0:T(8,128)(2,1)}, u32[]{:S(2)}) copy-start(bf16[1,512,512]{2,1,0:T(8,128)(2,1)} %param.25) | copy-start | bytes 1572868
  19.7 1.6 %collective-permute-start.2 = (bf16[256,512]{1,0:T(8,128)(2,1)S(1)}, bf16[256,512]{1,0:T(8,128)(2,1)S(1)}, u32[]{:S(2)}, u32[]{:S(2)}) collective-permute-start(bf16[256,512]{1,0:T(8,128)(2,1)S(1)} %get-tuple-element.25), channel_id=1, source_target_pairs={{0,1},{1,0},{2,3},{3,2},{4,5},{5,4},{6,7},{7,6},{8,9},{9,8},{10,11... | collective-permute-start | bytes 786440 | tf_op jit(solution)/shard_map/ppermute | solution.py:25
  21.4 9.6 %collective-permute-start.3 = (bf16[256,512]{1,0:T(8,128)(2,1)S(1)}, bf16[256,512]{1,0:T(8,128)(2,1)S(1)}, u32[]{:S(2)}, u32[]{:S(2)}) collective-permute-start(bf16[256,512]{1,0:T(8,128)(2,1)S(1)} %get-tuple-element.28), channel_id=1, source_target_pairs={{0,31},{1,2},{2,1},{3,4},{4,3},{5,6},{6,5},{7,8},{8,7},{9,10},{10,... | collective-permute-start | bytes 786440 | tf_op jit(solution)/shard_map/ppermute | solution.py:34
  26.7 8.5 %collective-permute-start.5 = (bf16[256,512]{1,0:T(8,128)(2,1)S(1)}, bf16[256,512]{1,0:T(8,128)(2,1)S(1)}, u32[]{:S(2)}, u32[]{:S(2)}) collective-permute-start(bf16[256,512]{1,0:T(8,128)(2,1)S(1)} %get-tuple-element.28), channel_id=1, source_target_pairs={{0,29},{1,4},{2,31},{3,6},{4,1},{5,8},{6,3},{7,10},{8,5},{9,12},{1... | collective-permute-start | bytes 786440 | tf_op jit(solution)/shard_map/ppermute | solution.py:34
  31.0 1.4 %collective-permute-start.4 = (bf16[128,512]{1,0:T(8,128)(2,1)S(1)}, bf16[128,512]{1,0:T(8,128)(2,1)S(1)}, u32[]{:S(2)}, u32[]{:S(2)}) collective-permute-start(bf16[128,512]{1,0:T(8,128)(2,1)S(1)} %slice.8), channel_id=1, source_target_pairs={{0,1},{1,0},{2,3},{3,2},{4,5},{5,4},{6,7},{7,6},{8,9},{9,8},{10,11... | collective-permute-start | bytes 393224 | tf_op jit(solution)/shard_map/ppermute | solution.py:25
  33.7 3.4 %collective-permute-start.6 = (bf16[128,512]{1,0:T(8,128)(2,1)S(1)}, bf16[128,512]{1,0:T(8,128)(2,1)S(1)}, u32[]{:S(2)}, u32[]{:S(2)}) collective-permute-start(bf16[128,512]{1,0:T(8,128)(2,1)S(1)} %attend_own.1.after.ring_own), channel_id=1, source_target_pairs={{0,1},{1,0},{2,3},{3,2},{4,5},{5,4},{6,7},{7,6},{8,9},{9,8},{10,11... | collective-permute-start | bytes 393224 | tf_op jit(solution)/shard_map/ppermute | solution.py:25
  37.0 1.4 %copy-start.2 = (f32[1024]{0:T(1024)S(1)}, f32[1024]{0:T(1024)}, u32[]{:S(2)}) copy-start(f32[1024]{0:T(1024)} %param.18) | copy-start | bytes 12292
  37.0 1.4 %collective-permute-start.7 = (bf16[128,512]{1,0:T(8,128)(2,1)S(1)}, bf16[128,512]{1,0:T(8,128)(2,1)S(1)}, u32[]{:S(2)}, u32[]{:S(2)}) collective-permute-start(bf16[128,512]{1,0:T(8,128)(2,1)S(1)} %slice.9), channel_id=1, source_target_pairs={{0,1},{1,0},{2,3},{3,2},{4,5},{5,4},{6,7},{7,6},{8,9},{9,8},{10,11... | collective-permute-start | bytes 393224 | tf_op jit(solution)/shard_map/ppermute | solution.py:25
